TPU v7x, 256 devices: a whole 4x4x8 slice. The times are simulated.
256 devices in a mesh: seq: 32 (over z, x), tp: 8 (over y, core).
Axes of the slice: x: 4, y: 4, z: 8, core: 2. Of those that a mesh axis runs over, the one named last changes fastest.
Arguments:
- resp_rows: bfloat16 [512, 16, 5120], P('seq', None, 'tp'), may hold values from -6 to 6
- resp_len: int32 [512], replicated, may hold values from 1 to 16, as said below
- resp_shard: int32 [512, 1], replicated, may hold values from 0 to 31; in each aligned block of 16 rows (0 to 15, 16 to 31, ...) no two rows name the same one
- group_prompt: int32 [32], replicated, may hold values from 0 to 31, each once
- prompt_kv: bfloat16 [2, 32, 256, 1024], P(None, 'seq', None, 'tp'), may hold values from -72 to 72
- w_query: bfloat16 [5120, 3072], P(None, 'tp'), may hold values from -0.078125 to 0.078125
- w_keyval: bfloat16 [2, 5120, 1024], P(None, None, 'tp'), may hold values from -0.078125 to 0.078125
- w_out: bfloat16 [3072, 5120], P('tp'), may hold values from -0.109375 to 0.109375
Outputs:
- attended: bfloat16 [1024, 16, 5120], P('seq', None, 'tp')
Inputs may be any that keep to these rules, and one draw needn't show every extreme that they name: `resp_shard`: in the rows of one device (one group) no learner appears more than 1 times, a bound that some block reaches. `group_prompt`: each prompt is answered by exactly one group. `resp_len`: some response has the full 16 tokens.
All inputs are finite; a program needn't handle non-finite values.
Results may differ from a plain program's by a relative error of at most 0.018.
Values may be sent and summed in bfloat16 or wider, within the bound.
No kernel may reach another device: no remote copies, remote signals or barrier semaphores. Data moves between devices by JAX's collectives and lax.ppermute only.
A program may use at most 128 MiB of HBM per device.

v0:
```python
import math

import jax
import jax.numpy as jnp
from jax import lax
from jax.sharding import PartitionSpec as P

HD = 128
PL = 256


ROPE_BASE = 1000000.0


def rope_tables(count, width, offset):
    places = (offset + jnp.arange(count)).astype(jnp.float32)
    freqs = ROPE_BASE ** (-(jnp.arange(width // 2).astype(jnp.float32) * 2.0 / width))
    angles = places[:, None] * freqs[None, :]
    return (jnp.cos(angles), jnp.sin(angles))


def rotate(values, cosine, sine):
    half = values.shape[-1] // 2
    first = values[..., :half]
    second = values[..., half:]
    cosine = cosine[:, None, :]
    sine = sine[:, None, :]
    return jnp.concatenate([first * cosine - second * sine, second * cosine + first * sine], -1)


def attend(queries, own_keys, own_values, cached_keys, cached_values, lengths):
    scale = 1.0 / math.sqrt(queries.shape[-1])
    prior = (
        jnp.einsum("stkrh,spkh->skrtp", queries, cached_keys, preferred_element_type=jnp.float32)
        * scale
    )
    recent = (
        jnp.einsum("stkrh,sukh->skrtu", queries, own_keys, preferred_element_type=jnp.float32)
        * scale
    )
    places = jnp.arange(queries.shape[1])
    causal = places[:, None] >= places[None, :]
    recent = jnp.where(causal, recent, -1e30)
    top = jnp.maximum(jnp.max(prior, -1), jnp.max(recent, -1))
    prior_exp = jnp.exp(prior - top[..., None])
    recent_exp = jnp.exp(recent - top[..., None])
    total = jnp.sum(prior_exp, -1) + jnp.sum(recent_exp, -1)
    prior_w = (prior_exp / total[..., None]).astype(jnp.bfloat16)
    recent_w = (recent_exp / total[..., None]).astype(jnp.bfloat16)
    mixed = jnp.einsum(
        "skrtp,spkh->stkrh", prior_w, cached_values, preferred_element_type=jnp.float32
    )
    mixed = mixed + jnp.einsum(
        "skrtu,sukh->stkrh", recent_w, own_values, preferred_element_type=jnp.float32
    )
    valid = places[None, :] < lengths[:, None]
    mixed = jnp.where(valid[:, :, None, None, None], mixed, 0.0)
    return mixed.astype(jnp.bfloat16).reshape(queries.shape[0], queries.shape[1], -1)


def choose(match, capacity):
    group_size = match.shape[1]
    rank = jnp.cumsum(match.astype(jnp.int32), axis=1) - 1
    picked = match[:, None, :] & (rank[:, None, :] == jnp.arange(capacity)[None, :, None])
    chosen = jnp.sum(jnp.where(picked, jnp.arange(group_size)[None, None, :], 0), -1)
    filled = jnp.any(picked, -1)
    return (chosen.reshape(-1), filled.reshape(-1))


def per_device(resp_rows, resp_len, resp_shard, group_prompt, prompt_kv, w_query, w_keyval, w_out):
    learners = lax.axis_size("seq")
    learner = lax.axis_index("seq")
    group_size = resp_rows.shape[0]
    capacity = (group_size + learners - 1) // learners
    table = resp_shard[:, 0].reshape(learners, group_size)
    own_targets = lax.dynamic_slice_in_dim(table, learner, 1, 0)[0]
    send_pick, send_filled = choose(own_targets[None, :] == jnp.arange(learners)[:, None], capacity)
    recv_pick, recv_filled = choose(table == learner, capacity)
    sources = jnp.repeat(jnp.arange(learners), capacity)
    slot_lengths = jnp.where(recv_filled, resp_len[sources * group_size + recv_pick], 0)
    prompts = group_prompt[sources]
    whole_rows = lax.all_gather(resp_rows, "tp", axis=2, tiled=True)
    taken = jnp.take(whole_rows, send_pick, axis=0)
    features = lax.all_to_all(
        jnp.where(send_filled[:, None, None], taken, jnp.zeros_like(taken)),
        "seq",
        split_axis=0,
        concat_axis=0,
        tiled=True,
    )
    caches = lax.all_gather(prompt_kv, "seq", axis=1, tiled=True)
    slot_cache = jnp.take(caches, prompts, axis=1)
    slots, token_count, width = features.shape
    flat = features.reshape(slots * token_count, width)
    kv_local = w_keyval.shape[2] // HD
    q_local = w_query.shape[1] // HD
    ratio = q_local // kv_local
    cosine, sine = rope_tables(token_count, HD, PL)
    queries = jnp.dot(flat, w_query, preferred_element_type=jnp.float32).reshape(
        slots, token_count, q_local, HD
    )
    queries = (
        rotate(queries, cosine, sine)
        .astype(jnp.bfloat16)
        .reshape(slots, token_count, kv_local, ratio, HD)
    )
    projected = jnp.einsum("nd,cde->cne", flat, w_keyval, preferred_element_type=jnp.float32)
    keys = rotate(projected[0].reshape(slots, token_count, kv_local, HD), cosine, sine).astype(
        jnp.bfloat16
    )
    values = projected[1].astype(jnp.bfloat16).reshape(slots, token_count, kv_local, HD)
    prompt_len = slot_cache.shape[2]
    cached_keys = slot_cache[0].reshape(slots, prompt_len, kv_local, HD)
    cached_values = slot_cache[1].reshape(slots, prompt_len, kv_local, HD)
    attn = attend(queries, keys, values, cached_keys, cached_values, slot_lengths)
    partial_value = jnp.dot(
        attn.reshape(-1, q_local * HD), w_out, preferred_element_type=jnp.float32
    ).astype(jnp.bfloat16)
    partial_value = (
        lax.optimization_barrier(partial_value).astype(jnp.float32).reshape(slots, token_count, -1)
    )
    summed = lax.psum_scatter(
        partial_value.astype(jnp.bfloat16), "tp", scatter_dimension=2, tiled=True
    )
    return summed


def solution(mesh):
    return jax.shard_map(
        per_device,
        mesh=mesh,
        in_specs=(
            P("seq", None, "tp"),
            P(),
            P(),
            P(),
            P(None, "seq", None, "tp"),
            P(None, "tp"),
            P(None, None, "tp"),
            P("tp", None),
        ),
        out_specs=P("seq", None, "tp"),
        check_vma=False,
    )
```

profile of v0, /device:TPU:2, one launch (start us, length us, event | category | flops | bytes accessed | tf_op | source)
XLA Modules:
  0.0 397.9 jit_solution(2337459180753430008)
XLA Ops:
  7.4 0.0 copy-start
  7.4 0.0 all-gather.5.cloned.1.call-start
  7.4 0.7 all-gather.5.cloned.1.call-update
  8.1 0.5 broadcast.355
  8.6 1.3 reduce.13
  10.0 0.1 reshape_squeeze.8
  10.1 0.2 reduce_window_sum.18
  10.2 0.1 fusion.38
  10.3 0.1 select_reduce_fusion
  10.5 31.5 %all-gather.5.cloned.1.call-done = bf16[16,16,5120]{2,1,0:T(8,128)(2,1)} async-done(((bf16[16,16,640]{2,1,0:T(8,128)(2,1)}), bf16[16,16,5120]{2,1,0:T(8,128)(2,1)}) %all-gather.5.cloned.1.call-update) | async-done | bytes 2621456 | tf_op jit(solution)/shard_map/all_gather | solution.py:82
  42.0 5.0 %gather_fusion.3 = bf16[32,16,5120]{2,1,0:T(8,128)(2,1)} fusion(bf16[16,16,5120]{2,1,0:T(8,128)(2,1)} %all-gather.5.cloned.1.call-done, s32[1024]{0:T(1024)S(1)} %pad_clamp_fusion), kind=kCustom, calls=%fused_computation.3 | custom fusion | bytes 10485888 | tf_op jit(solution)/shard_map/jit(_take)/gather | solution.py:83
  47.0 5.5 %select_select_fusion = bf16[32,16,5120]{2,1,0:T(8,128)(2,1)} fusion(bf16[32,16,5120]{2,1,0:T(8,128)(2,1)} %gather_fusion.3, pred[32]{0:T(512)(128)(4,1)S(1)} %compare_and_fusion, pred[32]{0:T(512)(128)(4,1)S(1)} %get-tuple-element.7), kind=kLoop, calls=%fused_computation.7 | loop fusion | flops 5242880 | bytes 10485824 | tf_op jit(solution)/shard_map/jit(_where)/select_n | solution.py:85
  52.4 0.0 copy-start.6
  52.4 10.3 %all-to-all-start = ((bf16[32,16,5120]{2,1,0:T(8,128)(2,1)}), bf16[32,16,5120]{2,1,0:T(8,128)(2,1)}, u32[]{:S(2)}, u32[]{:S(2)}) async-start(bf16[32,16,5120]{2,1,0:T(8,128)(2,1)} %select_select_fusion), calls=%async_computation | async-start | bytes 10485760 | tf_op jit(solution)/shard_map/all_to_all | solution.py:84
  62.8 0.0 copy-start.2
  62.8 0.0 all-gather.3.cloned.1.call-start
  62.8 0.5 all-gather.3.cloned.1.call-update
  63.3 0.0 reduce-scatter.4.cloned.1.call-start
  63.4 0.0 copy-done.6
  63.4 0.1 eq.106
  63.5 0.2 reduce_window_sum.17
  63.7 0.0 copy-start.3
  63.7 6.3 %copy.16 = bf16[5120,384]{0,1:T(8,128)(2,1)} copy(bf16[5120,384]{1,0:T(8,128)(2,1)} %param.13) | data formatting | bytes 7864320 | tf_op args[5]
  70.0 0.0 copy-done.2
  70.0 0.7 gather_fusion.1
  70.7 0.1 select_reduce_fusion.1
  70.8 0.1 reduce_or.18
  71.0 0.0 copy-done.3
  71.0 0.7 gather_fusion
  71.8 0.1 iota_compare_fusion.2
  71.9 0.1 multiply_cosine_fusion
  72.0 131.3 %all-gather.3.cloned.1.call-done = bf16[2,32,256,128]{3,2,1,0:T(8,128)(2,1)} async-done(((bf16[2,1,256,128]{3,2,1,0:T(8,128)(2,1)}), bf16[2,32,256,128]{3,2,1,0:T(8,128)(2,1)}) %all-gather.3.cloned.1.call-update) | async-done | bytes 4194320 | tf_op jit(solution)/shard_map/all_gather | solution.py:91
  203.3 5.2 %gather_fusion.2 = bf16[32,2,256,128]{3,2,1,0:T(8,128)(2,1)} fusion(bf16[2,32,256,128]{3,2,1,0:T(8,128)(2,1)} %all-gather.3.cloned.1.call-done, s32[1024]{0:T(1024)S(1)} %pad_clamp_fusion.1), kind=kCustom, calls=%fused_computation.2 | custom fusion | bytes 8388736 | tf_op jit(solution)/shard_map/jit(_take)/gather | solution.py:92
  208.6 4.8 %fusion.2 = bf16[2,32,256,128]{3,2,1,0:T(8,128)(2,1)} fusion(bf16[32,2,256,128]{3,2,1,0:T(8,128)(2,1)} %gather_fusion.2, pred[32]{0:T(512)(128)(4,1)S(1)} %compare_and_fusion.1), kind=kLoop, calls=%fused_computation.9 | loop fusion | flops 2097152 | bytes 8388640 | tf_op jit(solution)/shard_map/jit(_take)/select_n | solution.py:92
  213.3 0.0 all-to-all-done
  213.3 0.0 copy-done
  213.3 0.0 copy-start.5
  213.3 4.2 %convolution_bitcast_fusion = f32[2,512,128]{2,1,0:T(8,128)S(1)} fusion(bf16[512,5120,1]{1,0,2:T(8,128)(2,1)} %bitcast.25, bf16[2,5120,128]{2,1,0:T(8,128)(2,1)S(1)} %copy-done), kind=kOutput, calls=%fused_computation.24 | convolution fusion | flops 1342177280 | bytes 8388608 | tf_op jit(solution)/shard_map/nd,cde->cne/dot_general | solution.py:107
  217.6 0.1 fusion.23
  217.7 0.0 copy-done.5
  217.7 0.0 copy-start.4
  217.7 5.1 %fusion = f32[32,16,3,128]{3,1,2,0:T(8,128)S(1)} fusion(bf16[3,128,5120,1]{2,1,0,3:T(8,128)(2,1)S(1)} %bitcast.140, bf16[32,16,5120]{2,1,0:T(8,128)(2,1)} %all-to-all-done), kind=kOutput, calls=%fused_computation.5 | convolution fusion | flops 2013265920 | bytes 9961472 | tf_op jit(solution)/shard_map/dot_general | solution.py:99
  222.8 0.3 subtract_convert_fusion
  223.1 0.0 copy-done.4
  223.2 1.0 bitcast_reduce_fusion
  224.2 1.0 fusion.40
  225.2 0.3 fusion.17
  225.5 0.6 fusion.7
  226.1 0.4 fusion.20
  226.5 0.0 copy-start.7
  226.5 0.9 fusion.14
  227.4 0.3 copy.18
  227.6 1.0 copy-done.7
  228.6 4.6 %convolution_convert_fusion = bf16[512,5120]{1,0:T(8,128)(2,1)} fusion(bf16[384,5120]{1,0:T(8,128)(2,1)S(1)} %copy-done.7, bf16[64,8,3,128]{3,2,1,0:T(4,128)(2,1)S(1)} %bitcast.142), kind=kOutput, calls=%fused_computation.4 | convolution fusion | flops 2015887360 | bytes 9568256 | tf_op jit(solution)/shard_map/dot_general | solution.py:116
  233.2 34.1 %copy.25 = bf16[32,16,5120]{1,0,2:T(8,128)(2,1)} copy(bf16[32,16,5120]{2,1,0:T(8,128)(2,1)} %bitcast.139) | data formatting | bytes 10485760
  267.3 68.9 %reshape.429 = bf16[5120,512]{1,0:T(8,128)(2,1)} reshape(bf16[5120,32,16]{2,1,0:T(8,128)(2,1)} %bitcast.137) | data formatting | bytes 10485760
  336.2 0.0 reduce-scatter.4.cloned.1.call-update
  336.2 42.0 %reduce-scatter.4.cloned.1.call-done = bf16[640,512]{1,0:T(8,128)(2,1)} async-done(((bf16[5120,512]{1,0:T(8,128)(2,1)}), bf16[640,512]{1,0:T(8,128)(2,1)}) %reduce-scatter.4.cloned.1.call-update) | async-done | bytes 655376
  378.2 0.0 copy-start.1
  378.2 6.7 %reshape.430 = bf16[640,32,16]{2,1,0:T(8,128)(2,1)} reshape(bf16[640,512]{1,0:T(8,128)(2,1)} %reduce-scatter.4.cloned.1.call-done) | data formatting | bytes 1310720
  384.9 5.5 %copy.26 = bf16[32,16,640]{2,1,0:T(8,128)(2,1)} copy(bf16[32,16,640]{1,0,2:T(8,128)(2,1)} %bitcast.138) | data formatting | bytes 1310720
  390.4 0.0 copy-done.1
  (22 shorter events, 0.2 us)
Async XLA Ops:
  7.4 206.0 %copy-start = (bf16[2,5120,128]{2,1,0:T(8,128)(2,1)S(1)}, bf16[2,5120,128]{2,1,0:T(8,128)(2,1)}, u32[]{:S(2)}) copy-start(bf16[2,5120,128]{2,1,0:T(8,128)(2,1)} %param.14) | copy-start | bytes 7864324
  7.4 34.6 %all-gather.5.cloned.1.call-start = ((), (), s32[]{:S(2)}) async-start(), calls=%async_computation.3 | async-start | bytes 2949120 | tf_op jit(solution)/shard_map/all_gather | solution.py:82
  52.4 11.0 %copy-start.6 = (s32[512,1]{0,1:T(1,128)S(1)}, s32[512,1]{0,1:T(1,128)}, u32[]{:S(2)}) copy-start(s32[512,1]{0,1:T(1,128)} %param.10) | copy-start | bytes 6148
  52.4 160.9 %all-to-all-start = ((bf16[32,16,5120]{2,1,0:T(8,128)(2,1)}), bf16[32,16,5120]{2,1,0:T(8,128)(2,1)}, u32[]{:S(2)}, u32[]{:S(2)}) async-start(bf16[32,16,5120]{2,1,0:T(8,128)(2,1)} %select_select_fusion), calls=%async_computation | async-start | bytes 10485760 | tf_op jit(solution)/shard_map/all_to_all | solution.py:84
  62.8 7.3 %copy-start.2 = (s32[32]{0:T(128)S(1)}, s32[32]{0:T(128)}, u32[]{:S(2)}) copy-start(s32[32]{0:T(128)} %param.11) | copy-start | bytes 388
  62.8 140.6 %all-gather.3.cloned.1.call-start = ((), (), s32[]{:S(2)}) async-start(), calls=%async_computation.2 | async-start | bytes 4325376 | tf_op jit(solution)/shard_map/all_gather | solution.py:91
  63.3 314.9 %reduce-scatter.4.cloned.1.call-start = ((), (), s32[]{:S(2)}) async-start(), calls=%async_computation.4 | async-start | bytes 5898240
  63.7 7.3 %copy-start.3 = (s32[512]{0:T(512)S(1)}, s32[512]{0:T(512)}, u32[]{:S(2)}) copy-start(s32[512]{0:T(512)} %param.9) | copy-start | bytes 6148
  213.3 4.4 %copy-start.5 = (bf16[5120,384]{0,1:T(8,128)(2,1)S(1)}, bf16[5120,384]{0,1:T(8,128)(2,1)}, u32[]{:S(2)}) copy-start(bf16[5120,384]{0,1:T(8,128)(2,1)} %copy.16) | copy-start | bytes 11796484
  217.7 5.4 %copy-start.4 = (bf16[2,32,256,128]{3,2,1,0:T(8,128)(2,1)S(1)}, bf16[2,32,256,128]{3,2,1,0:T(8,128)(2,1)}, u32[]{:S(2)}) copy-start(bf16[2,32,256,128]{3,2,1,0:T(8,128)(2,1)} %fusion.2) | copy-start | bytes 12582916
  226.5 2.1 copy-start.7
  378.2 12.2 %copy-start.1 = (bf16[2,5120,128]{2,1,0:T(8,128)(2,1)S(1)}, bf16[2,5120,128]{2,1,0:T(8,128)(2,1)}, u32[]{:S(2)}) copy-start(bf16[2,5120,128]{2,1,0:T(8,128)(2,1)} %param.14) | copy-start | bytes 7864324
Sparse Core Ops, SparseCore 0:
  10.0 31.8 all-gather.4
  336.3 41.8 reduce-scatter.3
Sparse Core Ops, SparseCore 1:
  65.8 137.4 all-gather.2
where the time goes:
time: 399 us; the launch traced here: 398 us
  waiting for transfers between devices  206 us (52%)
  local copies, waits for them, and re-layouts  135 us (34%)
  matrix products  17.1 us (4%)
  between operations  15.1 us (4%)
  other arithmetic  14 us (4%)
  starting transfers between devices  10.4 us (3%)
    all_gather x1, waiting for transfers between devices, per_device(): caches = lax.all_gather(prompt_kv, 'seq', axis=1, tiled=True)  131 us
    unnamed x22, local copies, waits for them, and re-layouts  123 us
    unnamed x4, waiting for transfers between devices  43.3 us
    all_gather x1, waiting for transfers between devices, per_device(): whole_rows = lax.all_gather(resp_rows, 'tp', axis=2, tiled=True)  31.5 us
    all_to_all x1, starting transfers between devices, per_device(): lax.all_to_all(jnp.where(send_filled[:, None, None], taken, jnp.zeros_lik...  10.3 us
  transfers between devices with their start and end apart: 4, of which 3 were waited for; matrix products, arithmetic and copies ran while one was open for 5% of the time, Pallas kernels for 0%

commit v1 on v0

v1 whole, which is shorter than its diff:
```python
import functools
import math

import jax
import jax.numpy as jnp
from jax import lax
from jax.experimental import pallas as pl
from jax.experimental.pallas import tpu as pltpu
from jax.sharding import PartitionSpec as P

HD = 128
PL = 256
ROPE_BASE = 1000000.0
CHIPS = 4
CORES = 2


def chip_shift(step):
    return [
        (y * CORES + c, ((y + step) % CHIPS) * CORES + c) for y in range(CHIPS) for c in range(CORES)
    ]


CORE_SWAP = [(i, i ^ 1) for i in range(CHIPS * CORES)]


def rope_tables(count, rows):
    places = (PL + jnp.arange(count)).astype(jnp.float32)
    freqs = ROPE_BASE ** (-(jnp.arange(HD // 2).astype(jnp.float32) * 2.0 / HD))
    angles = places[:, None] * freqs[None, :]
    cosine, sine = jnp.cos(angles), jnp.sin(angles)
    cosine = jnp.concatenate([cosine, cosine], -1)
    sine = jnp.concatenate([-sine, sine], -1)
    return jnp.tile(cosine, (rows // count, 1)), jnp.tile(sine, (rows // count, 1))


def group_kernel(
    heads,
    tokens,
    from_ref,
    to_ref,
    *refs,
):
    xs = refs[:8]
    wq_ref, wkv_ref, cache_ref, cos_ref, sin_ref, valid_ref, wo_ref = refs[8:15]
    other_ref, mine_ref = refs[15:17]
    acc_q, acc_kv, attn = refs[17:]
    step = pl.program_id(0)
    rows = attn.shape[0]

    for k in range(8):

        @pl.when(step == k)
        def _():
            x = xs[k][...]
            q = jnp.dot(x, wq_ref[...], preferred_element_type=jnp.float32)
            keys = jnp.dot(x, wkv_ref[0], preferred_element_type=jnp.float32)
            values = jnp.dot(x, wkv_ref[1], preferred_element_type=jnp.float32)
            if k == 0:
                acc_q[...] = q
                acc_kv[0] = keys
                acc_kv[1] = values
            else:
                acc_q[...] += q
                acc_kv[0] += keys
                acc_kv[1] += values

    @pl.when(step == 7)
    def _():
        cosine, sine = cos_ref[...], sin_ref[...]

        def rotate(v):
            return (v * cosine + pltpu.roll(v, HD // 2, 1) * sine).astype(jnp.bfloat16)

        scale = 1.0 / math.sqrt(HD)
        own_keys = rotate(acc_kv[0])
        own_values = acc_kv[1].astype(jnp.bfloat16)
        half = cache_ref.shape[0] // 2
        cached_keys = cache_ref[:half].reshape(PL, HD)
        cached_values = cache_ref[half:].reshape(PL, HD)
        row = lax.broadcasted_iota(jnp.int32, (rows, rows), 0)
        col = lax.broadcasted_iota(jnp.int32, (rows, rows), 1)
        seen = (row // tokens == col // tokens) & (col <= row)
        nt = (((1,), (1,)), ((), ()))
        for h in range(heads):
            q = rotate(acc_q[:, h * HD : (h + 1) * HD])
            prior = lax.dot_general(q, cached_keys, nt, preferred_element_type=jnp.float32) * scale
            recent = lax.dot_general(q, own_keys, nt, preferred_element_type=jnp.float32) * scale
            recent = jnp.where(seen, recent, -1e30)
            top = jnp.maximum(
                jnp.max(prior, -1, keepdims=True), jnp.max(recent, -1, keepdims=True)
            )
            prior = jnp.exp(prior - top)
            recent = jnp.exp(recent - top)
            total = jnp.sum(prior, -1, keepdims=True) + jnp.sum(recent, -1, keepdims=True)
            inverse = 1.0 / total
            prior = (prior * inverse).astype(jnp.bfloat16)
            recent = (recent * inverse).astype(jnp.bfloat16)
            mixed = jnp.dot(prior, cached_values, preferred_element_type=jnp.float32)
            mixed += jnp.dot(recent, own_values, preferred_element_type=jnp.float32)
            mixed = jnp.where(valid_ref[...] > 0.0, mixed, 0.0)
            attn[:, h * HD : (h + 1) * HD] = mixed.astype(jnp.bfloat16)

    @pl.when((step >= 8) & (step < 12))
    def _():
        other_ref[0] = jnp.dot(
            attn[...], wo_ref[...], preferred_element_type=jnp.float32
        ).astype(jnp.bfloat16)

    @pl.when(step >= 12)
    def _():
        mine_ref[0] = jnp.dot(
            attn[...], wo_ref[...], preferred_element_type=jnp.float32
        ).astype(jnp.bfloat16)


def group_call(order_from, order_to, shards, w_query, w_keyval, cache, cosine, sine, valid, w_out, tokens):
    rows, width = shards[0].shape
    q_width = w_query.shape[1]
    heads = q_width // HD
    whole = lambda a: pl.BlockSpec(a.shape, lambda i, f, t, n=a.ndim: (0,) * n)
    grid_spec = pltpu.PrefetchScalarGridSpec(
        num_scalar_prefetch=2,
        grid=(16,),
        in_specs=[whole(x) for x in shards]
        + [
            pl.BlockSpec((width, q_width), lambda i, f, t: (f[jnp.minimum(i, 7)], 0)),
            pl.BlockSpec((2, width, HD), lambda i, f, t: (0, f[jnp.minimum(i, 7)], 0)),
            whole(cache),
            whole(cosine),
            whole(sine),
            whole(valid),
            pl.BlockSpec((q_width, width), lambda i, f, t: (0, t[jnp.maximum(i - 8, 0)])),
        ],
        out_specs=[
            pl.BlockSpec((1, rows, width), lambda i, f, t: (jnp.clip(i - 8, 0, 3), 0, 0)),
            pl.BlockSpec((1, rows, width), lambda i, f, t: (jnp.clip(i - 12, 0, 3), 0, 0)),
        ],
        scratch_shapes=[
            pltpu.VMEM((rows, q_width), jnp.float32),
            pltpu.VMEM((2, rows, HD), jnp.float32),
            pltpu.VMEM((rows, q_width), jnp.bfloat16),
        ],
    )
    block = jax.ShapeDtypeStruct((4, rows, width), jnp.bfloat16)
    return pl.pallas_call(
        functools.partial(group_kernel, heads, tokens),
        grid_spec=grid_spec,
        out_shape=[block, block],
        compiler_params=pltpu.CompilerParams(
            dimension_semantics=("arbitrary",), vmem_limit_bytes=32 * 1024 * 1024
        ),
        cost_estimate=pl.CostEstimate(
            flops=3_000_000_000, bytes_accessed=16_000_000, transcendentals=400_000
        ),
    )(order_from, order_to, *shards, w_query, w_keyval, cache, cosine, sine, valid, w_out)


def per_device(resp_rows, resp_len, resp_shard, group_prompt, prompt_kv, w_query, w_keyval, w_out):
    learners = lax.axis_size("seq")
    group = lax.axis_index("seq")
    me = lax.axis_index("tp")
    y, c = me // CORES, me % CORES
    group_size, tokens, width = resp_rows.shape
    rows = group_size * tokens

    pieces = prompt_kv.reshape(learners, -1, HD)
    pieces = lax.all_to_all(pieces, "seq", 0, 0, tiled=True)
    pieces = jnp.take(pieces, group_prompt, axis=0)
    cache = lax.all_to_all(pieces, "seq", 0, 0, tiled=True)

    x = resp_rows.reshape(rows, width)
    below = lax.ppermute(x, "tp", chip_shift(1))
    above = lax.ppermute(x, "tp", chip_shift(-1))
    across = lax.ppermute(x, "tp", chip_shift(2))
    near = [x, below, above, across]
    far = [lax.ppermute(v, "tp", CORE_SWAP) for v in near]

    def places(shifts):
        at = jnp.stack([(y + s) % CHIPS for s in shifts])
        return jnp.concatenate([at * CORES + c, at * CORES + 1 - c]).astype(jnp.int32)

    order_from = places((0, -1, 1, 2))
    order_to = places((0, 1, -1, 2))
    order_to = jnp.concatenate([order_to[4:], order_to[:4]])

    own_len = lax.dynamic_slice_in_dim(resp_len, group * group_size, group_size, 0)
    valid = (jnp.arange(tokens)[None, :] < own_len[:, None]).astype(jnp.float32)
    valid = jnp.broadcast_to(valid.reshape(rows, 1), (rows, HD))
    cosine, sine = rope_tables(tokens, rows)

    other, mine = group_call(
        order_from, order_to, near + far, w_query, w_keyval, cache, cosine, sine, valid, w_out, tokens
    )
    other = lax.ppermute(other, "tp", CORE_SWAP)
    both = mine.astype(jnp.float32) + other.astype(jnp.float32)
    sent = both[1:].astype(jnp.bfloat16)
    parts = [
        lax.ppermute(sent[0], "tp", chip_shift(1)),
        lax.ppermute(sent[1], "tp", chip_shift(-1)),
        lax.ppermute(sent[2], "tp", chip_shift(2)),
    ]
    total = both[0]
    for part in parts:
        total = total + part.astype(jnp.float32)
    total = total.astype(jnp.bfloat16).reshape(group_size, tokens, width)

    own_shard = lax.dynamic_slice_in_dim(resp_shard[:, 0], group * group_size, group_size, 0)
    match = own_shard[None, :] == jnp.arange(learners)[:, None]
    pick = jnp.sum(jnp.where(match, jnp.arange(group_size)[None, :], 0), -1)
    filled = jnp.any(match, -1)
    slots = jnp.where(filled[:, None, None], jnp.take(total, pick, axis=0), 0)
    return lax.all_to_all(slots.astype(jnp.bfloat16), "seq", 0, 0, tiled=True)


def solution(mesh):
    return jax.shard_map(
        per_device,
        mesh=mesh,
        in_specs=(
            P("seq", None, "tp"),
            P(),
            P(),
            P(),
            P(None, "seq", None, "tp"),
            P(None, "tp"),
            P(None, None, "tp"),
            P("tp", None),
        ),
        out_specs=P("seq", None, "tp"),
        check_vma=False,
    )
```

time: 399 us -> 109 us (0.27)
  waiting for transfers between devices: 206 us -> 30.9 us
  local copies, waits for them, and re-layouts: 135 us -> 10.1 us
  blocking collectives: 0 us -> 24.8 us
  starting transfers between devices: 10.4 us -> 28.3 us
  matrix products: 17.1 us -> 0 us
  between operations: 15.1 us -> 0.26 us
  Pallas kernels: 0 us -> 10.8 us
  other arithmetic: 14 us -> 3.51 us
    all_gather x2 -> x0, waiting for transfers between devices: 163 us -> none  [the longest x1 131 us: per_device(): caches = lax.all_gather(prompt_kv, 'seq', axis=1, tiled=True)]
    unnamed x22 -> x11, local copies, waits for them, and re-layouts: 123 us -> 7.77 us
    unnamed x4 -> x0, waiting for transfers between devices: 43.3 us -> none
    all_to_all x0 -> x1, blocking collectives: none -> 24.8 us  [per_device(): return lax.all_to_all(slots.astype(jnp.bfloat16), 'seq', 0, 0, tiled=True)]
    dot_general x7 -> x0, matrix products: 17.1 us -> none  [the longest x1 5.1 us: per_device(): jnp.dot(flat, w_query, preferred_element_type=jnp.float32)]
    ppermute x0 -> x11, waiting for transfers between devices: none -> 16.2 us  [the longest x1 7.3 us: per_device(): lax.ppermute(sent[2], 'tp', chip_shift(2))]
    all_to_all x1 -> x2, waiting for transfers between devices: 0.01 us -> 14.6 us  [the longest x1 7.92 us: per_device(): cache = lax.all_to_all(pieces, 'seq', 0, 0, tiled=True)]
    ppermute x0 -> x11, starting transfers between devices: none -> 11.1 us  [the longest x1 2.87 us: per_device(): lax.ppermute(sent[1], 'tp', chip_shift(-1))]
  transfers between devices with their start and end apart: 4 -> 13, of which waited for: 3 -> 5; matrix products, arithmetic and copies ran while one was open for 5% -> 4% of each run, Pallas kernels for 0% -> 0%
where the time goes in v1:
time: 109 us
  waiting for transfers between devices  30.9 us (28%)
  starting transfers between devices  28.3 us (26%)
  blocking collectives  24.8 us (23%)
  Pallas kernels  10.8 us (10%)
  local copies, waits for them, and re-layouts  10.1 us (9%)
  other arithmetic  3.51 us (3%)
    all_to_all x1, blocking collectives, per_device(): return lax.all_to_all(slots.astype(jnp.bfloat16), 'seq', 0, 0, tiled=True)  24.8 us
    all_to_all x1, starting transfers between devices, per_device(): pieces = lax.all_to_all(pieces, 'seq', 0, 0, tiled=True)  11.6 us
    pallas_call x1, Pallas kernels, group_call(): pl.pallas_call(functools.partial(group_kernel, heads, tokens), grid_spec=...  10.8 us
    all_to_all x1, waiting for transfers between devices, per_device(): cache = lax.all_to_all(pieces, 'seq', 0, 0, tiled=True)  7.92 us
    unnamed x11, local copies, waits for them, and re-layouts  7.77 us
    ppermute x1, waiting for transfers between devices, per_device(): lax.ppermute(sent[2], 'tp', chip_shift(2))  7.3 us
    all_to_all x1, waiting for transfers between devices, per_device(): pieces = lax.all_to_all(pieces, 'seq', 0, 0, tiled=True)  6.7 us
    ppermute x1, waiting for transfers between devices, per_device(): lax.ppermute(sent[0], 'tp', chip_shift(1))  6.18 us
  transfers between devices with their start and end apart: 13, of which 5 were waited for; matrix products, arithmetic and copies ran while one was open for 4% of the time, Pallas kernels for 0%

profile of v1, /device:TPU:2, one launch (start us, length us, event | category | flops | bytes accessed | tf_op | source)
XLA Modules:
  0.0 108.7 jit_solution(16465530221094985028)
XLA Ops:
  0.0 0.0 copy-start
  0.0 1.6 %collective-permute-start = (bf16[256,640]{1,0:T(8,128)(2,1)}, bf16[256,640]{1,0:T(8,128)(2,1)S(1)}, u32[]{:S(2)}, u32[]{:S(2)}) collective-permute-start(bf16[256,640]{1,0:T(8,128)(2,1)} %bitcast.33), channel_id=1, source_target_pairs={{0,2},{1,3},{2,4},{3,5},{4,6},{5,7},{6,0},{7,1},{8,10},{9,11},{10,... | collective-permute-start | bytes 983048 | tf_op jit(solution)/shard_map/ppermute | solution.py:173
  1.6 1.7 %collective-permute-start.1 = (bf16[256,640]{1,0:T(8,128)(2,1)}, bf16[256,640]{1,0:T(8,128)(2,1)S(1)}, u32[]{:S(2)}, u32[]{:S(2)}) collective-permute-start(bf16[256,640]{1,0:T(8,128)(2,1)} %bitcast.34), channel_id=1, source_target_pairs={{0,6},{1,7},{2,0},{3,1},{4,2},{5,3},{6,4},{7,5},{8,14},{9,15},{10,... | collective-permute-start | bytes 983048 | tf_op jit(solution)/shard_map/ppermute | solution.py:174
  3.2 2.0 %collective-permute-start.2 = (bf16[256,640]{1,0:T(8,128)(2,1)}, bf16[256,640]{1,0:T(8,128)(2,1)S(1)}, u32[]{:S(2)}, u32[]{:S(2)}) collective-permute-start(bf16[256,640]{1,0:T(8,128)(2,1)} %bitcast.35), channel_id=1, source_target_pairs={{0,4},{1,5},{2,6},{3,7},{4,0},{5,1},{6,2},{7,3},{8,12},{9,13},{10,... | collective-permute-start | bytes 983048 | tf_op jit(solution)/shard_map/ppermute | solution.py:175
  5.2 0.0 collective-permute-start.3
  5.2 11.6 %all-to-all-start = ((bf16[32,16,128]{2,1,0:T(8,128)(2,1)}), bf16[32,16,128]{2,1,0:T(8,128)(2,1)S(1)}, u32[]{:S(2)}, u32[]{:S(2)}) async-start(bf16[32,16,128]{2,1,0:T(8,128)(2,1)} %bitcast.39), calls=%async_computation | async-start | bytes 262144 | tf_op jit(solution)/shard_map/all_to_all | solution.py:168
  16.9 0.7 compare_select_fusion.1
  17.6 0.7 compare_and_fusion
  18.3 0.1 add_subtract_fusion
  18.4 0.8 dynamic_slice.7
  19.1 0.1 fusion.5
  19.2 0.1 fusion.6
  19.3 6.7 %all-to-all-done = bf16[32,16,128]{2,1,0:T(8,128)(2,1)S(1)} async-done(((bf16[32,16,128]{2,1,0:T(8,128)(2,1)}), bf16[32,16,128]{2,1,0:T(8,128)(2,1)S(1)}, u32[]{:S(2)}, u32[]{:S(2)}) %all-to-all-start) | async-done | bytes 131104 | tf_op jit(solution)/shard_map/all_to_all | solution.py:168
  26.0 0.6 gather_fusion
  26.6 0.8 broadcast_select_fusion
  27.4 5.6 %all-to-all-start.1 = ((bf16[32,16,128]{2,1,0:T(8,128)(2,1)}), bf16[32,16,128]{2,1,0:T(8,128)(2,1)S(1)}, u32[]{:S(2)}, u32[]{:S(2)}) async-start(bf16[32,16,128]{2,1,0:T(8,128)(2,1)} %broadcast_select_fusion), calls=%async_computation.1 | async-start | bytes 262144 | tf_op jit(solution)/shard_map/all_to_all | solution.py:170
  33.0 0.0 collective-permute-done.refs_1_
  33.0 0.1 collective-permute-start.4
  33.1 0.0 collective-permute-done.1.refs_2_
  33.2 0.5 collective-permute-start.5
  33.6 0.0 collective-permute-done.2.refs_3_
  33.6 0.1 collective-permute-start.6
  33.8 0.1 pad_add_fusion.1.to_ref
  33.8 0.1 reshape.78
  33.9 0.1 pad_add_fusion.from_ref
  34.0 0.1 pad_maximum_fusion
  34.1 0.0 collective-permute-done.3.refs_4_
  34.1 7.9 %all-to-all-done.1.refs_10_ = bf16[32,16,128]{2,1,0:T(8,128)(2,1)S(1)} async-done(((bf16[32,16,128]{2,1,0:T(8,128)(2,1)}), bf16[32,16,128]{2,1,0:T(8,128)(2,1)S(1)}, u32[]{:S(2)}, u32[]{:S(2)}) %all-to-all-start.1) | async-done | bytes 131104 | tf_op jit(solution)/shard_map/all_to_all | solution.py:170
  42.0 0.0 collective-permute-done.4.refs_5_
  42.0 0.0 collective-permute-done.5.refs_6_
  42.0 0.0 collective-permute-done.6.refs_7_
  42.0 0.1 broadcast_in_dim.66.refs_13_
  42.1 0.0 copy-start.1
  42.1 2.1 %copy-done.1 = bf16[5120,384]{1,0:T(8,128)(2,1)S(1)} copy-done((bf16[5120,384]{1,0:T(8,128)(2,1)S(1)}, bf16[5120,384]{1,0:T(8,128)(2,1)}, u32[]{:S(2)}) %copy-start.1) | copy-done | bytes 3932184
  44.2 0.0 copy-start.2
  44.2 2.1 %copy-done.2 = bf16[384,5120]{1,0:T(8,128)(2,1)S(1)} copy-done((bf16[384,5120]{1,0:T(8,128)(2,1)S(1)}, bf16[384,5120]{1,0:T(8,128)(2,1)}, u32[]{:S(2)}) %copy-start.2) | copy-done | bytes 3932184
  46.4 0.0 copy-start.3
  46.4 1.7 %copy-done.3 = bf16[2,5120,128]{2,1,0:T(8,128)(2,1)S(1)} copy-done((bf16[2,5120,128]{2,1,0:T(8,128)(2,1)S(1)}, bf16[2,5120,128]{2,1,0:T(8,128)(2,1)}, u32[]{:S(2)}) %copy-start.3) | copy-done | bytes 2621464
  48.1 0.0 copy-start.4
  48.1 1.0 copy-done.4
  49.1 10.8 %shard_map.82 = (bf16[4,256,640]{2,1,0:T(8,128)(2,1)S(1)}, bf16[4,256,640]{2,1,0:T(8,128)(2,1)S(1)}) custom-call(s32[8]{0:T(128)S(1)} %pad_add_fusion.from_ref, s32[8]{0:T(128)S(1)} %pad_add_fusion.1.to_ref, bf16[256,640]{1,0:T(8,128)(2,1)S(1)} %bitcast.37, bf16[256,640]{1,0:T(8,128)(2,1)S(1)} %collective-permute-done.refs_1_, ...), custom_call_target="tpu_custom_call" | custom-call | flops 3000000000 | bytes 16000000 | tf_op jit(solution)/shard_map/pallas_call | solution.py:146
  59.9 0.3 collective-permute-start.7
  60.2 0.0 copy-done
  60.2 0.1 dynamic-slice_bitcast_fusion
  60.3 0.1 select_reduce_fusion
  60.4 0.1 fusion.4
  60.5 2.7 %collective-permute-done.7 = bf16[4,256,640]{2,1,0:T(8,128)(2,1)S(1)} collective-permute-done((bf16[4,256,640]{2,1,0:T(8,128)(2,1)S(1)}, bf16[4,256,640]{2,1,0:T(8,128)(2,1)S(1)}, u32[]{:S(2)}, u32[]{:S(2)}) %collective-permute-start.7) | collective-permute-done | bytes 1310752 | tf_op jit(solution)/shard_map/ppermute | solution.py:195
  63.2 0.4 fusion.8
  63.6 0.1 slice_bitcast_fusion.3
  63.7 1.6 %collective-permute-start.10 = (bf16[256,640]{1,0:T(8,128)(2,1)S(1)}, bf16[256,640]{1,0:T(8,128)(2,1)S(1)}, u32[]{:S(2)}, u32[]{:S(2)}) collective-permute-start(bf16[256,640]{1,0:T(8,128)(2,1)S(1)} %get-tuple-element.16), channel_id=1, source_target_pairs={{0,4},{1,5},{2,6},{3,7},{4,0},{5,1},{6,2},{7,3},{8,12},{9,13},{10,... | collective-permute-start | bytes 983048 | tf_op jit(solution)/shard_map/ppermute | solution.py:201
  65.3 0.4 collective-permute-start.8
  65.7 2.9 %collective-permute-start.9 = (bf16[256,640]{1,0:T(8,128)(2,1)S(1)}, bf16[256,640]{1,0:T(8,128)(2,1)S(1)}, u32[]{:S(2)}, u32[]{:S(2)}) collective-permute-start(bf16[256,640]{1,0:T(8,128)(2,1)S(1)} %get-tuple-element.17), channel_id=1, source_target_pairs={{0,6},{1,7},{2,0},{3,1},{4,2},{5,3},{6,4},{7,5},{8,14},{9,15},{10,... | collective-permute-start | bytes 983048 | tf_op jit(solution)/shard_map/ppermute | solution.py:200
  68.5 7.3 %collective-permute-done.10 = bf16[256,640]{1,0:T(8,128)(2,1)S(1)} collective-permute-done((bf16[256,640]{1,0:T(8,128)(2,1)S(1)}, bf16[256,640]{1,0:T(8,128)(2,1)S(1)}, u32[]{:S(2)}, u32[]{:S(2)}) %collective-permute-start.10) | collective-permute-done | bytes 327712 | tf_op jit(solution)/shard_map/ppermute | solution.py:201
  75.8 6.2 %collective-permute-done.8 = bf16[256,640]{1,0:T(8,128)(2,1)S(1)} collective-permute-done((bf16[256,640]{1,0:T(8,128)(2,1)S(1)}, bf16[256,640]{1,0:T(8,128)(2,1)S(1)}, u32[]{:S(2)}, u32[]{:S(2)}) %collective-permute-start.8) | collective-permute-done | bytes 327712 | tf_op jit(solution)/shard_map/ppermute | solution.py:199
  82.0 0.0 collective-permute-done.9
  82.0 0.2 fusion.3
  82.2 0.7 gather_fusion.1
  82.9 0.2 select_select_fusion
  83.1 24.8 %all_to_all.15 = bf16[32,16,640]{2,1,0:T(8,128)(2,1)S(1)} all-to-all(bf16[32,16,640]{2,1,0:T(8,128)(2,1)S(1)} %select_select_fusion), channel_id=1, replica_groups=mesh['seq'=32,'tp'=8] {'seq'}, dimensions={0} | all-to-all | bytes 1310720 | tf_op jit(solution)/shard_map/all_to_all | solution.py:213
  107.8 0.8 copy.10
  (10 shorter events, 0.1 us)
Async XLA Ops:
  0.0 60.2 %copy-start = (s32[512,1]{0,1:T(1,128)S(1)}, s32[512,1]{0,1:T(1,128)}, u32[]{:S(2)}) copy-start(s32[512,1]{0,1:T(1,128)} %param.10) | copy-start | bytes 6148
  0.0 33.0 %collective-permute-start = (bf16[256,640]{1,0:T(8,128)(2,1)}, bf16[256,640]{1,0:T(8,128)(2,1)S(1)}, u32[]{:S(2)}, u32[]{:S(2)}) collective-permute-start(bf16[256,640]{1,0:T(8,128)(2,1)} %bitcast.33), channel_id=1, source_target_pairs={{0,2},{1,3},{2,4},{3,5},{4,6},{5,7},{6,0},{7,1},{8,10},{9,11},{10,... | collective-permute-start | bytes 983048 | tf_op jit(solution)/shard_map/ppermute | solution.py:173
  1.6 31.6 %collective-permute-start.1 = (bf16[256,640]{1,0:T(8,128)(2,1)}, bf16[256,640]{1,0:T(8,128)(2,1)S(1)}, u32[]{:S(2)}, u32[]{:S(2)}) collective-permute-start(bf16[256,640]{1,0:T(8,128)(2,1)} %bitcast.34), channel_id=1, source_target_pairs={{0,6},{1,7},{2,0},{3,1},{4,2},{5,3},{6,4},{7,5},{8,14},{9,15},{10,... | collective-permute-start | bytes 983048 | tf_op jit(solution)/shard_map/ppermute | solution.py:174
  3.2 30.4 %collective-permute-start.2 = (bf16[256,640]{1,0:T(8,128)(2,1)}, bf16[256,640]{1,0:T(8,128)(2,1)S(1)}, u32[]{:S(2)}, u32[]{:S(2)}) collective-permute-start(bf16[256,640]{1,0:T(8,128)(2,1)} %bitcast.35), channel_id=1, source_target_pairs={{0,4},{1,5},{2,6},{3,7},{4,0},{5,1},{6,2},{7,3},{8,12},{9,13},{10,... | collective-permute-start | bytes 983048 | tf_op jit(solution)/shard_map/ppermute | solution.py:175
  5.2 28.8 %collective-permute-start.3 = (bf16[256,640]{1,0:T(8,128)(2,1)}, bf16[256,640]{1,0:T(8,128)(2,1)S(1)}, u32[]{:S(2)}, u32[]{:S(2)}) collective-permute-start(bf16[256,640]{1,0:T(8,128)(2,1)} %bitcast.36), channel_id=1, source_target_pairs={{0,1},{1,0},{2,3},{3,2},{4,5},{5,4},{6,7},{7,6},{8,9},{9,8},{10,11... | collective-permute-start | bytes 983048 | tf_op jit(solution)/shard_map/ppermute | solution.py:177
  5.2 20.8 %all-to-all-start = ((bf16[32,16,128]{2,1,0:T(8,128)(2,1)}), bf16[32,16,128]{2,1,0:T(8,128)(2,1)S(1)}, u32[]{:S(2)}, u32[]{:S(2)}) async-start(bf16[32,16,128]{2,1,0:T(8,128)(2,1)} %bitcast.39), calls=%async_computation | async-start | bytes 262144 | tf_op jit(solution)/shard_map/all_to_all | solution.py:168
  27.4 14.6 %all-to-all-start.1 = ((bf16[32,16,128]{2,1,0:T(8,128)(2,1)}), bf16[32,16,128]{2,1,0:T(8,128)(2,1)S(1)}, u32[]{:S(2)}, u32[]{:S(2)}) async-start(bf16[32,16,128]{2,1,0:T(8,128)(2,1)} %broadcast_select_fusion), calls=%async_computation.1 | async-start | bytes 262144 | tf_op jit(solution)/shard_map/all_to_all | solution.py:170
  33.0 8.9 %collective-permute-start.4 = (bf16[256,640]{1,0:T(8,128)(2,1)S(1)}, bf16[256,640]{1,0:T(8,128)(2,1)S(1)}, u32[]{:S(2)}, u32[]{:S(2)}) collective-permute-start(bf16[256,640]{1,0:T(8,128)(2,1)S(1)} %collective-permute-done.refs_1_), channel_id=1, source_target_pairs={{0,1},{1,0},{2,3},{3,2},{4,5},{5,4},{6,7},{7,6},{8,9},{9,8},{10,11... | collective-permute-start | bytes 983048 | tf_op jit(solution)/shard_map/ppermute | solution.py:177
  33.2 8.8 %collective-permute-start.5 = (bf16[256,640]{1,0:T(8,128)(2,1)S(1)}, bf16[256,640]{1,0:T(8,128)(2,1)S(1)}, u32[]{:S(2)}, u32[]{:S(2)}) collective-permute-start(bf16[256,640]{1,0:T(8,128)(2,1)S(1)} %collective-permute-done.1.refs_2_), channel_id=1, source_target_pairs={{0,1},{1,0},{2,3},{3,2},{4,5},{5,4},{6,7},{7,6},{8,9},{9,8},{10,11... | collective-permute-start | bytes 983048 | tf_op jit(solution)/shard_map/ppermute | solution.py:177
  33.6 8.3 %collective-permute-start.6 = (bf16[256,640]{1,0:T(8,128)(2,1)S(1)}, bf16[256,640]{1,0:T(8,128)(2,1)S(1)}, u32[]{:S(2)}, u32[]{:S(2)}) collective-permute-start(bf16[256,640]{1,0:T(8,128)(2,1)S(1)} %collective-permute-done.2.refs_3_), channel_id=1, source_target_pairs={{0,1},{1,0},{2,3},{3,2},{4,5},{5,4},{6,7},{7,6},{8,9},{9,8},{10,11... | collective-permute-start | bytes 983048 | tf_op jit(solution)/shard_map/ppermute | solution.py:177
  42.1 2.1 %copy-start.1 = (bf16[5120,384]{1,0:T(8,128)(2,1)S(1)}, bf16[5120,384]{1,0:T(8,128)(2,1)}, u32[]{:S(2)}) copy-start(bf16[5120,384]{1,0:T(8,128)(2,1)} %refs_8_.1) | copy-start | bytes 11796484
  44.2 2.1 %copy-start.2 = (bf16[384,5120]{1,0:T(8,128)(2,1)S(1)}, bf16[384,5120]{1,0:T(8,128)(2,1)}, u32[]{:S(2)}) copy-start(bf16[384,5120]{1,0:T(8,128)(2,1)} %refs_14_.1) | copy-start | bytes 11796484
  46.4 1.7 %copy-start.3 = (bf16[2,5120,128]{2,1,0:T(8,128)(2,1)S(1)}, bf16[2,5120,128]{2,1,0:T(8,128)(2,1)}, u32[]{:S(2)}) copy-start(bf16[2,5120,128]{2,1,0:T(8,128)(2,1)} %refs_9_.1) | copy-start | bytes 7864324
  48.1 1.0 copy-start.4
  59.9 3.3 %collective-permute-start.7 = (bf16[4,256,640]{2,1,0:T(8,128)(2,1)S(1)}, bf16[4,256,640]{2,1,0:T(8,128)(2,1)S(1)}, u32[]{:S(2)}, u32[]{:S(2)}) collective-permute-start(bf16[4,256,640]{2,1,0:T(8,128)(2,1)S(1)} %get-tuple-element.8), channel_id=1, source_target_pairs={{0,1},{1,0},{2,3},{3,2},{4,5},{5,4},{6,7},{7,6},{8,9},{9,8},{10,11... | collective-permute-start | bytes 3932168 | tf_op jit(solution)/shard_map/ppermute | solution.py:195
  63.7 12.2 %collective-permute-start.10 = (bf16[256,640]{1,0:T(8,128)(2,1)S(1)}, bf16[256,640]{1,0:T(8,128)(2,1)S(1)}, u32[]{:S(2)}, u32[]{:S(2)}) collective-permute-start(bf16[256,640]{1,0:T(8,128)(2,1)S(1)} %get-tuple-element.16), channel_id=1, source_target_pairs={{0,4},{1,5},{2,6},{3,7},{4,0},{5,1},{6,2},{7,3},{8,12},{9,13},{10,... | collective-permute-start | bytes 983048 | tf_op jit(solution)/shard_map/ppermute | solution.py:201
  65.3 16.7 %collective-permute-start.8 = (bf16[256,640]{1,0:T(8,128)(2,1)S(1)}, bf16[256,640]{1,0:T(8,128)(2,1)S(1)}, u32[]{:S(2)}, u32[]{:S(2)}) collective-permute-start(bf16[256,640]{1,0:T(8,128)(2,1)S(1)} %get-tuple-element.15), channel_id=1, source_target_pairs={{0,2},{1,3},{2,4},{3,5},{4,6},{5,7},{6,0},{7,1},{8,10},{9,11},{10,... | collective-permute-start | bytes 983048 | tf_op jit(solution)/shard_map/ppermute | solution.py:199
  65.7 16.4 %collective-permute-start.9 = (bf16[256,640]{1,0:T(8,128)(2,1)S(1)}, bf16[256,640]{1,0:T(8,128)(2,1)S(1)}, u32[]{:S(2)}, u32[]{:S(2)}) collective-permute-start(bf16[256,640]{1,0:T(8,128)(2,1)S(1)} %get-tuple-element.17), channel_id=1, source_target_pairs={{0,6},{1,7},{2,0},{3,1},{4,2},{5,3},{6,4},{7,5},{8,14},{9,15},{10,... | collective-permute-start | bytes 983048 | tf_op jit(solution)/shard_map/ppermute | solution.py:200

commit v2 on v1

v2 whole, which is shorter than its diff:
```python
import functools
import math

import jax
import jax.numpy as jnp
from jax import lax
from jax.experimental import pallas as pl
from jax.experimental.pallas import tpu as pltpu
from jax.sharding import PartitionSpec as P

HD = 128
PL = 256
ROPE_BASE = 1000000.0
CHIPS = 4
CORES = 2


def chip_shift(step):
    return [
        (y * CORES + c, ((y + step) % CHIPS) * CORES + c) for y in range(CHIPS) for c in range(CORES)
    ]


CORE_SWAP = [(i, i ^ 1) for i in range(CHIPS * CORES)]


def rope_tables(count, rows):
    places = (PL + jnp.arange(count)).astype(jnp.float32)
    freqs = ROPE_BASE ** (-(jnp.arange(HD // 2).astype(jnp.float32) * 2.0 / HD))
    angles = places[:, None] * freqs[None, :]
    cosine, sine = jnp.cos(angles), jnp.sin(angles)
    cosine = jnp.concatenate([cosine, cosine], -1)
    sine = jnp.concatenate([-sine, sine], -1)
    return jnp.tile(cosine, (rows // count, 1)), jnp.tile(sine, (rows // count, 1))


VMEM = pl.BlockSpec(memory_space=pltpu.VMEM)
SMEM = pl.BlockSpec(memory_space=pltpu.SMEM)
ANY = pl.BlockSpec(memory_space=pl.ANY)


def in_hbm(x):
    return pltpu.with_memory_space_constraint(x, pltpu.HBM)


def params(mib):
    return pltpu.CompilerParams(vmem_limit_bytes=mib * 1024 * 1024)


def place_in_column(shifts, far):
    me = lax.axis_index("tp")
    y, c = me // CORES, me % CORES
    core = 1 - c if far else c
    return [((y + shift + CHIPS) % CHIPS) * CORES + core for shift in shifts]


def columns_at(index, width):
    return pl.ds(pl.multiple_of(index * width, width), width)


def route_kernel(pick_ref, piece_ref, out_ref):
    count, size, width = piece_ref.shape
    pieces = piece_ref[...].reshape(count * size, width)
    picked = jnp.dot(pick_ref[...], pieces, preferred_element_type=jnp.float32)
    out_ref[...] = picked.astype(jnp.bfloat16).reshape(count, size, width)


def route(pick, pieces):
    return pl.pallas_call(
        route_kernel,
        in_specs=[VMEM, VMEM],
        out_specs=VMEM,
        out_shape=jax.ShapeDtypeStruct(pieces.shape, pieces.dtype),
        compiler_params=params(8),
    )(pick, pieces)


def weight_row_copies(i, index, wq_hbm, wkv_hbm, weights, sems):
    width = weights.shape[1]
    first = wq_hbm.shape[1]
    at = columns_at(index, width)
    return (
        pltpu.make_async_copy(wq_hbm.at[at, :], weights.at[i, :, 0:first], sems.at[0, i]),
        pltpu.make_async_copy(
            wkv_hbm.at[0, at, :], weights.at[i, :, first : first + HD], sems.at[1, i]
        ),
        pltpu.make_async_copy(
            wkv_hbm.at[1, at, :], weights.at[i, :, first + HD : first + 2 * HD], sems.at[2, i]
        ),
    )


def project_pairs(rows_ref, weights, copies):
    _, width, columns = weights.shape
    total = None
    for pair in range(len(copies) // 2):
        for copy in copies[2 * pair] + copies[2 * pair + 1]:
            copy.wait()
        part = jnp.dot(
            rows_ref[:, 2 * pair * width : 2 * (pair + 1) * width],
            weights[2 * pair : 2 * (pair + 1)].reshape(2 * width, columns),
            preferred_element_type=jnp.float32,
        )
        total = part if total is None else total + part
    return total


def project_kernel(x_hbm, *refs):
    shards = refs[:7]
    wq_hbm, wkv_hbm, cos_ref, sin_ref = refs[7:11]
    q_ref, k_ref, v_ref, rows_ref, weights, sems, x_sem = refs[11:]
    width = weights.shape[1]
    heads = q_ref.shape[0]
    near = place_in_column((0, -1, 1, 2), False)
    far = place_in_column((0, -1, 1, 2), True)
    order = [index for pair in zip(near, far) for index in pair]
    own = pltpu.make_async_copy(x_hbm, rows_ref.at[:, 0:width], x_sem)
    own.start()
    copies = [
        weight_row_copies(i, index, wq_hbm, wkv_hbm, weights, sems) for i, index in enumerate(order)
    ]
    for triple in copies:
        for copy in triple:
            copy.start()
    for i, shard in enumerate(shards):
        rows_ref[:, (i + 1) * width : (i + 2) * width] = shard[...]
    own.wait()
    both = project_pairs(rows_ref, weights, copies)
    cosine, sine = cos_ref[...], sin_ref[...]

    def rotated(h):
        v = both[:, h * HD : (h + 1) * HD]
        return (v * cosine + pltpu.roll(v, HD // 2, 1) * sine).astype(jnp.bfloat16)

    for h in range(heads):
        q_ref[h] = rotated(h)
    k_ref[...] = rotated(heads)
    v_ref[...] = both[:, (heads + 1) * HD :].astype(jnp.bfloat16)


def project(x, shards, w_query, w_keyval, cosine, sine):
    rows, width = x.shape
    heads = w_query.shape[1] // HD
    columns = (heads + 2) * HD
    return pl.pallas_call(
        project_kernel,
        in_specs=[ANY] + [VMEM] * 7 + [ANY] * 2 + [VMEM] * 2,
        out_specs=[VMEM] * 3,
        out_shape=[
            jax.ShapeDtypeStruct((heads, rows, HD), jnp.bfloat16),
            jax.ShapeDtypeStruct((rows, HD), jnp.bfloat16),
            jax.ShapeDtypeStruct((rows, HD), jnp.bfloat16),
        ],
        scratch_shapes=[
            pltpu.VMEM((rows, 8 * width), jnp.bfloat16),
            pltpu.VMEM((8, width, columns), jnp.bfloat16),
            pltpu.SemaphoreType.DMA((3, 8)),
            pltpu.SemaphoreType.DMA,
        ],
        compiler_params=params(16),
        cost_estimate=pl.CostEstimate(
            flops=2 * rows * 8 * width * columns,
            bytes_accessed=16 * width * columns,
            transcendentals=0,
        ),
    )(in_hbm(x), *shards, in_hbm(w_query), in_hbm(w_keyval), cosine, sine)


def out_weight_copies(i, shift, near_hbm, far_hbm, wo_ref, sems):
    depth = near_hbm.shape[0]
    at = columns_at(place_in_column((shift,), False)[0], wo_ref.shape[2])
    return (
        pltpu.make_async_copy(near_hbm.at[:, at], wo_ref.at[i, 0:depth, :], sems.at[0, i]),
        pltpu.make_async_copy(far_hbm.at[:, at], wo_ref.at[i, depth : 2 * depth, :], sems.at[1, i]),
    )


def attend_kernel(
    tokens,
    shift,
    q_ref,
    k_ref,
    v_ref,
    cache_ref,
    valid_ref,
    near_hbm,
    far_hbm,
    attn_ref,
    wo_ref,
    sems,
):
    copies = out_weight_copies(0, shift, near_hbm, far_hbm, wo_ref, sems)
    for copy in copies:
        copy.start()
    heads, rows, _ = q_ref.shape
    scale = 1.0 / math.sqrt(HD)
    half = cache_ref.shape[0] // 2
    keys = jnp.concatenate([cache_ref[:half].reshape(PL, HD), k_ref[...]], 0)
    values = jnp.concatenate([cache_ref[half:].reshape(PL, HD), v_ref[...]], 0)
    row = lax.broadcasted_iota(jnp.int32, (rows, rows), 0)
    col = lax.broadcasted_iota(jnp.int32, (rows, rows), 1)
    seen = (row // tokens == col // tokens) & (col <= row)
    valid = valid_ref[...] > 0.0
    nt = (((1,), (1,)), ((), ()))
    scores = [
        lax.dot_general(q_ref[h], keys, nt, preferred_element_type=jnp.float32) * scale
        for h in range(heads)
    ]
    for h in range(heads):
        prior = scores[h][:, :PL]
        recent = jnp.where(seen, scores[h][:, PL:], -1e30)
        top = jnp.max(jnp.maximum(prior, recent), -1, keepdims=True)
        prior = jnp.exp(prior - top)
        recent = jnp.exp(recent - top)
        inverse = 1.0 / jnp.sum(prior + recent, -1, keepdims=True)
        weights = jnp.concatenate(
            [(prior * inverse).astype(jnp.bfloat16), (recent * inverse).astype(jnp.bfloat16)], -1
        )
        mixed = jnp.dot(weights, values, preferred_element_type=jnp.float32)
        attn_ref[:, h * HD : (h + 1) * HD] = jnp.where(valid, mixed, 0.0).astype(jnp.bfloat16)
    for copy in copies:
        copy.wait()


def attend(shift, queries, keys, values, cache, valid, out_near, out_far, tokens):
    heads, rows, _ = queries.shape
    depth, width = out_near.shape[0], out_near.shape[1] // (CHIPS * CORES)
    return pl.pallas_call(
        functools.partial(attend_kernel, tokens, shift),
        in_specs=[VMEM] * 5 + [ANY] * 2,
        out_specs=[VMEM] * 2,
        out_shape=[
            jax.ShapeDtypeStruct((rows, heads * HD), jnp.bfloat16),
            jax.ShapeDtypeStruct((1, 2 * depth, width), jnp.bfloat16),
        ],
        scratch_shapes=[pltpu.SemaphoreType.DMA((2, 1))],
        compiler_params=params(8),
        cost_estimate=pl.CostEstimate(
            flops=8 * heads * rows * PL * HD,
            bytes_accessed=4 * rows * heads * HD + 4 * depth * width,
            transcendentals=2 * heads * rows * PL,
        ),
    )(queries, keys, values, cache, valid, in_hbm(out_near), in_hbm(out_far))


def fetch_kernel(shift, after_ref, near_hbm, far_hbm, wo_ref, sems):
    del after_ref
    copies = out_weight_copies(0, shift, near_hbm, far_hbm, wo_ref, sems)
    for copy in copies:
        copy.start()
    for copy in copies:
        copy.wait()


def fetch(shift, after, out_near, out_far):
    depth, width = out_near.shape[0], out_near.shape[1] // (CHIPS * CORES)
    return pl.pallas_call(
        functools.partial(fetch_kernel, shift),
        in_specs=[ANY] * 3,
        out_specs=VMEM,
        out_shape=jax.ShapeDtypeStruct((1, 2 * depth, width), jnp.bfloat16),
        scratch_shapes=[pltpu.SemaphoreType.DMA((2, 1))],
        compiler_params=params(8),
        cost_estimate=pl.CostEstimate(
            flops=0, bytes_accessed=8 * depth * width, transcendentals=0
        ),
    )(after, in_hbm(out_near), in_hbm(out_far))


def output_kernel(ready, shifts, near_ref, far_ref, *refs):
    ready_refs = refs[:ready]
    refs = refs[ready:]
    copies = []
    if shifts:
        near_hbm, far_hbm = refs[:2]
        wo_ref, sems = refs[-2:]
        refs = refs[2:-2]
        copies = [
            out_weight_copies(i, shift, near_hbm, far_hbm, wo_ref, sems)
            for i, shift in enumerate(shifts)
        ]
    for pair in copies:
        for copy in pair:
            copy.start()
    both = jnp.concatenate([near_ref[...], far_ref[...]], -1)
    for i, out_ref in enumerate(refs):
        if i < ready:
            weights = ready_refs[i][0]
        else:
            for copy in copies[i - ready]:
                copy.wait()
            weights = wo_ref[i - ready]
        block = jnp.dot(both, weights, preferred_element_type=jnp.float32)
        out_ref[...] = block.astype(out_ref.dtype)


def output(near, far, ready, shifts, out_near, out_far, dtype):
    rows = near.shape[0]
    depth, width = out_near.shape[0], out_near.shape[1] // (CHIPS * CORES)
    count = len(ready) + len(shifts)
    hbm = [in_hbm(out_near), in_hbm(out_far)] if shifts else []
    scratch = [
        pltpu.VMEM((len(shifts), 2 * depth, width), jnp.bfloat16),
        pltpu.SemaphoreType.DMA((2, len(shifts))),
    ]
    return pl.pallas_call(
        functools.partial(output_kernel, len(ready), shifts),
        in_specs=[VMEM] * (2 + len(ready)) + [ANY] * len(hbm),
        out_specs=[VMEM] * count,
        out_shape=[jax.ShapeDtypeStruct((rows, width), dtype)] * count,
        scratch_shapes=scratch if shifts else [],
        compiler_params=params(8),
        cost_estimate=pl.CostEstimate(
            flops=4 * count * rows * depth * width,
            bytes_accessed=4 * count * depth * width,
            transcendentals=0,
        ),
    )(near, far, *ready, *hbm)


def place_kernel(pick_ref, mine_ref, *refs):
    parts, out_ref = refs[:3], refs[3]
    total = mine_ref[...]
    for part in parts:
        total = total + part[...].astype(jnp.float32)
    placed = jnp.dot(
        pick_ref[...], total.astype(jnp.bfloat16), preferred_element_type=jnp.float32
    )
    out_ref[...] = placed.astype(jnp.bfloat16).reshape(out_ref.shape)


def place(pick, mine, parts, slots, tokens):
    _, width = mine.shape
    return pl.pallas_call(
        place_kernel,
        in_specs=[VMEM] * 5,
        out_specs=VMEM,
        out_shape=jax.ShapeDtypeStruct((slots, tokens, width), jnp.bfloat16),
        compiler_params=params(8),
    )(pick, mine, *parts)


def block_picks(source, size, count):
    rows = source[:, None] * size + jnp.arange(size)[None, :]
    rows = jnp.where(source[:, None] >= 0, rows, -1).reshape(-1)
    return (rows[:, None] == jnp.arange(count * size)[None, :]).astype(jnp.bfloat16)


def per_device(resp_rows, resp_len, resp_shard, group_prompt, prompt_kv, w_query, w_keyval, w_out):
    learners = lax.axis_size("seq")
    group = lax.axis_index("seq")
    group_size, tokens, width = resp_rows.shape
    rows = group_size * tokens

    pieces = prompt_kv.reshape(learners, -1, HD)
    prompt_picks = block_picks(group_prompt, pieces.shape[1], learners)
    pieces = lax.all_to_all(pieces, "seq", 0, 0, tiled=True)

    x = resp_rows.reshape(rows, width)
    swap = lambda v: lax.ppermute(v, "tp", CORE_SWAP)
    below = lax.ppermute(x, "tp", chip_shift(1))
    above = lax.ppermute(x, "tp", chip_shift(-1))
    across = lax.ppermute(x, "tp", chip_shift(2))
    cache = lax.all_to_all(route(prompt_picks, pieces), "seq", 0, 0, tiled=True)
    out_far = swap(w_out)
    shards = [swap(x), below, swap(below), above, swap(above), across, swap(across)]

    own_len = lax.dynamic_slice_in_dim(resp_len, group * group_size, group_size, 0)
    valid = (jnp.arange(tokens)[None, :] < own_len[:, None]).astype(jnp.float32)
    valid = jnp.broadcast_to(valid.reshape(rows, 1), (rows, HD))
    cosine, sine = rope_tables(tokens, rows)
    own_shard = lax.dynamic_slice_in_dim(resp_shard[:, 0], group * group_size, group_size, 0)
    match = own_shard[None, :] == jnp.arange(learners)[:, None]
    pick = jnp.max(jnp.where(match, jnp.arange(group_size)[None, :], -1), -1)
    slot_picks = block_picks(pick, tokens, group_size)

    queries, keys, values = project(x, shards, w_query, w_keyval, cosine, sine)
    attn, w_across = attend(2, queries, keys, values, cache, valid, w_out, out_far, tokens)
    attn_far = swap(attn)
    w_above = fetch(1, attn, w_out, out_far)
    (to_across,) = output(attn, attn_far, [w_across], (), w_out, out_far, jnp.bfloat16)
    to_across, attn_far = lax.optimization_barrier((to_across, attn_far))
    to_above, to_below = output(
        attn, attn_far, [w_above], (-1,), w_out, out_far, jnp.bfloat16
    )
    (mine,) = output(attn, attn_far, [], (0,), w_out, out_far, jnp.float32)
    parts = [
        lax.ppermute(to_across, "tp", chip_shift(2)),
        lax.ppermute(to_above, "tp", chip_shift(1)),
        lax.ppermute(to_below, "tp", chip_shift(-1)),
    ]
    slots = place(slot_picks, mine, parts, learners, tokens)
    return lax.all_to_all(slots, "seq", 0, 0, tiled=True)


def solution(mesh):
    return jax.shard_map(
        per_device,
        mesh=mesh,
        in_specs=(
            P("seq", None, "tp"),
            P(),
            P(),
            P(),
            P(None, "seq", None, "tp"),
            P(None, "tp"),
            P(None, None, "tp"),
            P("tp", None),
        ),
        out_specs=P("seq", None, "tp"),
        check_vma=False,
    )
```

time: 109 us -> 94 us (0.86)
  waiting for transfers between devices: 30.9 us -> 21.5 us
  local copies, waits for them, and re-layouts: 10.1 us -> 2.03 us
  Pallas kernels: 10.8 us -> 14.7 us
  other arithmetic: 3.51 us -> 2.16 us
  starting transfers between devices: 28.3 us -> 27 us
  blocking collectives: 24.8 us -> 26 us
    unnamed x11 -> x3, local copies, waits for them, and re-layouts: 7.77 us -> 0.84 us
    all_to_all x1, waiting for transfers between devices: 7.92 us -> 3 us  [per_device(): cache = lax.all_to_all(route(prompt_picks, pieces), 'seq', 0, 0, tiled=True)]
    pallas_call x1 -> x8, Pallas kernels: 10.8 us -> 14.7 us  [the longest x1 5.96 us: project(): pl.pallas_call(project_kernel, in_specs=[ANY] + [VMEM] * 7 + [ANY] * 2 +...]
    ppermute x8 -> x9, waiting for transfers between devices: 16.2 us -> 12.9 us  [the longest x1 6.27 us: per_device(): lax.ppermute(to_above, 'tp', chip_shift(1))]
    select_n x4 -> x2, other arithmetic: 1.6 us -> 0.15 us  [block_picks(): rows = jnp.where(source[:, None] >= 0, rows, -1).reshape(-1)]
    ppermute x8 -> x9, starting transfers between devices: 5.83 us -> 4.47 us  [the longest x1 2.32 us: per_device(): lax.ppermute(to_below, 'tp', chip_shift(-1))]
    all_to_all x1, blocking collectives: 24.8 us -> 26 us  [per_device(): return lax.all_to_all(slots, 'seq', 0, 0, tiled=True)]
    gather x2 -> x0, local copies, waits for them, and re-layouts: 1.26 us -> none  [the longest x1 0.67 us: per_device(): slots = jnp.where(filled[:, None, None], jnp.take(total, pick, axis=0), 0)]
  transfers between devices with their start and end apart: 13 -> 14, of which waited for: 5 -> 6; matrix products, arithmetic and copies ran while one was open for 4% -> 3% of each run, Pallas kernels for 0% -> 11%
where the time goes in v2:
time: 94 us; the launch traced here: 93.6 us
  starting transfers between devices  27 us (29%)
  blocking collectives  26 us (28%)
  waiting for transfers between devices  21.5 us (23%)
  Pallas kernels  14.7 us (16%)
  other arithmetic  2.16 us (2%)
  local copies, waits for them, and re-layouts  2.03 us (2%)
    all_to_all x1, blocking collectives, per_device(): return lax.all_to_all(slots, 'seq', 0, 0, tiled=True)  26 us
    all_to_all x1, starting transfers between devices, per_device(): pieces = lax.all_to_all(pieces, 'seq', 0, 0, tiled=True)  11.6 us
    ppermute x1, waiting for transfers between devices, per_device(): lax.ppermute(to_above, 'tp', chip_shift(1))  6.27 us
    pallas_call x1, Pallas kernels, project(): pl.pallas_call(project_kernel, in_specs=[ANY] + [VMEM] * 7 + [ANY] * 2 +...  5.96 us
    ppermute x1, waiting for transfers between devices, per_device(): lax.ppermute(to_below, 'tp', chip_shift(-1))  5.73 us
    all_to_all x1, starting transfers between devices, per_device(): cache = lax.all_to_all(route(prompt_picks, pieces), 'seq', 0, 0, tiled=True)  5.64 us
    all_to_all x1, waiting for transfers between devices, per_device(): pieces = lax.all_to_all(pieces, 'seq', 0, 0, tiled=True)  5.56 us
    pallas_call x3, Pallas kernels, output(): pl.pallas_call(functools.partial(output_kernel, len(ready), shifts), in_s...  4.22 us
  transfers between devices with their start and end apart: 14, of which 6 were waited for; matrix products, arithmetic and copies ran while one was open for 3% of the time, Pallas kernels for 11%

profile of v2, /device:TPU:2, one launch (start us, length us, event | category | flops | bytes accessed | tf_op | source)
XLA Modules:
  0.0 93.6 jit_solution(12786831453491898529)
XLA Ops:
  0.0 0.0 copy-start
  0.0 0.0 collective-permute-start.7
  0.0 1.7 %collective-permute-start.1 = (bf16[256,640]{1,0:T(8,128)(2,1)}, bf16[256,640]{1,0:T(8,128)(2,1)S(1)}, u32[]{:S(2)}, u32[]{:S(2)}) collective-permute-start(bf16[256,640]{1,0:T(8,128)(2,1)} %bitcast.8), channel_id=1, source_target_pairs={{0,2},{1,3},{2,4},{3,5},{4,6},{5,7},{6,0},{7,1},{8,10},{9,11},{10,... | collective-permute-start | bytes 983048 | tf_op jit(solution)/shard_map/ppermute | solution.py:361
  1.7 1.7 %collective-permute-start.3 = (bf16[256,640]{1,0:T(8,128)(2,1)}, bf16[256,640]{1,0:T(8,128)(2,1)S(1)}, u32[]{:S(2)}, u32[]{:S(2)}) collective-permute-start(bf16[256,640]{1,0:T(8,128)(2,1)} %bitcast.9), channel_id=1, source_target_pairs={{0,6},{1,7},{2,0},{3,1},{4,2},{5,3},{6,4},{7,5},{8,14},{9,15},{10,... | collective-permute-start | bytes 983048 | tf_op jit(solution)/shard_map/ppermute | solution.py:362
  3.3 2.0 %collective-permute-start.5 = (bf16[256,640]{1,0:T(8,128)(2,1)}, bf16[256,640]{1,0:T(8,128)(2,1)S(1)}, u32[]{:S(2)}, u32[]{:S(2)}) collective-permute-start(bf16[256,640]{1,0:T(8,128)(2,1)} %bitcast.10), channel_id=1, source_target_pairs={{0,4},{1,5},{2,6},{3,7},{4,0},{5,1},{6,2},{7,3},{8,12},{9,13},{10,... | collective-permute-start | bytes 983048 | tf_op jit(solution)/shard_map/ppermute | solution.py:363
  5.3 0.0 collective-permute-start
  5.3 11.6 %all-to-all-start = ((bf16[32,16,128]{2,1,0:T(8,128)(2,1)}), bf16[32,16,128]{2,1,0:T(8,128)(2,1)S(1)}, u32[]{:S(2)}, u32[]{:S(2)}) async-start(bf16[32,16,128]{2,1,0:T(8,128)(2,1)} %bitcast.13), calls=%async_computation | async-start | bytes 262144 | tf_op jit(solution)/shard_map/all_to_all | solution.py:357
  16.9 0.7 broadcast_compare_fusion
  17.6 0.7 broadcast_multiply_fusion
  18.3 0.1 add_select_fusion
  18.3 0.1 select_n.34
  18.4 0.8 dynamic_slice.7
  19.2 0.0 copy-done
  19.2 0.1 dynamic-slice_bitcast_fusion
  19.3 0.1 fusion.3
  19.4 0.2 fusion.pick_ref
  19.6 0.1 fusion.2
  19.6 0.1 select_reduce_fusion
  19.7 0.1 reshape.108
  19.8 0.0 collective-permute-done.1.refs_1_
  19.8 0.1 collective-permute-start.2
  19.9 0.0 collective-permute-done.3.refs_3_
  19.9 0.5 collective-permute-start.4
  20.4 0.0 collective-permute-done.5.refs_5_
  20.4 0.1 collective-permute-start.6
  20.6 5.6 %all-to-all-done.piece_ref = bf16[32,16,128]{2,1,0:T(8,128)(2,1)S(1)} async-done(((bf16[32,16,128]{2,1,0:T(8,128)(2,1)}), bf16[32,16,128]{2,1,0:T(8,128)(2,1)S(1)}, u32[]{:S(2)}, u32[]{:S(2)}) %all-to-all-start) | async-done | bytes 131104 | tf_op jit(solution)/shard_map/all_to_all | solution.py:357
  26.1 1.0 %shard_map.83 = bf16[32,16,128]{2,1,0:T(8,128)(2,1)} custom-call(bf16[512,512]{1,0:T(8,128)(2,1)S(1)} %fusion.pick_ref, bf16[32,16,128]{2,1,0:T(8,128)(2,1)S(1)} %all-to-all-done.piece_ref), custom_call_target="tpu_custom_call" | custom-call | tf_op jit(solution)/shard_map/pallas_call | solution.py:69
  27.1 5.6 %all-to-all-start.1 = ((bf16[32,16,128]{2,1,0:T(8,128)(2,1)}), bf16[32,16,128]{2,1,0:T(8,128)(2,1)S(1)}, u32[]{:S(2)}, u32[]{:S(2)}) async-start(bf16[32,16,128]{2,1,0:T(8,128)(2,1)} %shard_map.83), calls=%async_computation.1 | async-start | bytes 262144 | tf_op jit(solution)/shard_map/all_to_all | solution.py:364
  32.7 0.1 pad_maximum_fusion
  32.8 0.0 collective-permute-done.refs_0_
  32.8 0.0 collective-permute-done.2.refs_2_
  32.8 0.0 collective-permute-done.4.refs_4_
  32.8 0.0 collective-permute-done.6.refs_6_
  32.9 6.0 %shard_map.82 = (bf16[3,256,128]{2,1,0:T(8,128)(2,1)S(1)}, bf16[256,128]{1,0:T(8,128)(2,1)S(1)}, bf16[256,128]{1,0:T(8,128)(2,1)S(1)}) custom-call(bf16[256,640]{1,0:T(8,128)(2,1)} %bitcast.12, bf16[256,640]{1,0:T(8,128)(2,1)S(1)} %collective-permute-done.refs_0_, bf16[256,640]{1,0:T(8,128)(2,1)S(1)} %collective-permute-done.1.refs_1_, ...), custom_call_target="tpu_custom_call" | custom-call | flops 1677721600 | bytes 6553600 | tf_op jit(solution)/shard_map/pallas_call | solution.py:145
  38.8 3.0 %all-to-all-done.1.cache_ref = bf16[32,16,128]{2,1,0:T(8,128)(2,1)S(1)} async-done(((bf16[32,16,128]{2,1,0:T(8,128)(2,1)}), bf16[32,16,128]{2,1,0:T(8,128)(2,1)S(1)}, u32[]{:S(2)}, u32[]{:S(2)}) %all-to-all-start.1) | async-done | bytes 131104 | tf_op jit(solution)/shard_map/all_to_all | solution.py:364
  41.8 0.0 collective-permute-done.7.far_hbm.refs_1_.refs_2_
  41.8 0.1 broadcast_in_dim.58.valid_ref
  41.9 1.9 %shard_map.84 = (bf16[256,384]{1,0:T(8,128)(2,1)S(1)}, bf16[1,768,640]{2,1,0:T(8,128)(2,1)S(1)}) custom-call(bf16[3,256,128]{2,1,0:T(8,128)(2,1)S(1)} %get-tuple-element.14.q_ref, bf16[256,128]{1,0:T(8,128)(2,1)S(1)} %get-tuple-element.15.k_ref, bf16[256,128]{1,0:T(8,128)(2,1)S(1)} %get-tuple-element.16.v_ref, ...), custom_call_target="tpu_custom_call" | custom-call | flops 201326592 | bytes 1376256 | tf_op jit(solution)/shard_map/pallas_call | solution.py:228
  43.8 0.1 collective-permute-start.8
  44.0 1.2 %shard_map.87.refs_0_ = bf16[1,768,640]{2,1,0:T(8,128)(2,1)S(1)} custom-call(bf16[256,384]{1,0:T(8,128)(2,1)S(1)} %get-tuple-element.17.near_ref.after_ref, bf16[384,5120]{1,0:T(8,128)(2,1)} %refs_1_.1, bf16[384,5120]{1,0:T(8,128)(2,1)} %collective-permute-done.7.far_hbm.refs_1_.refs_2_), custom_call_target="tpu_custom_call" | custom-call | bytes 1966080 | tf_op jit(solution)/shard_map/pallas_call | solution.py:257
  45.2 0.2 collective-permute-done.8.far_ref
  45.4 0.5 shard_map.85
  45.9 2.0 %shard_map.88 = (bf16[256,640]{1,0:T(8,128)(2,1)S(1)}, bf16[256,640]{1,0:T(8,128)(2,1)S(1)}) custom-call(bf16[256,384]{1,0:T(8,128)(2,1)S(1)} %get-tuple-element.17.near_ref.after_ref, bf16[256,384]{1,0:T(8,128)(2,1)S(1)} %collective-permute-done.8.far_ref, bf16[1,768,640]{2,1,0:T(8,128)(2,1)S(1)} %shard_map.87.refs_0_, bf16[384,5120]{1,0:T(8,128)(2,1)} %refs_1_.1, ...), custom_call_target="tpu_custom_call" | custom-call | flops 503316480 | bytes 1966080 | tf_op jit(solution)/shard_map/pallas_call | solution.py:306
  47.9 1.2 %collective-permute-start.10 = (bf16[256,640]{1,0:T(8,128)(2,1)S(1)}, bf16[256,640]{1,0:T(8,128)(2,1)S(1)}, u32[]{:S(2)}, u32[]{:S(2)}) collective-permute-start(bf16[256,640]{1,0:T(8,128)(2,1)S(1)} %get-tuple-element.21), channel_id=1, source_target_pairs={{0,2},{1,3},{2,4},{3,5},{4,6},{5,7},{6,0},{7,1},{8,10},{9,11},{10,... | collective-permute-start | bytes 983048 | tf_op jit(solution)/shard_map/ppermute | solution.py:389
  49.1 2.3 %collective-permute-start.11 = (bf16[256,640]{1,0:T(8,128)(2,1)S(1)}, bf16[256,640]{1,0:T(8,128)(2,1)S(1)}, u32[]{:S(2)}, u32[]{:S(2)}) collective-permute-start(bf16[256,640]{1,0:T(8,128)(2,1)S(1)} %get-tuple-element.22), channel_id=1, source_target_pairs={{0,6},{1,7},{2,0},{3,1},{4,2},{5,3},{6,4},{7,5},{8,14},{9,15},{10,... | collective-permute-start | bytes 983048 | tf_op jit(solution)/shard_map/ppermute | solution.py:390
  51.4 0.2 collective-permute-start.9
  51.6 0.1 add_select_fusion.1
  51.7 0.1 select_n.32
  51.7 0.1 fusion.1.pick_ref
  51.9 1.7 %shard_map.86.mine_ref = f32[256,640]{1,0:T(8,128)S(1)} custom-call(bf16[256,384]{1,0:T(8,128)(2,1)S(1)} %get-tuple-element.17.near_ref.after_ref, bf16[256,384]{1,0:T(8,128)(2,1)S(1)} %collective-permute-done.8.far_ref, bf16[384,5120]{1,0:T(8,128)(2,1)} %refs_1_.1, bf16[384,5120]{1,0:T(8,128)(2,1)} %collective-permute-done.7.far_hbm.refs_1_.refs_2_), custom_call_target="tpu_custom_call" | custom-call | flops 251658240 | bytes 983040 | tf_op jit(solution)/shard_map/pallas_call | solution.py:306
  53.6 6.3 %collective-permute-done.10.refs_1_ = bf16[256,640]{1,0:T(8,128)(2,1)S(1)} collective-permute-done((bf16[256,640]{1,0:T(8,128)(2,1)S(1)}, bf16[256,640]{1,0:T(8,128)(2,1)S(1)}, u32[]{:S(2)}, u32[]{:S(2)}) %collective-permute-start.10) | collective-permute-done | bytes 327712 | tf_op jit(solution)/shard_map/ppermute | solution.py:389
  59.9 5.7 %collective-permute-done.11.refs_2_ = bf16[256,640]{1,0:T(8,128)(2,1)S(1)} collective-permute-done((bf16[256,640]{1,0:T(8,128)(2,1)S(1)}, bf16[256,640]{1,0:T(8,128)(2,1)S(1)}, u32[]{:S(2)}, u32[]{:S(2)}) %collective-permute-start.11) | collective-permute-done | bytes 327712 | tf_op jit(solution)/shard_map/ppermute | solution.py:390
  65.6 0.7 collective-permute-done.9.refs_0_
  66.3 0.4 shard_map.89
  66.8 26.0 %all_to_all.15 = bf16[32,16,640]{2,1,0:T(8,128)(2,1)S(1)} all-to-all(bf16[32,16,640]{2,1,0:T(8,128)(2,1)S(1)} %shard_map.89), channel_id=1, replica_groups=mesh['seq'=32,'tp'=8] {'seq'}, dimensions={0} | all-to-all | bytes 1310720 | tf_op jit(solution)/shard_map/all_to_all | solution.py:393
  92.8 0.8 copy.10
  (6 shorter events, 0.0 us)
Async XLA Ops:
  0.0 19.2 %copy-start = (s32[512,1]{0,1:T(1,128)S(1)}, s32[512,1]{0,1:T(1,128)}, u32[]{:S(2)}) copy-start(s32[512,1]{0,1:T(1,128)} %param.10) | copy-start | bytes 6148
  0.0 41.8 %collective-permute-start.7 = (bf16[384,5120]{1,0:T(8,128)(2,1)}, bf16[384,5120]{1,0:T(8,128)(2,1)}, u32[]{:S(2)}, u32[]{:S(2)}) collective-permute-start(bf16[384,5120]{1,0:T(8,128)(2,1)} %refs_1_.1), channel_id=1, source_target_pairs={{0,1},{1,0},{2,3},{3,2},{4,5},{5,4},{6,7},{7,6},{8,9},{9,8},{10,11... | collective-permute-start | bytes 11796488 | tf_op jit(solution)/shard_map/ppermute | solution.py:360
  0.0 19.8 %collective-permute-start.1 = (bf16[256,640]{1,0:T(8,128)(2,1)}, bf16[256,640]{1,0:T(8,128)(2,1)S(1)}, u32[]{:S(2)}, u32[]{:S(2)}) collective-permute-start(bf16[256,640]{1,0:T(8,128)(2,1)} %bitcast.8), channel_id=1, source_target_pairs={{0,2},{1,3},{2,4},{3,5},{4,6},{5,7},{6,0},{7,1},{8,10},{9,11},{10,... | collective-permute-start | bytes 983048 | tf_op jit(solution)/shard_map/ppermute | solution.py:361
  1.7 18.3 %collective-permute-start.3 = (bf16[256,640]{1,0:T(8,128)(2,1)}, bf16[256,640]{1,0:T(8,128)(2,1)S(1)}, u32[]{:S(2)}, u32[]{:S(2)}) collective-permute-start(bf16[256,640]{1,0:T(8,128)(2,1)} %bitcast.9), channel_id=1, source_target_pairs={{0,6},{1,7},{2,0},{3,1},{4,2},{5,3},{6,4},{7,5},{8,14},{9,15},{10,... | collective-permute-start | bytes 983048 | tf_op jit(solution)/shard_map/ppermute | solution.py:362
  3.3 17.1 %collective-permute-start.5 = (bf16[256,640]{1,0:T(8,128)(2,1)}, bf16[256,640]{1,0:T(8,128)(2,1)S(1)}, u32[]{:S(2)}, u32[]{:S(2)}) collective-permute-start(bf16[256,640]{1,0:T(8,128)(2,1)} %bitcast.10), channel_id=1, source_target_pairs={{0,4},{1,5},{2,6},{3,7},{4,0},{5,1},{6,2},{7,3},{8,12},{9,13},{10,... | collective-permute-start | bytes 983048 | tf_op jit(solution)/shard_map/ppermute | solution.py:363
  5.3 27.5 %collective-permute-start = (bf16[256,640]{1,0:T(8,128)(2,1)}, bf16[256,640]{1,0:T(8,128)(2,1)S(1)}, u32[]{:S(2)}, u32[]{:S(2)}) collective-permute-start(bf16[256,640]{1,0:T(8,128)(2,1)} %bitcast.11), channel_id=1, source_target_pairs={{0,1},{1,0},{2,3},{3,2},{4,5},{5,4},{6,7},{7,6},{8,9},{9,8},{10,11... | collective-permute-start | bytes 983048 | tf_op jit(solution)/shard_map/ppermute | solution.py:360
  5.3 20.8 %all-to-all-start = ((bf16[32,16,128]{2,1,0:T(8,128)(2,1)}), bf16[32,16,128]{2,1,0:T(8,128)(2,1)S(1)}, u32[]{:S(2)}, u32[]{:S(2)}) async-start(bf16[32,16,128]{2,1,0:T(8,128)(2,1)} %bitcast.13), calls=%async_computation | async-start | bytes 262144 | tf_op jit(solution)/shard_map/all_to_all | solution.py:357
  19.8 13.0 %collective-permute-start.2 = (bf16[256,640]{1,0:T(8,128)(2,1)S(1)}, bf16[256,640]{1,0:T(8,128)(2,1)S(1)}, u32[]{:S(2)}, u32[]{:S(2)}) collective-permute-start(bf16[256,640]{1,0:T(8,128)(2,1)S(1)} %collective-permute-done.1.refs_1_), channel_id=1, source_target_pairs={{0,1},{1,0},{2,3},{3,2},{4,5},{5,4},{6,7},{7,6},{8,9},{9,8},{10,11... | collective-permute-start | bytes 983048 | tf_op jit(solution)/shard_map/ppermute | solution.py:360
  19.9 12.9 %collective-permute-start.4 = (bf16[256,640]{1,0:T(8,128)(2,1)S(1)}, bf16[256,640]{1,0:T(8,128)(2,1)S(1)}, u32[]{:S(2)}, u32[]{:S(2)}) collective-permute-start(bf16[256,640]{1,0:T(8,128)(2,1)S(1)} %collective-permute-done.3.refs_3_), channel_id=1, source_target_pairs={{0,1},{1,0},{2,3},{3,2},{4,5},{5,4},{6,7},{7,6},{8,9},{9,8},{10,11... | collective-permute-start | bytes 983048 | tf_op jit(solution)/shard_map/ppermute | solution.py:360
  20.4 12.4 %collective-permute-start.6 = (bf16[256,640]{1,0:T(8,128)(2,1)S(1)}, bf16[256,640]{1,0:T(8,128)(2,1)S(1)}, u32[]{:S(2)}, u32[]{:S(2)}) collective-permute-start(bf16[256,640]{1,0:T(8,128)(2,1)S(1)} %collective-permute-done.5.refs_5_), channel_id=1, source_target_pairs={{0,1},{1,0},{2,3},{3,2},{4,5},{5,4},{6,7},{7,6},{8,9},{9,8},{10,11... | collective-permute-start | bytes 983048 | tf_op jit(solution)/shard_map/ppermute | solution.py:360
  27.1 14.8 %all-to-all-start.1 = ((bf16[32,16,128]{2,1,0:T(8,128)(2,1)}), bf16[32,16,128]{2,1,0:T(8,128)(2,1)S(1)}, u32[]{:S(2)}, u32[]{:S(2)}) async-start(bf16[32,16,128]{2,1,0:T(8,128)(2,1)} %shard_map.83), calls=%async_computation.1 | async-start | bytes 262144 | tf_op jit(solution)/shard_map/all_to_all | solution.py:364
  43.8 1.5 %collective-permute-start.8 = (bf16[256,384]{1,0:T(8,128)(2,1)S(1)}, bf16[256,384]{1,0:T(8,128)(2,1)S(1)}, u32[]{:S(2)}, u32[]{:S(2)}) collective-permute-start(bf16[256,384]{1,0:T(8,128)(2,1)S(1)} %get-tuple-element.17.near_ref.after_ref), channel_id=1, source_target_pairs={{0,1},{1,0},{2,3},{3,2},{4,5},{5,4},{6,7},{7,6},{8,9},{9,8},{10,11... | collective-permute-start | bytes 589832 | tf_op jit(solution)/shard_map/ppermute | solution.py:360
  47.9 12.0 %collective-permute-start.10 = (bf16[256,640]{1,0:T(8,128)(2,1)S(1)}, bf16[256,640]{1,0:T(8,128)(2,1)S(1)}, u32[]{:S(2)}, u32[]{:S(2)}) collective-permute-start(bf16[256,640]{1,0:T(8,128)(2,1)S(1)} %get-tuple-element.21), channel_id=1, source_target_pairs={{0,2},{1,3},{2,4},{3,5},{4,6},{5,7},{6,0},{7,1},{8,10},{9,11},{10,... | collective-permute-start | bytes 983048 | tf_op jit(solution)/shard_map/ppermute | solution.py:389
  49.1 16.5 %collective-permute-start.11 = (bf16[256,640]{1,0:T(8,128)(2,1)S(1)}, bf16[256,640]{1,0:T(8,128)(2,1)S(1)}, u32[]{:S(2)}, u32[]{:S(2)}) collective-permute-start(bf16[256,640]{1,0:T(8,128)(2,1)S(1)} %get-tuple-element.22), channel_id=1, source_target_pairs={{0,6},{1,7},{2,0},{3,1},{4,2},{5,3},{6,4},{7,5},{8,14},{9,15},{10,... | collective-permute-start | bytes 983048 | tf_op jit(solution)/shard_map/ppermute | solution.py:390
  51.4 14.9 %collective-permute-start.9 = (bf16[256,640]{1,0:T(8,128)(2,1)S(1)}, bf16[256,640]{1,0:T(8,128)(2,1)S(1)}, u32[]{:S(2)}, u32[]{:S(2)}) collective-permute-start(bf16[256,640]{1,0:T(8,128)(2,1)S(1)} %shard_map.85), channel_id=1, source_target_pairs={{0,4},{1,5},{2,6},{3,7},{4,0},{5,1},{6,2},{7,3},{8,12},{9,13},{10,... | collective-permute-start | bytes 983048 | tf_op jit(solution)/shard_map/ppermute | solution.py:388

commit v3 on v2

--- a/solution.py
+++ b/solution.py
@@ -103,6 +103,15 @@
         )
         total = part if total is None else total + part
     return total
+
+
+def out_weight_copies(i, shift, near_hbm, far_hbm, wo_ref, sems):
+    depth = near_hbm.shape[0]
+    at = columns_at(place_in_column((shift,), False)[0], wo_ref.shape[2])
+    return (
+        pltpu.make_async_copy(near_hbm.at[:, at], wo_ref.at[i, 0:depth, :], sems.at[0, i]),
+        pltpu.make_async_copy(far_hbm.at[:, at], wo_ref.at[i, depth : 2 * depth, :], sems.at[1, i]),
+    )
 
 
 def project_kernel(x_hbm, *refs):
@@ -163,35 +172,17 @@
             bytes_accessed=16 * width * columns,
             transcendentals=0,
         ),
-    )(in_hbm(x), *shards, in_hbm(w_query), in_hbm(w_keyval), cosine, sine)
-
-
-def out_weight_copies(i, shift, near_hbm, far_hbm, wo_ref, sems):
-    depth = near_hbm.shape[0]
-    at = columns_at(place_in_column((shift,), False)[0], wo_ref.shape[2])
-    return (
-        pltpu.make_async_copy(near_hbm.at[:, at], wo_ref.at[i, 0:depth, :], sems.at[0, i]),
-        pltpu.make_async_copy(far_hbm.at[:, at], wo_ref.at[i, depth : 2 * depth, :], sems.at[1, i]),
-    )
-
-
-def attend_kernel(
-    tokens,
-    shift,
-    q_ref,
-    k_ref,
-    v_ref,
-    cache_ref,
-    valid_ref,
-    near_hbm,
-    far_hbm,
-    attn_ref,
-    wo_ref,
-    sems,
-):
-    copies = out_weight_copies(0, shift, near_hbm, far_hbm, wo_ref, sems)
-    for copy in copies:
-        copy.start()
+    )(
+        in_hbm(x),
+        *shards,
+        in_hbm(w_query),
+        in_hbm(w_keyval),
+        cosine,
+        sine,
+    )
+
+
+def attend_kernel(tokens, q_ref, k_ref, v_ref, cache_ref, valid_ref, attn_ref):
     heads, rows, _ = q_ref.shape
     scale = 1.0 / math.sqrt(HD)
     half = cache_ref.shape[0] // 2
@@ -218,29 +209,22 @@
         )
         mixed = jnp.dot(weights, values, preferred_element_type=jnp.float32)
         attn_ref[:, h * HD : (h + 1) * HD] = jnp.where(valid, mixed, 0.0).astype(jnp.bfloat16)
-    for copy in copies:
-        copy.wait()
-
-
-def attend(shift, queries, keys, values, cache, valid, out_near, out_far, tokens):
+
+
+def attend(queries, keys, values, cache, valid, tokens):
     heads, rows, _ = queries.shape
-    depth, width = out_near.shape[0], out_near.shape[1] // (CHIPS * CORES)
-    return pl.pallas_call(
-        functools.partial(attend_kernel, tokens, shift),
-        in_specs=[VMEM] * 5 + [ANY] * 2,
-        out_specs=[VMEM] * 2,
-        out_shape=[
-            jax.ShapeDtypeStruct((rows, heads * HD), jnp.bfloat16),
-            jax.ShapeDtypeStruct((1, 2 * depth, width), jnp.bfloat16),
-        ],
-        scratch_shapes=[pltpu.SemaphoreType.DMA((2, 1))],
+    return pl.pallas_call(
+        functools.partial(attend_kernel, tokens),
+        in_specs=[VMEM] * 5,
+        out_specs=VMEM,
+        out_shape=jax.ShapeDtypeStruct((rows, heads * HD), jnp.bfloat16),
         compiler_params=params(8),
         cost_estimate=pl.CostEstimate(
             flops=8 * heads * rows * PL * HD,
-            bytes_accessed=4 * rows * heads * HD + 4 * depth * width,
+            bytes_accessed=4 * rows * heads * HD,
             transcendentals=2 * heads * rows * PL,
         ),
-    )(queries, keys, values, cache, valid, in_hbm(out_near), in_hbm(out_far))
+    )(queries, keys, values, cache, valid)
 
 
 def fetch_kernel(shift, after_ref, near_hbm, far_hbm, wo_ref, sems):
@@ -267,59 +251,91 @@
     )(after, in_hbm(out_near), in_hbm(out_far))
 
 
-def output_kernel(ready, shifts, near_ref, far_ref, *refs):
-    ready_refs = refs[:ready]
-    refs = refs[ready:]
-    copies = []
-    if shifts:
-        near_hbm, far_hbm = refs[:2]
-        wo_ref, sems = refs[-2:]
-        refs = refs[2:-2]
-        copies = [
-            out_weight_copies(i, shift, near_hbm, far_hbm, wo_ref, sems)
-            for i, shift in enumerate(shifts)
-        ]
+def output_cost(count, rows, depth, width):
+    return pl.CostEstimate(
+        flops=2 * count * rows * depth * width,
+        bytes_accessed=2 * count * depth * width,
+        transcendentals=0,
+    )
+
+
+def output_halves_kernel(near_ref, far_ref, wo_ref, top_ref, bottom_ref):
+    half = top_ref.shape[0]
+    both = jnp.concatenate([near_ref[...], far_ref[...]], -1)
+    block = jnp.dot(both, wo_ref[0], preferred_element_type=jnp.float32).astype(jnp.bfloat16)
+    top_ref[...] = block[:half]
+    bottom_ref[...] = block[half:]
+
+
+def output_halves(near, far, weights):
+    rows = near.shape[0]
+    _, depth, width = weights.shape
+    return pl.pallas_call(
+        output_halves_kernel,
+        in_specs=[VMEM] * 3,
+        out_specs=[VMEM] * 2,
+        out_shape=[jax.ShapeDtypeStruct((rows // 2, width), jnp.bfloat16)] * 2,
+        compiler_params=params(8),
+        cost_estimate=output_cost(1, rows, depth, width),
+    )(near, far, weights)
+
+
+def output_kernel(shifts, near_ref, far_ref, near_hbm, far_hbm, *refs):
+    outs, (wo_ref, sems) = refs[:-2], refs[-2:]
+    copies = [
+        out_weight_copies(i, shift, near_hbm, far_hbm, wo_ref, sems)
+        for i, shift in enumerate(shifts)
+    ]
     for pair in copies:
         for copy in pair:
             copy.start()
     both = jnp.concatenate([near_ref[...], far_ref[...]], -1)
-    for i, out_ref in enumerate(refs):
-        if i < ready:
-            weights = ready_refs[i][0]
-        else:
-            for copy in copies[i - ready]:
-                copy.wait()
-            weights = wo_ref[i - ready]
-        block = jnp.dot(both, weights, preferred_element_type=jnp.float32)
-        out_ref[...] = block.astype(out_ref.dtype)
-
-
-def output(near, far, ready, shifts, out_near, out_far, dtype):
+    for i, out_ref in enumerate(outs):
+        for copy in copies[i]:
+            copy.wait()
+        out_ref[...] = jnp.dot(both, wo_ref[i], preferred_element_type=jnp.float32)
+
+
+def output(near, far, shifts, out_near, out_far):
     rows = near.shape[0]
     depth, width = out_near.shape[0], out_near.shape[1] // (CHIPS * CORES)
-    count = len(ready) + len(shifts)
-    hbm = [in_hbm(out_near), in_hbm(out_far)] if shifts else []
-    scratch = [
-        pltpu.VMEM((len(shifts), 2 * depth, width), jnp.bfloat16),
-        pltpu.SemaphoreType.DMA((2, len(shifts))),
-    ]
-    return pl.pallas_call(
-        functools.partial(output_kernel, len(ready), shifts),
-        in_specs=[VMEM] * (2 + len(ready)) + [ANY] * len(hbm),
-        out_specs=[VMEM] * count,
-        out_shape=[jax.ShapeDtypeStruct((rows, width), dtype)] * count,
-        scratch_shapes=scratch if shifts else [],
-        compiler_params=params(8),
-        cost_estimate=pl.CostEstimate(
-            flops=4 * count * rows * depth * width,
-            bytes_accessed=4 * count * depth * width,
-            transcendentals=0,
-        ),
-    )(near, far, *ready, *hbm)
+    return pl.pallas_call(
+        functools.partial(output_kernel, shifts),
+        in_specs=[VMEM] * 2 + [ANY] * 2,
+        out_specs=[VMEM] * len(shifts),
+        out_shape=[jax.ShapeDtypeStruct((rows, width), jnp.float32)] * len(shifts),
+        scratch_shapes=[
+            pltpu.VMEM((len(shifts), 2 * depth, width), jnp.bfloat16),
+            pltpu.SemaphoreType.DMA((2, len(shifts))),
+        ],
+        compiler_params=params(8),
+        cost_estimate=output_cost(len(shifts), rows, 2 * depth, width),
+    )(near, far, in_hbm(out_near), in_hbm(out_far))
+
+
+def pass_on_kernel(above_ref, below_ref, top_ref, bottom_ref, to_above_ref, to_below_ref):
+    half = top_ref.shape[0]
+    top = above_ref[:half] + top_ref[...].astype(jnp.float32)
+    to_above_ref[:half] = top.astype(jnp.bfloat16)
+    to_above_ref[half:] = above_ref[half:].astype(jnp.bfloat16)
+    bottom = below_ref[half:] + bottom_ref[...].astype(jnp.float32)
+    to_below_ref[:half] = below_ref[:half].astype(jnp.bfloat16)
+    to_below_ref[half:] = bottom.astype(jnp.bfloat16)
+
+
+def pass_on(above, below, top, bottom):
+    block = jax.ShapeDtypeStruct(above.shape, jnp.bfloat16)
+    return pl.pallas_call(
+        pass_on_kernel,
+        in_specs=[VMEM] * 4,
+        out_specs=[VMEM] * 2,
+        out_shape=[block, block],
+        compiler_params=params(8),
+    )(above, below, top, bottom)
 
 
 def place_kernel(pick_ref, mine_ref, *refs):
-    parts, out_ref = refs[:3], refs[3]
+    parts, out_ref = refs[:-1], refs[-1]
     total = mine_ref[...]
     for part in parts:
         total = total + part[...].astype(jnp.float32)
@@ -333,7 +349,7 @@
     _, width = mine.shape
     return pl.pallas_call(
         place_kernel,
-        in_specs=[VMEM] * 5,
+        in_specs=[VMEM] * (2 + len(parts)),
         out_specs=VMEM,
         out_shape=jax.ShapeDtypeStruct((slots, tokens, width), jnp.bfloat16),
         compiler_params=params(8),
@@ -375,17 +391,16 @@
     slot_picks = block_picks(pick, tokens, group_size)
 
     queries, keys, values = project(x, shards, w_query, w_keyval, cosine, sine)
-    attn, w_across = attend(2, queries, keys, values, cache, valid, w_out, out_far, tokens)
+    attn = attend(queries, keys, values, cache, valid, tokens)
     attn_far = swap(attn)
-    w_above = fetch(1, attn, w_out, out_far)
-    (to_across,) = output(attn, attn_far, [w_across], (), w_out, out_far, jnp.bfloat16)
-    to_across, attn_far = lax.optimization_barrier((to_across, attn_far))
-    to_above, to_below = output(
-        attn, attn_far, [w_above], (-1,), w_out, out_far, jnp.bfloat16
-    )
-    (mine,) = output(attn, attn_far, [], (0,), w_out, out_far, jnp.float32)
+    w_across = fetch(2, attn, w_out, out_far)
+    top, bottom = output_halves(attn, attn_far, w_across)
+    top = lax.ppermute(top, "tp", chip_shift(1))
+    bottom = lax.ppermute(bottom, "tp", chip_shift(-1))
+    for_above, for_below = output(attn, attn_far, (1, -1), w_out, out_far)
+    to_above, to_below = pass_on(for_above, for_below, top, bottom)
+    (mine,) = output(attn, attn_far, (0,), w_out, out_far)
     parts = [
-        lax.ppermute(to_across, "tp", chip_shift(2)),
         lax.ppermute(to_above, "tp", chip_shift(1)),
         lax.ppermute(to_below, "tp", chip_shift(-1)),
     ]

time: 94 us -> 91.2 us (0.970)
  waiting for transfers between devices: 21.5 us -> 18.6 us
  starting transfers between devices: 27 us -> 28.7 us
  blocking collectives: 26 us -> 24.9 us
    ppermute x1, waiting for transfers between devices: 5.73 us -> 0.01 us  [per_device(): lax.ppermute(to_below, 'tp', chip_shift(-1))]
    ppermute x1 -> x2, waiting for transfers between devices: 0.74 us -> 4.95 us  [the longest x1 2.83 us: per_device(): top = lax.ppermute(top, 'tp', chip_shift(1))]
    ppermute x1 -> x2, starting transfers between devices: 0.18 us -> 2.1 us  [the longest x1 1.98 us: per_device(): bottom = lax.ppermute(bottom, 'tp', chip_shift(-1))]
    ppermute x1, waiting for transfers between devices: 6.27 us -> 4.76 us  [per_device(): lax.ppermute(to_above, 'tp', chip_shift(1))]
    all_to_all x1, blocking collectives: 26 us -> 24.9 us  [per_device(): return lax.all_to_all(slots, 'seq', 0, 0, tiled=True)]
    ppermute x1, starting transfers between devices: 1.17 us -> 0.08 us  [per_device(): lax.ppermute(to_above, 'tp', chip_shift(1))]
    pallas_call x5 -> x6, Pallas kernels: 6.56 us -> 5.83 us  [the longest x2 3.96 us: output(): pl.pallas_call(functools.partial(output_kernel, shifts), in_specs=[VMEM]...]
  transfers between devices with their start and end apart: 14 -> 15, of which waited for: 6 -> 6; matrix products, arithmetic and copies ran while one was open for 3% -> 4% of each run, Pallas kernels for 11% -> 14%
where the time goes in v3:
time: 91.2 us; the launch traced here: 90.6 us
  starting transfers between devices  28.7 us (31%)
  blocking collectives  24.9 us (27%)
  waiting for transfers between devices  18.6 us (20%)
  Pallas kernels  14 us (15%)
  other arithmetic  2.16 us (2%)
  local copies, waits for them, and re-layouts  2.02 us (2%)
    all_to_all x1, blocking collectives, per_device(): return lax.all_to_all(slots, 'seq', 0, 0, tiled=True)  24.9 us
    all_to_all x1, starting transfers between devices, per_device(): pieces = lax.all_to_all(pieces, 'seq', 0, 0, tiled=True)  11.6 us
    pallas_call x1, Pallas kernels, project(): pl.pallas_call(project_kernel, in_specs=[ANY] + [VMEM] * 7 + [ANY] * 2 +...  5.96 us
    all_to_all x1, starting transfers between devices, per_device(): cache = lax.all_to_all(route(prompt_picks, pieces), 'seq', 0, 0, tiled=True)  5.64 us
    all_to_all x1, waiting for transfers between devices, per_device(): pieces = lax.all_to_all(pieces, 'seq', 0, 0, tiled=True)  5.62 us
    ppermute x1, waiting for transfers between devices, per_device(): lax.ppermute(to_above, 'tp', chip_shift(1))  4.76 us
    pallas_call x2, Pallas kernels, output(): pl.pallas_call(functools.partial(output_kernel, shifts), in_specs=[VMEM]...  3.96 us
    ppermute x1, starting transfers between devices, per_device(): lax.ppermute(to_below, 'tp', chip_shift(-1))  3.22 us
  transfers between devices with their start and end apart: 15, of which 6 were waited for; matrix products, arithmetic and copies ran while one was open for 4% of the time, Pallas kernels for 14%

profile of v3, /device:TPU:2, one launch (start us, length us, event | category | flops | bytes accessed | tf_op | source)
XLA Modules:
  0.0 90.6 jit_solution(18252582798364192304)
XLA Ops:
  0.0 0.0 copy-start
  0.0 0.0 collective-permute-start.8
  0.0 1.7 %collective-permute-start.1 = (bf16[256,640]{1,0:T(8,128)(2,1)}, bf16[256,640]{1,0:T(8,128)(2,1)S(1)}, u32[]{:S(2)}, u32[]{:S(2)}) collective-permute-start(bf16[256,640]{1,0:T(8,128)(2,1)} %bitcast.8), channel_id=1, source_target_pairs={{0,2},{1,3},{2,4},{3,5},{4,6},{5,7},{6,0},{7,1},{8,10},{9,11},{10,... | collective-permute-start | bytes 983048 | tf_op jit(solution)/shard_map/ppermute | solution.py:377
  1.7 1.7 %collective-permute-start.3 = (bf16[256,640]{1,0:T(8,128)(2,1)}, bf16[256,640]{1,0:T(8,128)(2,1)S(1)}, u32[]{:S(2)}, u32[]{:S(2)}) collective-permute-start(bf16[256,640]{1,0:T(8,128)(2,1)} %bitcast.9), channel_id=1, source_target_pairs={{0,6},{1,7},{2,0},{3,1},{4,2},{5,3},{6,4},{7,5},{8,14},{9,15},{10,... | collective-permute-start | bytes 983048 | tf_op jit(solution)/shard_map/ppermute | solution.py:378
  3.3 2.0 %collective-permute-start.5 = (bf16[256,640]{1,0:T(8,128)(2,1)}, bf16[256,640]{1,0:T(8,128)(2,1)S(1)}, u32[]{:S(2)}, u32[]{:S(2)}) collective-permute-start(bf16[256,640]{1,0:T(8,128)(2,1)} %bitcast.10), channel_id=1, source_target_pairs={{0,4},{1,5},{2,6},{3,7},{4,0},{5,1},{6,2},{7,3},{8,12},{9,13},{10,... | collective-permute-start | bytes 983048 | tf_op jit(solution)/shard_map/ppermute | solution.py:379
  5.3 0.0 collective-permute-start
  5.3 11.6 %all-to-all-start = ((bf16[32,16,128]{2,1,0:T(8,128)(2,1)}), bf16[32,16,128]{2,1,0:T(8,128)(2,1)S(1)}, u32[]{:S(2)}, u32[]{:S(2)}) async-start(bf16[32,16,128]{2,1,0:T(8,128)(2,1)} %bitcast.13), calls=%async_computation | async-start | bytes 262144 | tf_op jit(solution)/shard_map/all_to_all | solution.py:373
  16.9 0.8 dynamic_slice.7
  17.7 0.1 fusion.3
  17.8 0.1 pad_maximum_fusion
  17.9 0.7 broadcast_compare_fusion
  18.6 0.7 broadcast_multiply_fusion
  19.2 0.1 add_select_fusion
  19.3 0.1 fusion.2
  19.4 0.0 copy-done
  19.4 0.1 dynamic-slice_bitcast_fusion
  19.5 0.1 reshape.108
  19.5 0.1 select_n.34
  19.6 0.0 collective-permute-done.1.refs_1_
  19.6 0.1 collective-permute-start.2
  19.7 0.0 collective-permute-done.3.refs_3_
  19.7 0.5 collective-permute-start.4
  20.2 0.0 collective-permute-done.5.refs_5_
  20.2 0.1 collective-permute-start.6
  20.3 0.1 fusion.pick_ref
  20.5 5.6 %all-to-all-done.piece_ref = bf16[32,16,128]{2,1,0:T(8,128)(2,1)S(1)} async-done(((bf16[32,16,128]{2,1,0:T(8,128)(2,1)}), bf16[32,16,128]{2,1,0:T(8,128)(2,1)S(1)}, u32[]{:S(2)}, u32[]{:S(2)}) %all-to-all-start) | async-done | bytes 131104 | tf_op jit(solution)/shard_map/all_to_all | solution.py:373
  26.1 0.9 %shard_map.83 = bf16[32,16,128]{2,1,0:T(8,128)(2,1)} custom-call(bf16[512,512]{1,0:T(8,128)(2,1)S(1)} %fusion.pick_ref, bf16[32,16,128]{2,1,0:T(8,128)(2,1)S(1)} %all-to-all-done.piece_ref), custom_call_target="tpu_custom_call" | custom-call | tf_op jit(solution)/shard_map/pallas_call | solution.py:69
  27.1 5.6 %all-to-all-start.1 = ((bf16[32,16,128]{2,1,0:T(8,128)(2,1)}), bf16[32,16,128]{2,1,0:T(8,128)(2,1)S(1)}, u32[]{:S(2)}, u32[]{:S(2)}) async-start(bf16[32,16,128]{2,1,0:T(8,128)(2,1)} %shard_map.83), calls=%async_computation.1 | async-start | bytes 262144 | tf_op jit(solution)/shard_map/all_to_all | solution.py:380
  32.7 0.1 select_reduce_fusion
  32.8 0.0 collective-permute-done.refs_0_
  32.8 0.0 collective-permute-done.2.refs_2_
  32.8 0.0 collective-permute-done.4.refs_4_
  32.9 0.0 collective-permute-done.6.refs_6_
  32.9 6.0 %shard_map.82 = (bf16[3,256,128]{2,1,0:T(8,128)(2,1)S(1)}, bf16[256,128]{1,0:T(8,128)(2,1)S(1)}, bf16[256,128]{1,0:T(8,128)(2,1)S(1)}) custom-call(bf16[256,640]{1,0:T(8,128)(2,1)} %bitcast.12, bf16[256,640]{1,0:T(8,128)(2,1)S(1)} %collective-permute-done.refs_0_, bf16[256,640]{1,0:T(8,128)(2,1)S(1)} %collective-permute-done.1.refs_1_, ...), custom_call_target="tpu_custom_call" | custom-call | flops 1677721600 | bytes 6553600 | tf_op jit(solution)/shard_map/pallas_call | solution.py:154
  38.9 3.0 %all-to-all-done.1.cache_ref = bf16[32,16,128]{2,1,0:T(8,128)(2,1)S(1)} async-done(((bf16[32,16,128]{2,1,0:T(8,128)(2,1)}), bf16[32,16,128]{2,1,0:T(8,128)(2,1)S(1)}, u32[]{:S(2)}, u32[]{:S(2)}) %all-to-all-start.1) | async-done | bytes 131104 | tf_op jit(solution)/shard_map/all_to_all | solution.py:380
  41.9 0.1 broadcast_in_dim.58.valid_ref
  42.0 0.9 %shard_map.84.near_ref.after_ref = bf16[256,384]{1,0:T(8,128)(2,1)S(1)} custom-call(bf16[3,256,128]{2,1,0:T(8,128)(2,1)S(1)} %get-tuple-element.14.q_ref, bf16[256,128]{1,0:T(8,128)(2,1)S(1)} %get-tuple-element.15.k_ref, bf16[256,128]{1,0:T(8,128)(2,1)S(1)} %get-tuple-element.16.v_ref, bf16[32,16,128]{2,1,0:T(8,128)(2,1)S(1)} %all-to-all-done.1.cache_ref, ...), custom_call_target="tpu_custom_call" | custom-call | flops 201326592 | bytes 393216 | tf_op jit(solution)/shard_map/pallas_call | solution.py:216
  42.9 0.1 collective-permute-start.7
  43.0 0.0 collective-permute-done.8.far_hbm
  43.1 1.2 %shard_map.87.wo_ref = bf16[1,768,640]{2,1,0:T(8,128)(2,1)S(1)} custom-call(bf16[256,384]{1,0:T(8,128)(2,1)S(1)} %shard_map.84.near_ref.after_ref, bf16[384,5120]{1,0:T(8,128)(2,1)} %near_hbm.5, bf16[384,5120]{1,0:T(8,128)(2,1)} %collective-permute-done.8.far_hbm), custom_call_target="tpu_custom_call" | custom-call | bytes 1966080 | tf_op jit(solution)/shard_map/pallas_call | solution.py:241
  44.3 0.2 collective-permute-done.7.far_ref
  44.5 0.5 shard_map.88
  44.9 2.0 %collective-permute-start.10 = (bf16[128,640]{1,0:T(8,128)(2,1)S(1)}, bf16[128,640]{1,0:T(8,128)(2,1)S(1)}, u32[]{:S(2)}, u32[]{:S(2)}) collective-permute-start(bf16[128,640]{1,0:T(8,128)(2,1)S(1)} %get-tuple-element.20), channel_id=1, source_target_pairs={{0,6},{1,7},{2,0},{3,1},{4,2},{5,3},{6,4},{7,5},{8,14},{9,15},{10,... | collective-permute-start | bytes 491528 | tf_op jit(solution)/shard_map/ppermute | solution.py:399
  46.9 0.1 collective-permute-start.9
  47.1 2.3 %shard_map.86 = (f32[256,640]{1,0:T(8,128)S(1)}, f32[256,640]{1,0:T(8,128)S(1)}) custom-call(bf16[256,384]{1,0:T(8,128)(2,1)S(1)} %shard_map.84.near_ref.after_ref, bf16[256,384]{1,0:T(8,128)(2,1)S(1)} %collective-permute-done.7.far_ref, bf16[384,5120]{1,0:T(8,128)(2,1)} %near_hbm.5, bf16[384,5120]{1,0:T(8,128)(2,1)} %collective-permute-done.8.far_hbm), custom_call_target="tpu_custom_call" | custom-call | flops 503316480 | bytes 1966080 | tf_op jit(solution)/shard_map/pallas_call | solution.py:302
  49.3 2.1 %collective-permute-done.10.bottom_ref = bf16[128,640]{1,0:T(8,128)(2,1)S(1)} collective-permute-done((bf16[128,640]{1,0:T(8,128)(2,1)S(1)}, bf16[128,640]{1,0:T(8,128)(2,1)S(1)}, u32[]{:S(2)}, u32[]{:S(2)}) %collective-permute-start.10) | collective-permute-done | bytes 163872 | tf_op jit(solution)/shard_map/ppermute | solution.py:399
  51.4 2.8 %collective-permute-done.9.top_ref = bf16[128,640]{1,0:T(8,128)(2,1)S(1)} collective-permute-done((bf16[128,640]{1,0:T(8,128)(2,1)S(1)}, bf16[128,640]{1,0:T(8,128)(2,1)S(1)}, u32[]{:S(2)}, u32[]{:S(2)}) %collective-permute-start.9) | collective-permute-done | bytes 163872 | tf_op jit(solution)/shard_map/ppermute | solution.py:398
  54.3 0.1 shard_map.89
  54.4 0.1 collective-permute-start.11
  54.5 3.2 %collective-permute-start.12 = (bf16[256,640]{1,0:T(8,128)(2,1)S(1)}, bf16[256,640]{1,0:T(8,128)(2,1)S(1)}, u32[]{:S(2)}, u32[]{:S(2)}) collective-permute-start(bf16[256,640]{1,0:T(8,128)(2,1)S(1)} %get-tuple-element.22), channel_id=1, source_target_pairs={{0,6},{1,7},{2,0},{3,1},{4,2},{5,3},{6,4},{7,5},{8,14},{9,15},{10,... | collective-permute-start | bytes 983048 | tf_op jit(solution)/shard_map/ppermute | solution.py:405
  57.7 0.1 add_select_fusion.1
  57.8 0.1 select_n.32
  57.8 0.1 fusion.1.pick_ref
  58.0 1.7 %shard_map.85.mine_ref = f32[256,640]{1,0:T(8,128)S(1)} custom-call(bf16[256,384]{1,0:T(8,128)(2,1)S(1)} %shard_map.84.near_ref.after_ref, bf16[256,384]{1,0:T(8,128)(2,1)S(1)} %collective-permute-done.7.far_ref, bf16[384,5120]{1,0:T(8,128)(2,1)} %near_hbm.5, bf16[384,5120]{1,0:T(8,128)(2,1)} %collective-permute-done.8.far_hbm), custom_call_target="tpu_custom_call" | custom-call | flops 251658240 | bytes 983040 | tf_op jit(solution)/shard_map/pallas_call | solution.py:302
  59.7 4.8 %collective-permute-done.11.refs_0_ = bf16[256,640]{1,0:T(8,128)(2,1)S(1)} collective-permute-done((bf16[256,640]{1,0:T(8,128)(2,1)S(1)}, bf16[256,640]{1,0:T(8,128)(2,1)S(1)}, u32[]{:S(2)}, u32[]{:S(2)}) %collective-permute-start.11) | collective-permute-done | bytes 327712 | tf_op jit(solution)/shard_map/ppermute | solution.py:404
  64.5 0.0 collective-permute-done.12.refs_1_
  64.5 0.4 shard_map.90
  64.8 24.9 %all_to_all.15 = bf16[32,16,640]{2,1,0:T(8,128)(2,1)S(1)} all-to-all(bf16[32,16,640]{2,1,0:T(8,128)(2,1)S(1)} %shard_map.90), channel_id=1, replica_groups=mesh['seq'=32,'tp'=8] {'seq'}, dimensions={0} | all-to-all | bytes 1310720 | tf_op jit(solution)/shard_map/all_to_all | solution.py:408
  89.7 0.8 copy.10
  (6 shorter events, 0.0 us)
Async XLA Ops:
  0.0 19.4 %copy-start = (s32[512,1]{0,1:T(1,128)S(1)}, s32[512,1]{0,1:T(1,128)}, u32[]{:S(2)}) copy-start(s32[512,1]{0,1:T(1,128)} %param.10) | copy-start | bytes 6148
  0.0 43.0 %collective-permute-start.8 = (bf16[384,5120]{1,0:T(8,128)(2,1)}, bf16[384,5120]{1,0:T(8,128)(2,1)}, u32[]{:S(2)}, u32[]{:S(2)}) collective-permute-start(bf16[384,5120]{1,0:T(8,128)(2,1)} %near_hbm.5), channel_id=1, source_target_pairs={{0,1},{1,0},{2,3},{3,2},{4,5},{5,4},{6,7},{7,6},{8,9},{9,8},{10,11... | collective-permute-start | bytes 11796488 | tf_op jit(solution)/shard_map/ppermute | solution.py:376
  0.0 19.6 %collective-permute-start.1 = (bf16[256,640]{1,0:T(8,128)(2,1)}, bf16[256,640]{1,0:T(8,128)(2,1)S(1)}, u32[]{:S(2)}, u32[]{:S(2)}) collective-permute-start(bf16[256,640]{1,0:T(8,128)(2,1)} %bitcast.8), channel_id=1, source_target_pairs={{0,2},{1,3},{2,4},{3,5},{4,6},{5,7},{6,0},{7,1},{8,10},{9,11},{10,... | collective-permute-start | bytes 983048 | tf_op jit(solution)/shard_map/ppermute | solution.py:377
  1.7 18.1 %collective-permute-start.3 = (bf16[256,640]{1,0:T(8,128)(2,1)}, bf16[256,640]{1,0:T(8,128)(2,1)S(1)}, u32[]{:S(2)}, u32[]{:S(2)}) collective-permute-start(bf16[256,640]{1,0:T(8,128)(2,1)} %bitcast.9), channel_id=1, source_target_pairs={{0,6},{1,7},{2,0},{3,1},{4,2},{5,3},{6,4},{7,5},{8,14},{9,15},{10,... | collective-permute-start | bytes 983048 | tf_op jit(solution)/shard_map/ppermute | solution.py:378
  3.3 16.9 %collective-permute-start.5 = (bf16[256,640]{1,0:T(8,128)(2,1)}, bf16[256,640]{1,0:T(8,128)(2,1)S(1)}, u32[]{:S(2)}, u32[]{:S(2)}) collective-permute-start(bf16[256,640]{1,0:T(8,128)(2,1)} %bitcast.10), channel_id=1, source_target_pairs={{0,4},{1,5},{2,6},{3,7},{4,0},{5,1},{6,2},{7,3},{8,12},{9,13},{10,... | collective-permute-start | bytes 983048 | tf_op jit(solution)/shard_map/ppermute | solution.py:379
  5.3 27.5 %collective-permute-start = (bf16[256,640]{1,0:T(8,128)(2,1)}, bf16[256,640]{1,0:T(8,128)(2,1)S(1)}, u32[]{:S(2)}, u32[]{:S(2)}) collective-permute-start(bf16[256,640]{1,0:T(8,128)(2,1)} %bitcast.11), channel_id=1, source_target_pairs={{0,1},{1,0},{2,3},{3,2},{4,5},{5,4},{6,7},{7,6},{8,9},{9,8},{10,11... | collective-permute-start | bytes 983048 | tf_op jit(solution)/shard_map/ppermute | solution.py:376
  5.3 20.8 %all-to-all-start = ((bf16[32,16,128]{2,1,0:T(8,128)(2,1)}), bf16[32,16,128]{2,1,0:T(8,128)(2,1)S(1)}, u32[]{:S(2)}, u32[]{:S(2)}) async-start(bf16[32,16,128]{2,1,0:T(8,128)(2,1)} %bitcast.13), calls=%async_computation | async-start | bytes 262144 | tf_op jit(solution)/shard_map/all_to_all | solution.py:373
  19.6 13.2 %collective-permute-start.2 = (bf16[256,640]{1,0:T(8,128)(2,1)S(1)}, bf16[256,640]{1,0:T(8,128)(2,1)S(1)}, u32[]{:S(2)}, u32[]{:S(2)}) collective-permute-start(bf16[256,640]{1,0:T(8,128)(2,1)S(1)} %collective-permute-done.1.refs_1_), channel_id=1, source_target_pairs={{0,1},{1,0},{2,3},{3,2},{4,5},{5,4},{6,7},{7,6},{8,9},{9,8},{10,11... | collective-permute-start | bytes 983048 | tf_op jit(solution)/shard_map/ppermute | solution.py:376
  19.7 13.1 %collective-permute-start.4 = (bf16[256,640]{1,0:T(8,128)(2,1)S(1)}, bf16[256,640]{1,0:T(8,128)(2,1)S(1)}, u32[]{:S(2)}, u32[]{:S(2)}) collective-permute-start(bf16[256,640]{1,0:T(8,128)(2,1)S(1)} %collective-permute-done.3.refs_3_), channel_id=1, source_target_pairs={{0,1},{1,0},{2,3},{3,2},{4,5},{5,4},{6,7},{7,6},{8,9},{9,8},{10,11... | collective-permute-start | bytes 983048 | tf_op jit(solution)/shard_map/ppermute | solution.py:376
  20.2 12.6 %collective-permute-start.6 = (bf16[256,640]{1,0:T(8,128)(2,1)S(1)}, bf16[256,640]{1,0:T(8,128)(2,1)S(1)}, u32[]{:S(2)}, u32[]{:S(2)}) collective-permute-start(bf16[256,640]{1,0:T(8,128)(2,1)S(1)} %collective-permute-done.5.refs_5_), channel_id=1, source_target_pairs={{0,1},{1,0},{2,3},{3,2},{4,5},{5,4},{6,7},{7,6},{8,9},{9,8},{10,11... | collective-permute-start | bytes 983048 | tf_op jit(solution)/shard_map/ppermute | solution.py:376
  27.1 14.8 %all-to-all-start.1 = ((bf16[32,16,128]{2,1,0:T(8,128)(2,1)}), bf16[32,16,128]{2,1,0:T(8,128)(2,1)S(1)}, u32[]{:S(2)}, u32[]{:S(2)}) async-start(bf16[32,16,128]{2,1,0:T(8,128)(2,1)} %shard_map.83), calls=%async_computation.1 | async-start | bytes 262144 | tf_op jit(solution)/shard_map/all_to_all | solution.py:380
  42.9 1.5 %collective-permute-start.7 = (bf16[256,384]{1,0:T(8,128)(2,1)S(1)}, bf16[256,384]{1,0:T(8,128)(2,1)S(1)}, u32[]{:S(2)}, u32[]{:S(2)}) collective-permute-start(bf16[256,384]{1,0:T(8,128)(2,1)S(1)} %shard_map.84.near_ref.after_ref), channel_id=1, source_target_pairs={{0,1},{1,0},{2,3},{3,2},{4,5},{5,4},{6,7},{7,6},{8,9},{9,8},{10,11... | collective-permute-start | bytes 589832 | tf_op jit(solution)/shard_map/ppermute | solution.py:376
  44.9 6.5 %collective-permute-start.10 = (bf16[128,640]{1,0:T(8,128)(2,1)S(1)}, bf16[128,640]{1,0:T(8,128)(2,1)S(1)}, u32[]{:S(2)}, u32[]{:S(2)}) collective-permute-start(bf16[128,640]{1,0:T(8,128)(2,1)S(1)} %get-tuple-element.20), channel_id=1, source_target_pairs={{0,6},{1,7},{2,0},{3,1},{4,2},{5,3},{6,4},{7,5},{8,14},{9,15},{10,... | collective-permute-start | bytes 491528 | tf_op jit(solution)/shard_map/ppermute | solution.py:399
  46.9 7.3 %collective-permute-start.9 = (bf16[128,640]{1,0:T(8,128)(2,1)S(1)}, bf16[128,640]{1,0:T(8,128)(2,1)S(1)}, u32[]{:S(2)}, u32[]{:S(2)}) collective-permute-start(bf16[128,640]{1,0:T(8,128)(2,1)S(1)} %get-tuple-element.19), channel_id=1, source_target_pairs={{0,2},{1,3},{2,4},{3,5},{4,6},{5,7},{6,0},{7,1},{8,10},{9,11},{10,... | collective-permute-start | bytes 491528 | tf_op jit(solution)/shard_map/ppermute | solution.py:398
  54.4 10.1 %collective-permute-start.11 = (bf16[256,640]{1,0:T(8,128)(2,1)S(1)}, bf16[256,640]{1,0:T(8,128)(2,1)S(1)}, u32[]{:S(2)}, u32[]{:S(2)}) collective-permute-start(bf16[256,640]{1,0:T(8,128)(2,1)S(1)} %get-tuple-element.21), channel_id=1, source_target_pairs={{0,2},{1,3},{2,4},{3,5},{4,6},{5,7},{6,0},{7,1},{8,10},{9,11},{10,... | collective-permute-start | bytes 983048 | tf_op jit(solution)/shard_map/ppermute | solution.py:404
  54.5 10.0 %collective-permute-start.12 = (bf16[256,640]{1,0:T(8,128)(2,1)S(1)}, bf16[256,640]{1,0:T(8,128)(2,1)S(1)}, u32[]{:S(2)}, u32[]{:S(2)}) collective-permute-start(bf16[256,640]{1,0:T(8,128)(2,1)S(1)} %get-tuple-element.22), channel_id=1, source_target_pairs={{0,6},{1,7},{2,0},{3,1},{4,2},{5,3},{6,4},{7,5},{8,14},{9,15},{10,... | collective-permute-start | bytes 983048 | tf_op jit(solution)/shard_map/ppermute | solution.py:405

commit v4 on v3

--- a/solution.py
+++ b/solution.py
@@ -24,14 +24,12 @@
 CORE_SWAP = [(i, i ^ 1) for i in range(CHIPS * CORES)]
 
 
-def rope_tables(count, rows):
+def rope_tables(count):
     places = (PL + jnp.arange(count)).astype(jnp.float32)
     freqs = ROPE_BASE ** (-(jnp.arange(HD // 2).astype(jnp.float32) * 2.0 / HD))
     angles = places[:, None] * freqs[None, :]
     cosine, sine = jnp.cos(angles), jnp.sin(angles)
-    cosine = jnp.concatenate([cosine, cosine], -1)
-    sine = jnp.concatenate([-sine, sine], -1)
-    return jnp.tile(cosine, (rows // count, 1)), jnp.tile(sine, (rows // count, 1))
+    return jnp.concatenate([cosine, cosine], -1), jnp.concatenate([-sine, sine], -1)
 
 
 VMEM = pl.BlockSpec(memory_space=pltpu.VMEM)
@@ -90,12 +88,16 @@
     )
 
 
-def project_pairs(rows_ref, weights, copies):
+def project_pairs(rows_ref, weights, copies, later):
     _, width, columns = weights.shape
     total = None
     for pair in range(len(copies) // 2):
         for copy in copies[2 * pair] + copies[2 * pair + 1]:
             copy.wait()
+        if pair == 0:
+            for group in later:
+                for copy in group:
+                    copy.start()
         part = jnp.dot(
             rows_ref[:, 2 * pair * width : 2 * (pair + 1) * width],
             weights[2 * pair : 2 * (pair + 1)].reshape(2 * width, columns),
@@ -114,87 +116,91 @@
     )
 
 
-def project_kernel(x_hbm, *refs):
-    shards = refs[:7]
-    wq_hbm, wkv_hbm, cos_ref, sin_ref = refs[7:11]
-    q_ref, k_ref, v_ref, rows_ref, weights, sems, x_sem = refs[11:]
+def project_kernel(*refs):
+    shards = refs[:6]
+    wq_hbm, wkv_hbm, acc_ref, last_ref, rows_ref, weights, sems, last_sems, row_sems = refs[6:]
     width = weights.shape[1]
-    heads = q_ref.shape[0]
     near = place_in_column((0, -1, 1, 2), False)
     far = place_in_column((0, -1, 1, 2), True)
     order = [index for pair in zip(near, far) for index in pair]
-    own = pltpu.make_async_copy(x_hbm, rows_ref.at[:, 0:width], x_sem)
-    own.start()
     copies = [
-        weight_row_copies(i, index, wq_hbm, wkv_hbm, weights, sems) for i, index in enumerate(order)
-    ]
-    for triple in copies:
-        for copy in triple:
+        (
+            pltpu.make_async_copy(
+                shard, rows_ref.at[:, i * width : (i + 1) * width], row_sems.at[i]
+            ),
+            *weight_row_copies(i, index, wq_hbm, wkv_hbm, weights, sems),
+        )
+        for i, (shard, index) in enumerate(zip(shards, order))
+    ]
+    last = [
+        weight_row_copies(i, index, wq_hbm, wkv_hbm, last_ref, last_sems)
+        for i, index in enumerate(order[6:])
+    ]
+    for group in copies[:4]:
+        for copy in group:
             copy.start()
-    for i, shard in enumerate(shards):
-        rows_ref[:, (i + 1) * width : (i + 2) * width] = shard[...]
-    own.wait()
-    both = project_pairs(rows_ref, weights, copies)
-    cosine, sine = cos_ref[...], sin_ref[...]
-
-    def rotated(h):
-        v = both[:, h * HD : (h + 1) * HD]
-        return (v * cosine + pltpu.roll(v, HD // 2, 1) * sine).astype(jnp.bfloat16)
-
-    for h in range(heads):
-        q_ref[h] = rotated(h)
-    k_ref[...] = rotated(heads)
-    v_ref[...] = both[:, (heads + 1) * HD :].astype(jnp.bfloat16)
-
-
-def project(x, shards, w_query, w_keyval, cosine, sine):
+    acc_ref[...] = project_pairs(rows_ref, weights, copies, copies[4:] + last)
+    for group in last:
+        for copy in group:
+            copy.wait()
+
+
+def project(x, shards, w_query, w_keyval):
     rows, width = x.shape
-    heads = w_query.shape[1] // HD
-    columns = (heads + 2) * HD
+    columns = w_query.shape[1] + 2 * HD
     return pl.pallas_call(
         project_kernel,
-        in_specs=[ANY] + [VMEM] * 7 + [ANY] * 2 + [VMEM] * 2,
-        out_specs=[VMEM] * 3,
+        in_specs=[ANY] * 8,
+        out_specs=[VMEM] * 2,
         out_shape=[
-            jax.ShapeDtypeStruct((heads, rows, HD), jnp.bfloat16),
-            jax.ShapeDtypeStruct((rows, HD), jnp.bfloat16),
-            jax.ShapeDtypeStruct((rows, HD), jnp.bfloat16),
+            jax.ShapeDtypeStruct((rows, columns), jnp.float32),
+            jax.ShapeDtypeStruct((2, width, columns), jnp.bfloat16),
         ],
         scratch_shapes=[
-            pltpu.VMEM((rows, 8 * width), jnp.bfloat16),
-            pltpu.VMEM((8, width, columns), jnp.bfloat16),
-            pltpu.SemaphoreType.DMA((3, 8)),
-            pltpu.SemaphoreType.DMA,
+            pltpu.VMEM((rows, 6 * width), jnp.bfloat16),
+            pltpu.VMEM((6, width, columns), jnp.bfloat16),
+            pltpu.SemaphoreType.DMA((3, 6)),
+            pltpu.SemaphoreType.DMA((3, 2)),
+            pltpu.SemaphoreType.DMA((6,)),
         ],
         compiler_params=params(16),
         cost_estimate=pl.CostEstimate(
-            flops=2 * rows * 8 * width * columns,
+            flops=2 * rows * 6 * width * columns,
             bytes_accessed=16 * width * columns,
             transcendentals=0,
         ),
-    )(
-        in_hbm(x),
-        *shards,
-        in_hbm(w_query),
-        in_hbm(w_keyval),
-        cosine,
-        sine,
+    )(*[in_hbm(v) for v in (x, *shards, w_query, w_keyval)])
+
+
+def attend_kernel(
+    tokens, acc_ref, near_ref, far_ref, weight_ref, cos_ref, sin_ref, cache_ref, valid_ref, attn_ref
+):
+    rows, columns = acc_ref.shape
+    heads = columns // HD - 2
+    width = near_ref.shape[1]
+    shard = jnp.concatenate([near_ref[...], far_ref[...]], -1)
+    both = acc_ref[...] + jnp.dot(
+        shard, weight_ref[...].reshape(2 * width, columns), preferred_element_type=jnp.float32
     )
-
-
-def attend_kernel(tokens, q_ref, k_ref, v_ref, cache_ref, valid_ref, attn_ref):
-    heads, rows, _ = q_ref.shape
+    cosine, sine = cos_ref[...][None], sin_ref[...][None]
+
+    def rotated(h):
+        v = both[:, h * HD : (h + 1) * HD]
+        turned = pltpu.roll(v, HD // 2, 1).reshape(-1, tokens, HD) * sine
+        return (v.reshape(-1, tokens, HD) * cosine + turned).astype(jnp.bfloat16).reshape(rows, HD)
+
     scale = 1.0 / math.sqrt(HD)
     half = cache_ref.shape[0] // 2
-    keys = jnp.concatenate([cache_ref[:half].reshape(PL, HD), k_ref[...]], 0)
-    values = jnp.concatenate([cache_ref[half:].reshape(PL, HD), v_ref[...]], 0)
+    own_values = both[:, (heads + 1) * HD :].astype(jnp.bfloat16)
+    keys = jnp.concatenate([cache_ref[:half].reshape(PL, HD), rotated(heads)], 0)
+    values = jnp.concatenate([cache_ref[half:].reshape(PL, HD), own_values], 0)
     row = lax.broadcasted_iota(jnp.int32, (rows, rows), 0)
     col = lax.broadcasted_iota(jnp.int32, (rows, rows), 1)
     seen = (row // tokens == col // tokens) & (col <= row)
-    valid = valid_ref[...] > 0.0
+    valid = valid_ref[...].astype(jnp.float32) > 0.0
     nt = (((1,), (1,)), ((), ()))
     scores = [
-        lax.dot_general(q_ref[h], keys, nt, preferred_element_type=jnp.float32) * scale
+        lax.dot_general(rotated(h), keys, nt, preferred_element_type=jnp.float32) * scale
         for h in range(heads)
     ]
     for h in range(heads):
@@ -211,20 +217,21 @@
         attn_ref[:, h * HD : (h + 1) * HD] = jnp.where(valid, mixed, 0.0).astype(jnp.bfloat16)
 
 
-def attend(queries, keys, values, cache, valid, tokens):
-    heads, rows, _ = queries.shape
+def attend(acc, near, far, weights, cosine, sine, cache, valid, tokens):
+    rows, columns = acc.shape
+    heads = columns // HD - 2
     return pl.pallas_call(
         functools.partial(attend_kernel, tokens),
-        in_specs=[VMEM] * 5,
+        in_specs=[VMEM] * 8,
         out_specs=VMEM,
         out_shape=jax.ShapeDtypeStruct((rows, heads * HD), jnp.bfloat16),
-        compiler_params=params(8),
+        compiler_params=params(16),
         cost_estimate=pl.CostEstimate(
             flops=8 * heads * rows * PL * HD,
             bytes_accessed=4 * rows * heads * HD,
             transcendentals=2 * heads * rows * PL,
         ),
-    )(queries, keys, values, cache, valid)
+    )(acc, near, far, weights, cosine, sine, cache, valid)
 
 
 def fetch_kernel(shift, after_ref, near_hbm, far_hbm, wo_ref, sems):
@@ -339,9 +346,14 @@
     total = mine_ref[...]
     for part in parts:
         total = total + part[...].astype(jnp.float32)
-    placed = jnp.dot(
-        pick_ref[...], total.astype(jnp.bfloat16), preferred_element_type=jnp.float32
-    )
+    slots, tokens, _ = out_ref.shape
+    rows = total.shape[0]
+    source = lax.broadcasted_iota(jnp.int32, (slots, rows), 1) // tokens
+    row = lax.broadcasted_iota(jnp.int32, (slots, tokens, rows), 2) % tokens
+    token = lax.broadcasted_iota(jnp.int32, (slots, tokens, rows), 1)
+    chosen = jnp.where(source == pick_ref[...], 1.0, 0.0)[:, None, :]
+    picks = jnp.where(row == token, chosen, 0.0).astype(jnp.bfloat16).reshape(-1, rows)
+    placed = jnp.dot(picks, total.astype(jnp.bfloat16), preferred_element_type=jnp.float32)
     out_ref[...] = placed.astype(jnp.bfloat16).reshape(out_ref.shape)
 
 
@@ -376,22 +388,24 @@
     swap = lambda v: lax.ppermute(v, "tp", CORE_SWAP)
     below = lax.ppermute(x, "tp", chip_shift(1))
     above = lax.ppermute(x, "tp", chip_shift(-1))
-    across = lax.ppermute(x, "tp", chip_shift(2))
+    x_again, below, above = lax.optimization_barrier((x, below, above))
+    across = lax.ppermute(x_again, "tp", chip_shift(2))
+    out_far = swap(w_out)
+    shards = [swap(x), below, swap(below), above, swap(above)]
+    pieces, *shards = lax.optimization_barrier((pieces, *shards))
     cache = lax.all_to_all(route(prompt_picks, pieces), "seq", 0, 0, tiled=True)
-    out_far = swap(w_out)
-    shards = [swap(x), below, swap(below), above, swap(above), across, swap(across)]
 
     own_len = lax.dynamic_slice_in_dim(resp_len, group * group_size, group_size, 0)
-    valid = (jnp.arange(tokens)[None, :] < own_len[:, None]).astype(jnp.float32)
+    valid = (jnp.arange(tokens)[None, :] < own_len[:, None]).astype(jnp.bfloat16)
     valid = jnp.broadcast_to(valid.reshape(rows, 1), (rows, HD))
-    cosine, sine = rope_tables(tokens, rows)
+    cosine, sine = rope_tables(tokens)
     own_shard = lax.dynamic_slice_in_dim(resp_shard[:, 0], group * group_size, group_size, 0)
     match = own_shard[None, :] == jnp.arange(learners)[:, None]
     pick = jnp.max(jnp.where(match, jnp.arange(group_size)[None, :], -1), -1)
-    slot_picks = block_picks(pick, tokens, group_size)
-
-    queries, keys, values = project(x, shards, w_query, w_keyval, cosine, sine)
-    attn = attend(queries, keys, values, cache, valid, tokens)
+    pick = jnp.broadcast_to(pick[:, None], (learners, rows)).astype(jnp.int32)
+
+    acc, w_last = project(x, shards, w_query, w_keyval)
+    attn = attend(acc, across, swap(across), w_last, cosine, sine, cache, valid, tokens)
     attn_far = swap(attn)
     w_across = fetch(2, attn, w_out, out_far)
     top, bottom = output_halves(attn, attn_far, w_across)
@@ -404,7 +418,7 @@
         lax.ppermute(to_above, "tp", chip_shift(1)),
         lax.ppermute(to_below, "tp", chip_shift(-1)),
     ]
-    slots = place(slot_picks, mine, parts, learners, tokens)
+    slots = place(pick, mine, parts, learners, tokens)
     return lax.all_to_all(slots, "seq", 0, 0, tiled=True)
 
 

time: 91.2 us -> 88.5 us (0.970)
  blocking collectives: 24.9 us -> 23.8 us
    all_to_all x1, waiting for transfers between devices: 5.62 us -> 4.02 us  [per_device(): pieces = lax.all_to_all(pieces, 'seq', 0, 0, tiled=True)]
    pallas_call x1, Pallas kernels: 5.96 us -> 4.51 us  [project(): pl.pallas_call(project_kernel, in_specs=[ANY] * 8, out_specs=[VMEM] * 2,...]
    all_to_all x1, blocking collectives: 24.9 us -> 23.8 us  [per_device(): return lax.all_to_all(slots, 'seq', 0, 0, tiled=True)]
    all_to_all x1, waiting for transfers between devices: 3.03 us -> 3.96 us  [per_device(): cache = lax.all_to_all(route(prompt_picks, pieces), 'seq', 0, 0, tiled=True)]
  transfers between devices with their start and end apart: 15 -> 15, of which waited for: 6 -> 6; matrix products, arithmetic and copies ran while one was open for 4% -> 3% of each run, Pallas kernels for 14% -> 14%
where the time goes in v4:
time: 88.5 us; the launch traced here: 87.9 us
  starting transfers between devices  28.9 us (33%)
  blocking collectives  23.8 us (27%)
  waiting for transfers between devices  17.8 us (20%)
  Pallas kernels  13.2 us (15%)
  local copies, waits for them, and re-layouts  2.03 us (2%)
  other arithmetic  1.94 us (2%)
    all_to_all x1, blocking collectives, per_device(): return lax.all_to_all(slots, 'seq', 0, 0, tiled=True)  23.8 us
    all_to_all x1, starting transfers between devices, per_device(): pieces = lax.all_to_all(pieces, 'seq', 0, 0, tiled=True)  11.6 us
    all_to_all x1, starting transfers between devices, per_device(): cache = lax.all_to_all(route(prompt_picks, pieces), 'seq', 0, 0, tiled=True)  5.78 us
    ppermute x1, waiting for transfers between devices, per_device(): lax.ppermute(to_above, 'tp', chip_shift(1))  4.84 us
    pallas_call x1, Pallas kernels, project(): pl.pallas_call(project_kernel, in_specs=[ANY] * 8, out_specs=[VMEM] * 2,...  4.51 us
    all_to_all x1, waiting for transfers between devices, per_device(): pieces = lax.all_to_all(pieces, 'seq', 0, 0, tiled=True)  4.02 us
    pallas_call x2, Pallas kernels, output(): pl.pallas_call(functools.partial(output_kernel, shifts), in_specs=[VMEM]...  3.96 us
    all_to_all x1, waiting for transfers between devices, per_device(): cache = lax.all_to_all(route(prompt_picks, pieces), 'seq', 0, 0, tiled=True)  3.96 us
  transfers between devices with their start and end apart: 15, of which 6 were waited for; matrix products, arithmetic and copies ran while one was open for 3% of the time, Pallas kernels for 14%

profile of v4, /device:TPU:2, one launch (start us, length us, event | category | flops | bytes accessed | tf_op | source)
XLA Modules:
  0.0 87.9 jit_solution(828255606724792452)
XLA Ops:
  0.0 0.0 copy-start
  0.0 0.0 collective-permute-start.8
  0.0 1.7 %collective-permute-start.1 = (bf16[256,640]{1,0:T(8,128)(2,1)}, bf16[256,640]{1,0:T(8,128)(2,1)S(1)}, u32[]{:S(2)}, u32[]{:S(2)}) collective-permute-start(bf16[256,640]{1,0:T(8,128)(2,1)} %bitcast.4), channel_id=1, source_target_pairs={{0,2},{1,3},{2,4},{3,5},{4,6},{5,7},{6,0},{7,1},{8,10},{9,11},{10,... | collective-permute-start | bytes 983048 | tf_op jit(solution)/shard_map/ppermute | solution.py:389
  1.7 1.7 %collective-permute-start.2 = (bf16[256,640]{1,0:T(8,128)(2,1)}, bf16[256,640]{1,0:T(8,128)(2,1)S(1)}, u32[]{:S(2)}, u32[]{:S(2)}) collective-permute-start(bf16[256,640]{1,0:T(8,128)(2,1)} %bitcast.5), channel_id=1, source_target_pairs={{0,6},{1,7},{2,0},{3,1},{4,2},{5,3},{6,4},{7,5},{8,14},{9,15},{10,... | collective-permute-start | bytes 983048 | tf_op jit(solution)/shard_map/ppermute | solution.py:390
  3.3 0.0 collective-permute-start
  3.3 11.6 %all-to-all-start = ((bf16[32,16,128]{2,1,0:T(8,128)(2,1)}), bf16[32,16,128]{2,1,0:T(8,128)(2,1)S(1)}, u32[]{:S(2)}, u32[]{:S(2)}) async-start(bf16[32,16,128]{2,1,0:T(8,128)(2,1)} %bitcast.9), calls=%async_computation | async-start | bytes 262144 | tf_op jit(solution)/shard_map/all_to_all | solution.py:385
  15.0 0.7 broadcast_compare_fusion
  15.6 0.7 broadcast_multiply_fusion
  16.3 0.1 fusion.2
  16.4 0.0 collective-permute-done.1.refs_2_
  16.4 0.0 copy-start.1
  16.4 0.0 collective-permute-done.2.refs_4_
  16.4 0.0 copy-start.2
  16.5 0.1 collective-permute-start.3
  16.6 0.5 collective-permute-start.4
  17.1 2.0 %collective-permute-start.5 = (bf16[256,640]{1,0:T(8,128)(2,1)}, bf16[256,640]{1,0:T(8,128)(2,1)S(1)}, u32[]{:S(2)}, u32[]{:S(2)}) collective-permute-start(bf16[256,640]{1,0:T(8,128)(2,1)} %bitcast.7), channel_id=1, source_target_pairs={{0,4},{1,5},{2,6},{3,7},{4,0},{5,1},{6,2},{7,3},{8,12},{9,13},{10,... | collective-permute-start | bytes 983048 | tf_op jit(solution)/shard_map/ppermute | solution.py:392
  19.0 0.1 add_select_fusion
  19.1 0.1 select_n.22
  19.2 0.8 dynamic_slice.7
  20.0 0.1 fusion.pick_ref
  20.1 4.0 %all-to-all-done.piece_ref = bf16[32,16,128]{2,1,0:T(8,128)(2,1)S(1)} async-done(((bf16[32,16,128]{2,1,0:T(8,128)(2,1)}), bf16[32,16,128]{2,1,0:T(8,128)(2,1)S(1)}, u32[]{:S(2)}, u32[]{:S(2)}) %all-to-all-start) | async-done | bytes 131104 | tf_op jit(solution)/shard_map/all_to_all | solution.py:385
  24.1 0.0 collective-permute-done.refs_1_
  24.1 0.0 collective-permute-done.3.refs_3_
  24.1 0.0 copy-start.4
  24.2 0.0 collective-permute-done.4.refs_5_
  24.2 0.0 copy-start.5
  24.2 1.0 %shard_map.83 = bf16[32,16,128]{2,1,0:T(8,128)(2,1)} custom-call(bf16[512,512]{1,0:T(8,128)(2,1)S(1)} %fusion.pick_ref, bf16[32,16,128]{2,1,0:T(8,128)(2,1)S(1)} %all-to-all-done.piece_ref), custom_call_target="tpu_custom_call" | custom-call | tf_op jit(solution)/shard_map/pallas_call | solution.py:67
  25.2 5.8 %all-to-all-start.1 = ((bf16[32,16,128]{2,1,0:T(8,128)(2,1)}), bf16[32,16,128]{2,1,0:T(8,128)(2,1)S(1)}, u32[]{:S(2)}, u32[]{:S(2)}) async-start(bf16[32,16,128]{2,1,0:T(8,128)(2,1)} %shard_map.83), calls=%async_computation.1 | async-start | bytes 262144 | tf_op jit(solution)/shard_map/all_to_all | solution.py:396
  31.0 0.0 copy-done.2
  31.0 0.0 collective-permute-done.5.near_ref
  31.0 0.1 collective-permute-start.6
  31.1 0.1 fusion.1
  31.2 0.1 reshape.70
  31.2 0.0 copy-done.3
  31.3 0.0 copy-done.4
  31.3 0.1 pad_maximum_fusion
  31.3 0.0 copy-done.1
  31.4 4.5 %shard_map.82 = (f32[256,640]{1,0:T(8,128)S(1)}, bf16[2,640,640]{2,1,0:T(8,128)(2,1)S(1)}) custom-call(bf16[256,640]{1,0:T(8,128)(2,1)} %bitcast.8, bf16[256,640]{1,0:T(8,128)(2,1)} %copy-done.3, bf16[256,640]{1,0:T(8,128)(2,1)} %copy-done.1, bf16[256,640]{1,0:T(8,128)(2,1)} %copy-done.4, bf16[256,640]{1,0:T(8,128)(2,1)} %copy-done.2, ...), custom_call_target="tpu_custom_call" | custom-call | flops 1258291200 | bytes 6553600 | tf_op jit(solution)/shard_map/pallas_call | solution.py:151
  35.9 4.0 %all-to-all-done.1.cache_ref = bf16[32,16,128]{2,1,0:T(8,128)(2,1)S(1)} async-done(((bf16[32,16,128]{2,1,0:T(8,128)(2,1)}), bf16[32,16,128]{2,1,0:T(8,128)(2,1)S(1)}, u32[]{:S(2)}, u32[]{:S(2)}) %all-to-all-start.1) | async-done | bytes 131104 | tf_op jit(solution)/shard_map/all_to_all | solution.py:396
  39.8 0.0 collective-permute-done.6.far_ref
  39.8 0.1 broadcast_in_dim.33.valid_ref
  39.9 1.5 %shard_map.84.near_ref.after_ref = bf16[256,384]{1,0:T(8,128)(2,1)S(1)} custom-call(f32[256,640]{1,0:T(8,128)S(1)} %get-tuple-element.29.acc_ref, bf16[256,640]{1,0:T(8,128)(2,1)S(1)} %collective-permute-done.5.near_ref, bf16[256,640]{1,0:T(8,128)(2,1)S(1)} %collective-permute-done.6.far_ref, bf16[2,640,640]{2,1,0:T(8,128)(2,1)S(1)} %get-tuple-element.31.weight_ref, ...), custom_call_target="tpu_custom_call" | custom-call | flops 201326592 | bytes 393216 | tf_op jit(solution)/shard_map/pallas_call | solution.py:223
  41.5 0.1 collective-permute-start.7
  41.6 0.0 collective-permute-done.8.far_hbm
  41.6 1.2 %shard_map.87.wo_ref = bf16[1,768,640]{2,1,0:T(8,128)(2,1)S(1)} custom-call(bf16[256,384]{1,0:T(8,128)(2,1)S(1)} %shard_map.84.near_ref.after_ref, bf16[384,5120]{1,0:T(8,128)(2,1)} %near_hbm.5, bf16[384,5120]{1,0:T(8,128)(2,1)} %collective-permute-done.8.far_hbm), custom_call_target="tpu_custom_call" | custom-call | bytes 1966080 | tf_op jit(solution)/shard_map/pallas_call | solution.py:248
  42.8 0.2 collective-permute-done.7.far_ref
  43.0 0.5 shard_map.88
  43.5 1.8 %collective-permute-start.10 = (bf16[128,640]{1,0:T(8,128)(2,1)S(1)}, bf16[128,640]{1,0:T(8,128)(2,1)S(1)}, u32[]{:S(2)}, u32[]{:S(2)}) collective-permute-start(bf16[128,640]{1,0:T(8,128)(2,1)S(1)} %get-tuple-element.36), channel_id=1, source_target_pairs={{0,6},{1,7},{2,0},{3,1},{4,2},{5,3},{6,4},{7,5},{8,14},{9,15},{10,... | collective-permute-start | bytes 491528 | tf_op jit(solution)/shard_map/ppermute | solution.py:413
  45.3 0.3 collective-permute-start.9
  45.6 2.3 %shard_map.86 = (f32[256,640]{1,0:T(8,128)S(1)}, f32[256,640]{1,0:T(8,128)S(1)}) custom-call(bf16[256,384]{1,0:T(8,128)(2,1)S(1)} %shard_map.84.near_ref.after_ref, bf16[256,384]{1,0:T(8,128)(2,1)S(1)} %collective-permute-done.7.far_ref, bf16[384,5120]{1,0:T(8,128)(2,1)} %near_hbm.5, bf16[384,5120]{1,0:T(8,128)(2,1)} %collective-permute-done.8.far_hbm), custom_call_target="tpu_custom_call" | custom-call | flops 503316480 | bytes 1966080 | tf_op jit(solution)/shard_map/pallas_call | solution.py:309
  47.9 2.1 %collective-permute-done.10.bottom_ref = bf16[128,640]{1,0:T(8,128)(2,1)S(1)} collective-permute-done((bf16[128,640]{1,0:T(8,128)(2,1)S(1)}, bf16[128,640]{1,0:T(8,128)(2,1)S(1)}, u32[]{:S(2)}, u32[]{:S(2)}) %collective-permute-start.10) | collective-permute-done | bytes 163872 | tf_op jit(solution)/shard_map/ppermute | solution.py:413
  50.0 2.7 %collective-permute-done.9.top_ref = bf16[128,640]{1,0:T(8,128)(2,1)S(1)} collective-permute-done((bf16[128,640]{1,0:T(8,128)(2,1)S(1)}, bf16[128,640]{1,0:T(8,128)(2,1)S(1)}, u32[]{:S(2)}, u32[]{:S(2)}) %collective-permute-start.9) | collective-permute-done | bytes 163872 | tf_op jit(solution)/shard_map/ppermute | solution.py:412
  52.6 0.1 shard_map.89
  52.7 0.1 collective-permute-start.11
  52.8 3.2 %collective-permute-start.12 = (bf16[256,640]{1,0:T(8,128)(2,1)S(1)}, bf16[256,640]{1,0:T(8,128)(2,1)S(1)}, u32[]{:S(2)}, u32[]{:S(2)}) collective-permute-start(bf16[256,640]{1,0:T(8,128)(2,1)S(1)} %get-tuple-element.38), channel_id=1, source_target_pairs={{0,6},{1,7},{2,0},{3,1},{4,2},{5,3},{6,4},{7,5},{8,14},{9,15},{10,... | collective-permute-start | bytes 983048 | tf_op jit(solution)/shard_map/ppermute | solution.py:419
  56.0 0.1 dynamic-slice_bitcast_fusion
  56.1 0.1 select_reduce_fusion
  56.2 1.7 %shard_map.85.mine_ref = f32[256,640]{1,0:T(8,128)S(1)} custom-call(bf16[256,384]{1,0:T(8,128)(2,1)S(1)} %shard_map.84.near_ref.after_ref, bf16[256,384]{1,0:T(8,128)(2,1)S(1)} %collective-permute-done.7.far_ref, bf16[384,5120]{1,0:T(8,128)(2,1)} %near_hbm.5, bf16[384,5120]{1,0:T(8,128)(2,1)} %collective-permute-done.8.far_hbm), custom_call_target="tpu_custom_call" | custom-call | flops 251658240 | bytes 983040 | tf_op jit(solution)/shard_map/pallas_call | solution.py:309
  57.9 4.8 %collective-permute-done.11.refs_0_ = bf16[256,640]{1,0:T(8,128)(2,1)S(1)} collective-permute-done((bf16[256,640]{1,0:T(8,128)(2,1)S(1)}, bf16[256,640]{1,0:T(8,128)(2,1)S(1)}, u32[]{:S(2)}, u32[]{:S(2)}) %collective-permute-start.11) | collective-permute-done | bytes 327712 | tf_op jit(solution)/shard_map/ppermute | solution.py:418
  62.8 0.0 collective-permute-done.12.refs_1_
  62.8 0.1 broadcast_in_dim.30.pick_ref
  62.9 0.4 shard_map.90
  63.3 23.8 %all_to_all.15 = bf16[32,16,640]{2,1,0:T(8,128)(2,1)S(1)} all-to-all(bf16[32,16,640]{2,1,0:T(8,128)(2,1)S(1)} %shard_map.90), channel_id=1, replica_groups=mesh['seq'=32,'tp'=8] {'seq'}, dimensions={0} | all-to-all | bytes 1310720 | tf_op jit(solution)/shard_map/all_to_all | solution.py:422
  87.0 0.8 copy.10
  (5 shorter events, 0.0 us)
Async XLA Ops:
  0.0 56.0 %copy-start = (s32[512,1]{0,1:T(1,128)S(1)}, s32[512,1]{0,1:T(1,128)}, u32[]{:S(2)}) copy-start(s32[512,1]{0,1:T(1,128)} %param.10) | copy-start | bytes 6148
  0.0 41.6 %collective-permute-start.8 = (bf16[384,5120]{1,0:T(8,128)(2,1)}, bf16[384,5120]{1,0:T(8,128)(2,1)}, u32[]{:S(2)}, u32[]{:S(2)}) collective-permute-start(bf16[384,5120]{1,0:T(8,128)(2,1)} %near_hbm.5), channel_id=1, source_target_pairs={{0,1},{1,0},{2,3},{3,2},{4,5},{5,4},{6,7},{7,6},{8,9},{9,8},{10,11... | collective-permute-start | bytes 11796488 | tf_op jit(solution)/shard_map/ppermute | solution.py:388
  0.0 16.4 %collective-permute-start.1 = (bf16[256,640]{1,0:T(8,128)(2,1)}, bf16[256,640]{1,0:T(8,128)(2,1)S(1)}, u32[]{:S(2)}, u32[]{:S(2)}) collective-permute-start(bf16[256,640]{1,0:T(8,128)(2,1)} %bitcast.4), channel_id=1, source_target_pairs={{0,2},{1,3},{2,4},{3,5},{4,6},{5,7},{6,0},{7,1},{8,10},{9,11},{10,... | collective-permute-start | bytes 983048 | tf_op jit(solution)/shard_map/ppermute | solution.py:389
  1.7 14.8 %collective-permute-start.2 = (bf16[256,640]{1,0:T(8,128)(2,1)}, bf16[256,640]{1,0:T(8,128)(2,1)S(1)}, u32[]{:S(2)}, u32[]{:S(2)}) collective-permute-start(bf16[256,640]{1,0:T(8,128)(2,1)} %bitcast.5), channel_id=1, source_target_pairs={{0,6},{1,7},{2,0},{3,1},{4,2},{5,3},{6,4},{7,5},{8,14},{9,15},{10,... | collective-permute-start | bytes 983048 | tf_op jit(solution)/shard_map/ppermute | solution.py:390
  3.3 20.8 %collective-permute-start = (bf16[256,640]{1,0:T(8,128)(2,1)}, bf16[256,640]{1,0:T(8,128)(2,1)S(1)}, u32[]{:S(2)}, u32[]{:S(2)}) collective-permute-start(bf16[256,640]{1,0:T(8,128)(2,1)} %bitcast.6), channel_id=1, source_target_pairs={{0,1},{1,0},{2,3},{3,2},{4,5},{5,4},{6,7},{7,6},{8,9},{9,8},{10,11... | collective-permute-start | bytes 983048 | tf_op jit(solution)/shard_map/ppermute | solution.py:388
  3.3 20.8 %all-to-all-start = ((bf16[32,16,128]{2,1,0:T(8,128)(2,1)}), bf16[32,16,128]{2,1,0:T(8,128)(2,1)S(1)}, u32[]{:S(2)}, u32[]{:S(2)}) async-start(bf16[32,16,128]{2,1,0:T(8,128)(2,1)} %bitcast.9), calls=%async_computation | async-start | bytes 262144 | tf_op jit(solution)/shard_map/all_to_all | solution.py:385
  16.4 14.9 %copy-start.1 = (bf16[256,640]{1,0:T(8,128)(2,1)}, bf16[256,640]{1,0:T(8,128)(2,1)S(1)}, u32[]{:S(2)}) copy-start(bf16[256,640]{1,0:T(8,128)(2,1)S(1)} %collective-permute-done.1.refs_2_) | copy-start | bytes 983044
  16.4 14.5 %copy-start.2 = (bf16[256,640]{1,0:T(8,128)(2,1)}, bf16[256,640]{1,0:T(8,128)(2,1)S(1)}, u32[]{:S(2)}) copy-start(bf16[256,640]{1,0:T(8,128)(2,1)S(1)} %collective-permute-done.2.refs_4_) | copy-start | bytes 983044
  16.5 7.7 %collective-permute-start.3 = (bf16[256,640]{1,0:T(8,128)(2,1)S(1)}, bf16[256,640]{1,0:T(8,128)(2,1)S(1)}, u32[]{:S(2)}, u32[]{:S(2)}) collective-permute-start(bf16[256,640]{1,0:T(8,128)(2,1)S(1)} %collective-permute-done.1.refs_2_), channel_id=1, source_target_pairs={{0,1},{1,0},{2,3},{3,2},{4,5},{5,4},{6,7},{7,6},{8,9},{9,8},{10,11... | collective-permute-start | bytes 983048 | tf_op jit(solution)/shard_map/ppermute | solution.py:388
  16.6 7.6 %collective-permute-start.4 = (bf16[256,640]{1,0:T(8,128)(2,1)S(1)}, bf16[256,640]{1,0:T(8,128)(2,1)S(1)}, u32[]{:S(2)}, u32[]{:S(2)}) collective-permute-start(bf16[256,640]{1,0:T(8,128)(2,1)S(1)} %collective-permute-done.2.refs_4_), channel_id=1, source_target_pairs={{0,1},{1,0},{2,3},{3,2},{4,5},{5,4},{6,7},{7,6},{8,9},{9,8},{10,11... | collective-permute-start | bytes 983048 | tf_op jit(solution)/shard_map/ppermute | solution.py:388
  17.1 13.9 %collective-permute-start.5 = (bf16[256,640]{1,0:T(8,128)(2,1)}, bf16[256,640]{1,0:T(8,128)(2,1)S(1)}, u32[]{:S(2)}, u32[]{:S(2)}) collective-permute-start(bf16[256,640]{1,0:T(8,128)(2,1)} %bitcast.7), channel_id=1, source_target_pairs={{0,4},{1,5},{2,6},{3,7},{4,0},{5,1},{6,2},{7,3},{8,12},{9,13},{10,... | collective-permute-start | bytes 983048 | tf_op jit(solution)/shard_map/ppermute | solution.py:392
  24.1 7.1 %copy-start.3 = (bf16[256,640]{1,0:T(8,128)(2,1)}, bf16[256,640]{1,0:T(8,128)(2,1)S(1)}, u32[]{:S(2)}) copy-start(bf16[256,640]{1,0:T(8,128)(2,1)S(1)} %collective-permute-done.refs_1_) | copy-start | bytes 983044
  24.1 7.1 %copy-start.4 = (bf16[256,640]{1,0:T(8,128)(2,1)}, bf16[256,640]{1,0:T(8,128)(2,1)S(1)}, u32[]{:S(2)}) copy-start(bf16[256,640]{1,0:T(8,128)(2,1)S(1)} %collective-permute-done.3.refs_3_) | copy-start | bytes 983044
  24.2 7.1 %copy-start.5 = (bf16[256,640]{1,0:T(8,128)(2,1)}, bf16[256,640]{1,0:T(8,128)(2,1)S(1)}, u32[]{:S(2)}) copy-start(bf16[256,640]{1,0:T(8,128)(2,1)S(1)} %collective-permute-done.4.refs_5_) | copy-start | bytes 983044
  25.2 14.7 %all-to-all-start.1 = ((bf16[32,16,128]{2,1,0:T(8,128)(2,1)}), bf16[32,16,128]{2,1,0:T(8,128)(2,1)S(1)}, u32[]{:S(2)}, u32[]{:S(2)}) async-start(bf16[32,16,128]{2,1,0:T(8,128)(2,1)} %shard_map.83), calls=%async_computation.1 | async-start | bytes 262144 | tf_op jit(solution)/shard_map/all_to_all | solution.py:396
  31.0 8.8 %collective-permute-start.6 = (bf16[256,640]{1,0:T(8,128)(2,1)S(1)}, bf16[256,640]{1,0:T(8,128)(2,1)S(1)}, u32[]{:S(2)}, u32[]{:S(2)}) collective-permute-start(bf16[256,640]{1,0:T(8,128)(2,1)S(1)} %collective-permute-done.5.near_ref), channel_id=1, source_target_pairs={{0,1},{1,0},{2,3},{3,2},{4,5},{5,4},{6,7},{7,6},{8,9},{9,8},{10,11... | collective-permute-start | bytes 983048 | tf_op jit(solution)/shard_map/ppermute | solution.py:388
  41.5 1.5 %collective-permute-start.7 = (bf16[256,384]{1,0:T(8,128)(2,1)S(1)}, bf16[256,384]{1,0:T(8,128)(2,1)S(1)}, u32[]{:S(2)}, u32[]{:S(2)}) collective-permute-start(bf16[256,384]{1,0:T(8,128)(2,1)S(1)} %shard_map.84.near_ref.after_ref), channel_id=1, source_target_pairs={{0,1},{1,0},{2,3},{3,2},{4,5},{5,4},{6,7},{7,6},{8,9},{9,8},{10,11... | collective-permute-start | bytes 589832 | tf_op jit(solution)/shard_map/ppermute | solution.py:388
  43.5 6.5 %collective-permute-start.10 = (bf16[128,640]{1,0:T(8,128)(2,1)S(1)}, bf16[128,640]{1,0:T(8,128)(2,1)S(1)}, u32[]{:S(2)}, u32[]{:S(2)}) collective-permute-start(bf16[128,640]{1,0:T(8,128)(2,1)S(1)} %get-tuple-element.36), channel_id=1, source_target_pairs={{0,6},{1,7},{2,0},{3,1},{4,2},{5,3},{6,4},{7,5},{8,14},{9,15},{10,... | collective-permute-start | bytes 491528 | tf_op jit(solution)/shard_map/ppermute | solution.py:413
  45.3 7.3 %collective-permute-start.9 = (bf16[128,640]{1,0:T(8,128)(2,1)S(1)}, bf16[128,640]{1,0:T(8,128)(2,1)S(1)}, u32[]{:S(2)}, u32[]{:S(2)}) collective-permute-start(bf16[128,640]{1,0:T(8,128)(2,1)S(1)} %get-tuple-element.35), channel_id=1, source_target_pairs={{0,2},{1,3},{2,4},{3,5},{4,6},{5,7},{6,0},{7,1},{8,10},{9,11},{10,... | collective-permute-start | bytes 491528 | tf_op jit(solution)/shard_map/ppermute | solution.py:412
  52.7 10.1 %collective-permute-start.11 = (bf16[256,640]{1,0:T(8,128)(2,1)S(1)}, bf16[256,640]{1,0:T(8,128)(2,1)S(1)}, u32[]{:S(2)}, u32[]{:S(2)}) collective-permute-start(bf16[256,640]{1,0:T(8,128)(2,1)S(1)} %get-tuple-element.37), channel_id=1, source_target_pairs={{0,2},{1,3},{2,4},{3,5},{4,6},{5,7},{6,0},{7,1},{8,10},{9,11},{10,... | collective-permute-start | bytes 983048 | tf_op jit(solution)/shard_map/ppermute | solution.py:418
  52.8 10.0 %collective-permute-start.12 = (bf16[256,640]{1,0:T(8,128)(2,1)S(1)}, bf16[256,640]{1,0:T(8,128)(2,1)S(1)}, u32[]{:S(2)}, u32[]{:S(2)}) collective-permute-start(bf16[256,640]{1,0:T(8,128)(2,1)S(1)} %get-tuple-element.38), channel_id=1, source_target_pairs={{0,6},{1,7},{2,0},{3,1},{4,2},{5,3},{6,4},{7,5},{8,14},{9,15},{10,... | collective-permute-start | bytes 983048 | tf_op jit(solution)/shard_map/ppermute | solution.py:419

commit v5 on v4

--- a/solution.py
+++ b/solution.py
@@ -54,6 +54,14 @@
 
 def columns_at(index, width):
     return pl.ds(pl.multiple_of(index * width, width), width)
+
+
+def block_picks(source, slots, size, rows):
+    block = lax.broadcasted_iota(jnp.int32, (slots, rows), 1) // size
+    row = lax.broadcasted_iota(jnp.int32, (slots, size, rows), 2) % size
+    place = lax.broadcasted_iota(jnp.int32, (slots, size, rows), 1)
+    chosen = jnp.where(block == source, 1.0, 0.0)[:, None, :]
+    return jnp.where(row == place, chosen, 0.0).astype(jnp.bfloat16).reshape(-1, rows)
 
 
 def route_kernel(pick_ref, piece_ref, out_ref):
@@ -94,10 +102,9 @@
     for pair in range(len(copies) // 2):
         for copy in copies[2 * pair] + copies[2 * pair + 1]:
             copy.wait()
-        if pair == 0:
-            for group in later:
-                for copy in group:
-                    copy.start()
+        for group in later[pair] if pair < len(later) else ():
+            for copy in group:
+                copy.start()
         part = jnp.dot(
             rows_ref[:, 2 * pair * width : 2 * (pair + 1) * width],
             weights[2 * pair : 2 * (pair + 1)].reshape(2 * width, columns),
@@ -139,7 +146,7 @@
     for group in copies[:4]:
         for copy in group:
             copy.start()
-    acc_ref[...] = project_pairs(rows_ref, weights, copies, copies[4:] + last)
+    acc_ref[...] = project_pairs(rows_ref, weights, copies, [copies[4:], last])
     for group in last:
         for copy in group:
             copy.wait()
@@ -173,7 +180,7 @@
 
 
 def attend_kernel(
-    tokens, acc_ref, near_ref, far_ref, weight_ref, cos_ref, sin_ref, cache_ref, valid_ref, attn_ref
+    tokens, acc_ref, near_ref, far_ref, weight_ref, cos_ref, sin_ref, cache_ref, attn_ref
 ):
     rows, columns = acc_ref.shape
     heads = columns // HD - 2
@@ -197,7 +204,6 @@
     row = lax.broadcasted_iota(jnp.int32, (rows, rows), 0)
     col = lax.broadcasted_iota(jnp.int32, (rows, rows), 1)
     seen = (row // tokens == col // tokens) & (col <= row)
-    valid = valid_ref[...].astype(jnp.float32) > 0.0
     nt = (((1,), (1,)), ((), ()))
     scores = [
         lax.dot_general(rotated(h), keys, nt, preferred_element_type=jnp.float32) * scale
@@ -214,15 +220,15 @@
             [(prior * inverse).astype(jnp.bfloat16), (recent * inverse).astype(jnp.bfloat16)], -1
         )
         mixed = jnp.dot(weights, values, preferred_element_type=jnp.float32)
-        attn_ref[:, h * HD : (h + 1) * HD] = jnp.where(valid, mixed, 0.0).astype(jnp.bfloat16)
-
-
-def attend(acc, near, far, weights, cosine, sine, cache, valid, tokens):
+        attn_ref[:, h * HD : (h + 1) * HD] = mixed.astype(jnp.bfloat16)
+
+
+def attend(acc, near, far, weights, cosine, sine, cache, tokens):
     rows, columns = acc.shape
     heads = columns // HD - 2
     return pl.pallas_call(
         functools.partial(attend_kernel, tokens),
-        in_specs=[VMEM] * 8,
+        in_specs=[VMEM] * 7,
         out_specs=VMEM,
         out_shape=jax.ShapeDtypeStruct((rows, heads * HD), jnp.bfloat16),
         compiler_params=params(16),
@@ -231,7 +237,7 @@
             bytes_accessed=4 * rows * heads * HD,
             transcendentals=2 * heads * rows * PL,
         ),
-    )(acc, near, far, weights, cosine, sine, cache, valid)
+    )(acc, near, far, weights, cosine, sine, cache)
 
 
 def fetch_kernel(shift, after_ref, near_hbm, far_hbm, wo_ref, sems):
@@ -341,37 +347,28 @@
     )(above, below, top, bottom)
 
 
-def place_kernel(pick_ref, mine_ref, *refs):
+def place_kernel(pick_ref, count_ref, mine_ref, *refs):
     parts, out_ref = refs[:-1], refs[-1]
     total = mine_ref[...]
     for part in parts:
         total = total + part[...].astype(jnp.float32)
-    slots, tokens, _ = out_ref.shape
-    rows = total.shape[0]
-    source = lax.broadcasted_iota(jnp.int32, (slots, rows), 1) // tokens
-    row = lax.broadcasted_iota(jnp.int32, (slots, tokens, rows), 2) % tokens
-    token = lax.broadcasted_iota(jnp.int32, (slots, tokens, rows), 1)
-    chosen = jnp.where(source == pick_ref[...], 1.0, 0.0)[:, None, :]
-    picks = jnp.where(row == token, chosen, 0.0).astype(jnp.bfloat16).reshape(-1, rows)
+    slots, tokens, width = out_ref.shape
+    picks = block_picks(pick_ref[...], slots, tokens, total.shape[0])
     placed = jnp.dot(picks, total.astype(jnp.bfloat16), preferred_element_type=jnp.float32)
-    out_ref[...] = placed.astype(jnp.bfloat16).reshape(out_ref.shape)
-
-
-def place(pick, mine, parts, slots, tokens):
+    token = lax.broadcasted_iota(jnp.int32, (slots, tokens, width), 1)
+    valid = token < count_ref[:, 0:1][:, None, :]
+    out_ref[...] = jnp.where(valid, placed.reshape(slots, tokens, width), 0.0).astype(jnp.bfloat16)
+
+
+def place(pick, count, mine, parts, slots, tokens):
     _, width = mine.shape
     return pl.pallas_call(
         place_kernel,
-        in_specs=[VMEM] * (2 + len(parts)),
+        in_specs=[VMEM] * (3 + len(parts)),
         out_specs=VMEM,
         out_shape=jax.ShapeDtypeStruct((slots, tokens, width), jnp.bfloat16),
         compiler_params=params(8),
-    )(pick, mine, *parts)
-
-
-def block_picks(source, size, count):
-    rows = source[:, None] * size + jnp.arange(size)[None, :]
-    rows = jnp.where(source[:, None] >= 0, rows, -1).reshape(-1)
-    return (rows[:, None] == jnp.arange(count * size)[None, :]).astype(jnp.bfloat16)
+    )(pick, count, mine, *parts)
 
 
 def per_device(resp_rows, resp_len, resp_shard, group_prompt, prompt_kv, w_query, w_keyval, w_out):
@@ -381,7 +378,9 @@
     rows = group_size * tokens
 
     pieces = prompt_kv.reshape(learners, -1, HD)
-    prompt_picks = block_picks(group_prompt, pieces.shape[1], learners)
+    size = pieces.shape[1]
+    source = group_prompt[:, None] * size + jnp.arange(size)[None, :]
+    prompts = (source.reshape(-1)[:, None] == jnp.arange(learners * size)[None, :]).astype(jnp.bfloat16)
     pieces = lax.all_to_all(pieces, "seq", 0, 0, tiled=True)
 
     x = resp_rows.reshape(rows, width)
@@ -389,23 +388,24 @@
     below = lax.ppermute(x, "tp", chip_shift(1))
     above = lax.ppermute(x, "tp", chip_shift(-1))
     x_again, below, above = lax.optimization_barrier((x, below, above))
-    across = lax.ppermute(x_again, "tp", chip_shift(2))
+    x_far = swap(x_again)
+    x_last, x_far = lax.optimization_barrier((x, x_far))
+    across = lax.ppermute(x_last, "tp", chip_shift(2))
     out_far = swap(w_out)
-    shards = [swap(x), below, swap(below), above, swap(above)]
+    shards = [x_far, below, swap(below), above, swap(above)]
     pieces, *shards = lax.optimization_barrier((pieces, *shards))
-    cache = lax.all_to_all(route(prompt_picks, pieces), "seq", 0, 0, tiled=True)
-
+    cache = lax.all_to_all(route(prompts, pieces), "seq", 0, 0, tiled=True)
+
+    cosine, sine = rope_tables(tokens)
+    acc, w_last = project(x, shards, w_query, w_keyval)
+    attn = attend(acc, across, swap(across), w_last, cosine, sine, cache, tokens)
+    resp_len, resp_shard, attn = lax.optimization_barrier((resp_len, resp_shard, attn))
     own_len = lax.dynamic_slice_in_dim(resp_len, group * group_size, group_size, 0)
-    valid = (jnp.arange(tokens)[None, :] < own_len[:, None]).astype(jnp.bfloat16)
-    valid = jnp.broadcast_to(valid.reshape(rows, 1), (rows, HD))
-    cosine, sine = rope_tables(tokens)
     own_shard = lax.dynamic_slice_in_dim(resp_shard[:, 0], group * group_size, group_size, 0)
     match = own_shard[None, :] == jnp.arange(learners)[:, None]
     pick = jnp.max(jnp.where(match, jnp.arange(group_size)[None, :], -1), -1)
-    pick = jnp.broadcast_to(pick[:, None], (learners, rows)).astype(jnp.int32)
-
-    acc, w_last = project(x, shards, w_query, w_keyval)
-    attn = attend(acc, across, swap(across), w_last, cosine, sine, cache, valid, tokens)
+    count = jnp.max(jnp.where(match, own_len[None, :], 0), -1)
+    spread = lambda v: jnp.broadcast_to(v[:, None], (learners, rows)).astype(jnp.int32)
     attn_far = swap(attn)
     w_across = fetch(2, attn, w_out, out_far)
     top, bottom = output_halves(attn, attn_far, w_across)
@@ -418,7 +418,7 @@
         lax.ppermute(to_above, "tp", chip_shift(1)),
         lax.ppermute(to_below, "tp", chip_shift(-1)),
     ]
-    slots = place(pick, mine, parts, learners, tokens)
+    slots = place(spread(pick), spread(count), mine, parts, learners, tokens)
     return lax.all_to_all(slots, "seq", 0, 0, tiled=True)
 
 

time: 88.5 us -> 87.7 us (level)
    ppermute x6, waiting for transfers between devices: 0.2 us -> 1.33 us  [per_device(): swap = lambda v: lax.ppermute(v, 'tp', CORE_SWAP)]
  transfers between devices with their start and end apart: 15 -> 15, of which waited for: 6 -> 7; matrix products, arithmetic and copies ran while one was open for 3% -> 2% of each run, Pallas kernels for 14% -> 14%
where the time goes in v5:
time: 87.7 us; the launch traced here: 87.1 us
  starting transfers between devices  28.9 us (33%)
  blocking collectives  23.7 us (27%)
  waiting for transfers between devices  18 us (21%)
  Pallas kernels  13.1 us (15%)
  local copies, waits for them, and re-layouts  1.9 us (2%)
  other arithmetic  1.19 us (1%)
    all_to_all x1, blocking collectives, per_device(): return lax.all_to_all(slots, 'seq', 0, 0, tiled=True)  23.7 us
    all_to_all x1, starting transfers between devices, per_device(): pieces = lax.all_to_all(pieces, 'seq', 0, 0, tiled=True)  11.6 us
    all_to_all x1, starting transfers between devices, per_device(): cache = lax.all_to_all(route(prompts, pieces), 'seq', 0, 0, tiled=True)  5.72 us
    pallas_call x1, Pallas kernels, project(): pl.pallas_call(project_kernel, in_specs=[ANY] * 8, out_specs=[VMEM] * 2,...  4.51 us
    ppermute x1, waiting for transfers between devices, per_device(): lax.ppermute(to_above, 'tp', chip_shift(1))  4.12 us
    all_to_all x1, waiting for transfers between devices, per_device(): pieces = lax.all_to_all(pieces, 'seq', 0, 0, tiled=True)  4.09 us
    all_to_all x1, waiting for transfers between devices, per_device(): cache = lax.all_to_all(route(prompts, pieces), 'seq', 0, 0, tiled=True)  4 us
    pallas_call x2, Pallas kernels, output(): pl.pallas_call(functools.partial(output_kernel, shifts), in_specs=[VMEM]...  3.95 us
  transfers between devices with their start and end apart: 15, of which 7 were waited for; matrix products, arithmetic and copies ran while one was open for 2% of the time, Pallas kernels for 14%

profile of v5, /device:TPU:2, one launch (start us, length us, event | category | flops | bytes accessed | tf_op | source)
XLA Modules:
  0.0 87.1 jit_solution(4539243544932925764)
XLA Ops:
  0.0 0.0 copy-start
  0.0 0.0 collective-permute-start.8
  0.0 1.7 %collective-permute-start = (bf16[256,640]{1,0:T(8,128)(2,1)}, bf16[256,640]{1,0:T(8,128)(2,1)S(1)}, u32[]{:S(2)}, u32[]{:S(2)}) collective-permute-start(bf16[256,640]{1,0:T(8,128)(2,1)} %bitcast.4), channel_id=1, source_target_pairs={{0,2},{1,3},{2,4},{3,5},{4,6},{5,7},{6,0},{7,1},{8,10},{9,11},{10,... | collective-permute-start | bytes 983048 | tf_op jit(solution)/shard_map/ppermute | solution.py:388
  1.7 1.7 %collective-permute-start.1 = (bf16[256,640]{1,0:T(8,128)(2,1)}, bf16[256,640]{1,0:T(8,128)(2,1)S(1)}, u32[]{:S(2)}, u32[]{:S(2)}) collective-permute-start(bf16[256,640]{1,0:T(8,128)(2,1)} %bitcast.5), channel_id=1, source_target_pairs={{0,6},{1,7},{2,0},{3,1},{4,2},{5,3},{6,4},{7,5},{8,14},{9,15},{10,... | collective-permute-start | bytes 983048 | tf_op jit(solution)/shard_map/ppermute | solution.py:389
  3.3 11.6 %all-to-all-start = ((bf16[32,16,128]{2,1,0:T(8,128)(2,1)}), bf16[32,16,128]{2,1,0:T(8,128)(2,1)S(1)}, u32[]{:S(2)}, u32[]{:S(2)}) async-start(bf16[32,16,128]{2,1,0:T(8,128)(2,1)} %bitcast.9), calls=%async_computation | async-start | bytes 262144 | tf_op jit(solution)/shard_map/all_to_all | solution.py:384
  14.9 0.7 broadcast_multiply_fusion
  15.6 0.0 collective-permute-done.refs_2_
  15.6 0.0 copy-start.1
  15.6 0.0 collective-permute-done.1.refs_4_
  15.6 0.0 copy-start.2
  15.6 0.1 collective-permute-start.2
  15.7 0.1 iota_add_fusion
  15.8 0.5 collective-permute-start.3
  16.3 0.1 collective-permute-start.4
  16.4 1.1 %collective-permute-done.2.refs_1_ = bf16[256,640]{1,0:T(8,128)(2,1)S(1)} collective-permute-done((bf16[256,640]{1,0:T(8,128)(2,1)}, bf16[256,640]{1,0:T(8,128)(2,1)S(1)}, u32[]{:S(2)}, u32[]{:S(2)}) %collective-permute-start.2) | collective-permute-done | bytes 327712 | tf_op jit(solution)/shard_map/ppermute | solution.py:387
  17.6 0.0 copy-start.3
  17.6 2.0 %collective-permute-start.5 = (bf16[256,640]{1,0:T(8,128)(2,1)}, bf16[256,640]{1,0:T(8,128)(2,1)S(1)}, u32[]{:S(2)}, u32[]{:S(2)}) collective-permute-start(bf16[256,640]{1,0:T(8,128)(2,1)} %bitcast.7), channel_id=1, source_target_pairs={{0,4},{1,5},{2,6},{3,7},{4,0},{5,1},{6,2},{7,3},{8,12},{9,13},{10,... | collective-permute-start | bytes 983048 | tf_op jit(solution)/shard_map/ppermute | solution.py:393
  19.5 0.0 copy-done.3
  19.5 0.1 add.43
  19.6 0.2 fusion.pick_ref
  19.8 4.1 %all-to-all-done.piece_ref = bf16[32,16,128]{2,1,0:T(8,128)(2,1)S(1)} async-done(((bf16[32,16,128]{2,1,0:T(8,128)(2,1)}), bf16[32,16,128]{2,1,0:T(8,128)(2,1)S(1)}, u32[]{:S(2)}, u32[]{:S(2)}) %all-to-all-start) | async-done | bytes 131104 | tf_op jit(solution)/shard_map/all_to_all | solution.py:384
  23.9 0.0 collective-permute-done.3.refs_3_
  23.9 0.0 copy-start.4
  23.9 0.0 collective-permute-done.4.refs_5_
  23.9 0.0 copy-start.5
  23.9 0.9 %shard_map.83 = bf16[32,16,128]{2,1,0:T(8,128)(2,1)} custom-call(bf16[512,512]{1,0:T(8,128)(2,1)S(1)} %fusion.pick_ref, bf16[32,16,128]{2,1,0:T(8,128)(2,1)S(1)} %all-to-all-done.piece_ref), custom_call_target="tpu_custom_call" | custom-call | tf_op jit(solution)/shard_map/pallas_call | solution.py:75
  24.9 5.7 %all-to-all-start.1 = ((bf16[32,16,128]{2,1,0:T(8,128)(2,1)}), bf16[32,16,128]{2,1,0:T(8,128)(2,1)S(1)}, u32[]{:S(2)}, u32[]{:S(2)}) async-start(bf16[32,16,128]{2,1,0:T(8,128)(2,1)} %shard_map.83), calls=%async_computation.1 | async-start | bytes 262144 | tf_op jit(solution)/shard_map/all_to_all | solution.py:397
  30.6 0.0 collective-permute-done.5.near_ref
  30.6 0.1 collective-permute-start.6
  30.7 0.1 fusion.1
  30.8 0.0 copy-done.1
  30.8 0.0 copy-done.2
  30.8 0.0 copy-done.4
  30.8 0.0 copy-done.5
  30.9 0.1 pad_maximum_fusion
  30.9 4.5 %shard_map.82 = (f32[256,640]{1,0:T(8,128)S(1)}, bf16[2,640,640]{2,1,0:T(8,128)(2,1)S(1)}) custom-call(bf16[256,640]{1,0:T(8,128)(2,1)} %bitcast.8, bf16[256,640]{1,0:T(8,128)(2,1)} %copy-done.3, bf16[256,640]{1,0:T(8,128)(2,1)} %copy-done.1, bf16[256,640]{1,0:T(8,128)(2,1)} %copy-done.4, bf16[256,640]{1,0:T(8,128)(2,1)} %copy-done.2, ...), custom_call_target="tpu_custom_call" | custom-call | flops 1258291200 | bytes 6553600 | tf_op jit(solution)/shard_map/pallas_call | solution.py:158
  35.5 4.0 %all-to-all-done.1.cache_ref = bf16[32,16,128]{2,1,0:T(8,128)(2,1)S(1)} async-done(((bf16[32,16,128]{2,1,0:T(8,128)(2,1)}), bf16[32,16,128]{2,1,0:T(8,128)(2,1)S(1)}, u32[]{:S(2)}, u32[]{:S(2)}) %all-to-all-start.1) | async-done | bytes 131104 | tf_op jit(solution)/shard_map/all_to_all | solution.py:397
  39.5 0.0 collective-permute-done.6.far_ref
  39.5 1.5 %shard_map.84.near_ref.after_ref = bf16[256,384]{1,0:T(8,128)(2,1)S(1)} custom-call(f32[256,640]{1,0:T(8,128)S(1)} %get-tuple-element.36.acc_ref, bf16[256,640]{1,0:T(8,128)(2,1)S(1)} %collective-permute-done.5.near_ref, bf16[256,640]{1,0:T(8,128)(2,1)S(1)} %collective-permute-done.6.far_ref, bf16[2,640,640]{2,1,0:T(8,128)(2,1)S(1)} %get-tuple-element.38.weight_ref, ...), custom_call_target="tpu_custom_call" | custom-call | flops 201326592 | bytes 393216 | tf_op jit(solution)/shard_map/pallas_call | solution.py:229
  41.0 0.1 collective-permute-start.7
  41.1 0.0 collective-permute-done.8.far_hbm
  41.1 1.2 %shard_map.87.wo_ref = bf16[1,768,640]{2,1,0:T(8,128)(2,1)S(1)} custom-call(bf16[256,384]{1,0:T(8,128)(2,1)S(1)} %shard_map.84.near_ref.after_ref, bf16[384,5120]{1,0:T(8,128)(2,1)} %near_hbm.5, bf16[384,5120]{1,0:T(8,128)(2,1)} %collective-permute-done.8.far_hbm), custom_call_target="tpu_custom_call" | custom-call | bytes 1966080 | tf_op jit(solution)/shard_map/pallas_call | solution.py:254
  42.3 0.2 collective-permute-done.7.far_ref
  42.5 0.5 shard_map.88
  43.0 1.5 %collective-permute-start.10 = (bf16[128,640]{1,0:T(8,128)(2,1)S(1)}, bf16[128,640]{1,0:T(8,128)(2,1)S(1)}, u32[]{:S(2)}, u32[]{:S(2)}) collective-permute-start(bf16[128,640]{1,0:T(8,128)(2,1)S(1)} %get-tuple-element.46), channel_id=1, source_target_pairs={{0,6},{1,7},{2,0},{3,1},{4,2},{5,3},{6,4},{7,5},{8,14},{9,15},{10,... | collective-permute-start | bytes 491528 | tf_op jit(solution)/shard_map/ppermute | solution.py:413
  44.5 0.6 collective-permute-start.9
  45.1 2.3 %shard_map.86 = (f32[256,640]{1,0:T(8,128)S(1)}, f32[256,640]{1,0:T(8,128)S(1)}) custom-call(bf16[256,384]{1,0:T(8,128)(2,1)S(1)} %shard_map.84.near_ref.after_ref, bf16[256,384]{1,0:T(8,128)(2,1)S(1)} %collective-permute-done.7.far_ref, bf16[384,5120]{1,0:T(8,128)(2,1)} %near_hbm.5, bf16[384,5120]{1,0:T(8,128)(2,1)} %collective-permute-done.8.far_hbm), custom_call_target="tpu_custom_call" | custom-call | flops 503316480 | bytes 1966080 | tf_op jit(solution)/shard_map/pallas_call | solution.py:315
  47.4 2.1 %collective-permute-done.10.bottom_ref = bf16[128,640]{1,0:T(8,128)(2,1)S(1)} collective-permute-done((bf16[128,640]{1,0:T(8,128)(2,1)S(1)}, bf16[128,640]{1,0:T(8,128)(2,1)S(1)}, u32[]{:S(2)}, u32[]{:S(2)}) %collective-permute-start.10) | collective-permute-done | bytes 163872 | tf_op jit(solution)/shard_map/ppermute | solution.py:413
  49.5 2.3 %collective-permute-done.9.top_ref = bf16[128,640]{1,0:T(8,128)(2,1)S(1)} collective-permute-done((bf16[128,640]{1,0:T(8,128)(2,1)S(1)}, bf16[128,640]{1,0:T(8,128)(2,1)S(1)}, u32[]{:S(2)}, u32[]{:S(2)}) %collective-permute-start.9) | collective-permute-done | bytes 163872 | tf_op jit(solution)/shard_map/ppermute | solution.py:412
  51.8 0.1 shard_map.89
  51.9 0.1 collective-permute-start.11
  52.0 3.2 %collective-permute-start.12 = (bf16[256,640]{1,0:T(8,128)(2,1)S(1)}, bf16[256,640]{1,0:T(8,128)(2,1)S(1)}, u32[]{:S(2)}, u32[]{:S(2)}) collective-permute-start(bf16[256,640]{1,0:T(8,128)(2,1)S(1)} %get-tuple-element.48), channel_id=1, source_target_pairs={{0,6},{1,7},{2,0},{3,1},{4,2},{5,3},{6,4},{7,5},{8,14},{9,15},{10,... | collective-permute-start | bytes 983048 | tf_op jit(solution)/shard_map/ppermute | solution.py:419
  55.2 0.8 dynamic_slice.7
  56.0 0.0 copy-done
  56.0 0.1 dynamic-slice_bitcast_fusion
  56.0 0.1 select_reduce_fusion
  56.1 1.7 %shard_map.85.mine_ref = f32[256,640]{1,0:T(8,128)S(1)} custom-call(bf16[256,384]{1,0:T(8,128)(2,1)S(1)} %shard_map.84.near_ref.after_ref, bf16[256,384]{1,0:T(8,128)(2,1)S(1)} %collective-permute-done.7.far_ref, bf16[384,5120]{1,0:T(8,128)(2,1)} %near_hbm.5, bf16[384,5120]{1,0:T(8,128)(2,1)} %collective-permute-done.8.far_hbm), custom_call_target="tpu_custom_call" | custom-call | flops 251658240 | bytes 983040 | tf_op jit(solution)/shard_map/pallas_call | solution.py:315
  57.8 4.1 %collective-permute-done.11.refs_0_ = bf16[256,640]{1,0:T(8,128)(2,1)S(1)} collective-permute-done((bf16[256,640]{1,0:T(8,128)(2,1)S(1)}, bf16[256,640]{1,0:T(8,128)(2,1)S(1)}, u32[]{:S(2)}, u32[]{:S(2)}) %collective-permute-start.11) | collective-permute-done | bytes 327712 | tf_op jit(solution)/shard_map/ppermute | solution.py:418
  62.0 0.0 collective-permute-done.12.refs_1_
  62.0 0.1 broadcast_in_dim.23.pick_ref
  62.0 0.1 broadcast_in_dim.43.count_ref
  62.1 0.4 shard_map.90
  62.5 23.7 %all_to_all.15 = bf16[32,16,640]{2,1,0:T(8,128)(2,1)S(1)} all-to-all(bf16[32,16,640]{2,1,0:T(8,128)(2,1)S(1)} %shard_map.90), channel_id=1, replica_groups=mesh['seq'=32,'tp'=8] {'seq'}, dimensions={0} | all-to-all | bytes 1310720 | tf_op jit(solution)/shard_map/all_to_all | solution.py:422
  86.3 0.8 copy.10
  (2 shorter events, 0.0 us)
Async XLA Ops:
  0.0 56.0 %copy-start = (s32[512,1]{0,1:T(1,128)S(1)}, s32[512,1]{0,1:T(1,128)}, u32[]{:S(2)}) copy-start(s32[512,1]{0,1:T(1,128)} %param.10) | copy-start | bytes 6148
  0.0 41.1 %collective-permute-start.8 = (bf16[384,5120]{1,0:T(8,128)(2,1)}, bf16[384,5120]{1,0:T(8,128)(2,1)}, u32[]{:S(2)}, u32[]{:S(2)}) collective-permute-start(bf16[384,5120]{1,0:T(8,128)(2,1)} %near_hbm.5), channel_id=1, source_target_pairs={{0,1},{1,0},{2,3},{3,2},{4,5},{5,4},{6,7},{7,6},{8,9},{9,8},{10,11... | collective-permute-start | bytes 11796488 | tf_op jit(solution)/shard_map/ppermute | solution.py:387
  0.0 15.6 %collective-permute-start = (bf16[256,640]{1,0:T(8,128)(2,1)}, bf16[256,640]{1,0:T(8,128)(2,1)S(1)}, u32[]{:S(2)}, u32[]{:S(2)}) collective-permute-start(bf16[256,640]{1,0:T(8,128)(2,1)} %bitcast.4), channel_id=1, source_target_pairs={{0,2},{1,3},{2,4},{3,5},{4,6},{5,7},{6,0},{7,1},{8,10},{9,11},{10,... | collective-permute-start | bytes 983048 | tf_op jit(solution)/shard_map/ppermute | solution.py:388
  1.7 13.9 %collective-permute-start.1 = (bf16[256,640]{1,0:T(8,128)(2,1)}, bf16[256,640]{1,0:T(8,128)(2,1)S(1)}, u32[]{:S(2)}, u32[]{:S(2)}) collective-permute-start(bf16[256,640]{1,0:T(8,128)(2,1)} %bitcast.5), channel_id=1, source_target_pairs={{0,6},{1,7},{2,0},{3,1},{4,2},{5,3},{6,4},{7,5},{8,14},{9,15},{10,... | collective-permute-start | bytes 983048 | tf_op jit(solution)/shard_map/ppermute | solution.py:389
  3.3 20.6 %all-to-all-start = ((bf16[32,16,128]{2,1,0:T(8,128)(2,1)}), bf16[32,16,128]{2,1,0:T(8,128)(2,1)S(1)}, u32[]{:S(2)}, u32[]{:S(2)}) async-start(bf16[32,16,128]{2,1,0:T(8,128)(2,1)} %bitcast.9), calls=%async_computation | async-start | bytes 262144 | tf_op jit(solution)/shard_map/all_to_all | solution.py:384
  15.6 15.2 %copy-start.1 = (bf16[256,640]{1,0:T(8,128)(2,1)}, bf16[256,640]{1,0:T(8,128)(2,1)S(1)}, u32[]{:S(2)}) copy-start(bf16[256,640]{1,0:T(8,128)(2,1)S(1)} %collective-permute-done.refs_2_) | copy-start | bytes 983044
  15.6 15.2 %copy-start.2 = (bf16[256,640]{1,0:T(8,128)(2,1)}, bf16[256,640]{1,0:T(8,128)(2,1)S(1)}, u32[]{:S(2)}) copy-start(bf16[256,640]{1,0:T(8,128)(2,1)S(1)} %collective-permute-done.1.refs_4_) | copy-start | bytes 983044
  15.6 1.9 %collective-permute-start.2 = (bf16[256,640]{1,0:T(8,128)(2,1)}, bf16[256,640]{1,0:T(8,128)(2,1)S(1)}, u32[]{:S(2)}, u32[]{:S(2)}) collective-permute-start(bf16[256,640]{1,0:T(8,128)(2,1)} %bitcast.6), channel_id=1, source_target_pairs={{0,1},{1,0},{2,3},{3,2},{4,5},{5,4},{6,7},{7,6},{8,9},{9,8},{10,11... | collective-permute-start | bytes 983048 | tf_op jit(solution)/shard_map/ppermute | solution.py:387
  15.8 8.1 %collective-permute-start.3 = (bf16[256,640]{1,0:T(8,128)(2,1)S(1)}, bf16[256,640]{1,0:T(8,128)(2,1)S(1)}, u32[]{:S(2)}, u32[]{:S(2)}) collective-permute-start(bf16[256,640]{1,0:T(8,128)(2,1)S(1)} %collective-permute-done.refs_2_), channel_id=1, source_target_pairs={{0,1},{1,0},{2,3},{3,2},{4,5},{5,4},{6,7},{7,6},{8,9},{9,8},{10,11... | collective-permute-start | bytes 983048 | tf_op jit(solution)/shard_map/ppermute | solution.py:387
  16.3 7.6 %collective-permute-start.4 = (bf16[256,640]{1,0:T(8,128)(2,1)S(1)}, bf16[256,640]{1,0:T(8,128)(2,1)S(1)}, u32[]{:S(2)}, u32[]{:S(2)}) collective-permute-start(bf16[256,640]{1,0:T(8,128)(2,1)S(1)} %collective-permute-done.1.refs_4_), channel_id=1, source_target_pairs={{0,1},{1,0},{2,3},{3,2},{4,5},{5,4},{6,7},{7,6},{8,9},{9,8},{10,11... | collective-permute-start | bytes 983048 | tf_op jit(solution)/shard_map/ppermute | solution.py:387
  17.6 2.0 %copy-start.3 = (bf16[256,640]{1,0:T(8,128)(2,1)}, bf16[256,640]{1,0:T(8,128)(2,1)S(1)}, u32[]{:S(2)}) copy-start(bf16[256,640]{1,0:T(8,128)(2,1)S(1)} %collective-permute-done.2.refs_1_) | copy-start | bytes 983044
  17.6 13.0 %collective-permute-start.5 = (bf16[256,640]{1,0:T(8,128)(2,1)}, bf16[256,640]{1,0:T(8,128)(2,1)S(1)}, u32[]{:S(2)}, u32[]{:S(2)}) collective-permute-start(bf16[256,640]{1,0:T(8,128)(2,1)} %bitcast.7), channel_id=1, source_target_pairs={{0,4},{1,5},{2,6},{3,7},{4,0},{5,1},{6,2},{7,3},{8,12},{9,13},{10,... | collective-permute-start | bytes 983048 | tf_op jit(solution)/shard_map/ppermute | solution.py:393
  23.9 6.9 %copy-start.4 = (bf16[256,640]{1,0:T(8,128)(2,1)}, bf16[256,640]{1,0:T(8,128)(2,1)S(1)}, u32[]{:S(2)}) copy-start(bf16[256,640]{1,0:T(8,128)(2,1)S(1)} %collective-permute-done.3.refs_3_) | copy-start | bytes 983044
  23.9 6.9 %copy-start.5 = (bf16[256,640]{1,0:T(8,128)(2,1)}, bf16[256,640]{1,0:T(8,128)(2,1)S(1)}, u32[]{:S(2)}) copy-start(bf16[256,640]{1,0:T(8,128)(2,1)S(1)} %collective-permute-done.4.refs_5_) | copy-start | bytes 983044
  24.9 14.6 %all-to-all-start.1 = ((bf16[32,16,128]{2,1,0:T(8,128)(2,1)}), bf16[32,16,128]{2,1,0:T(8,128)(2,1)S(1)}, u32[]{:S(2)}, u32[]{:S(2)}) async-start(bf16[32,16,128]{2,1,0:T(8,128)(2,1)} %shard_map.83), calls=%async_computation.1 | async-start | bytes 262144 | tf_op jit(solution)/shard_map/all_to_all | solution.py:397
  30.6 8.9 %collective-permute-start.6 = (bf16[256,640]{1,0:T(8,128)(2,1)S(1)}, bf16[256,640]{1,0:T(8,128)(2,1)S(1)}, u32[]{:S(2)}, u32[]{:S(2)}) collective-permute-start(bf16[256,640]{1,0:T(8,128)(2,1)S(1)} %collective-permute-done.5.near_ref), channel_id=1, source_target_pairs={{0,1},{1,0},{2,3},{3,2},{4,5},{5,4},{6,7},{7,6},{8,9},{9,8},{10,11... | collective-permute-start | bytes 983048 | tf_op jit(solution)/shard_map/ppermute | solution.py:387
  41.0 1.5 %collective-permute-start.7 = (bf16[256,384]{1,0:T(8,128)(2,1)S(1)}, bf16[256,384]{1,0:T(8,128)(2,1)S(1)}, u32[]{:S(2)}, u32[]{:S(2)}) collective-permute-start(bf16[256,384]{1,0:T(8,128)(2,1)S(1)} %shard_map.84.near_ref.after_ref), channel_id=1, source_target_pairs={{0,1},{1,0},{2,3},{3,2},{4,5},{5,4},{6,7},{7,6},{8,9},{9,8},{10,11... | collective-permute-start | bytes 589832 | tf_op jit(solution)/shard_map/ppermute | solution.py:387
  43.0 6.5 %collective-permute-start.10 = (bf16[128,640]{1,0:T(8,128)(2,1)S(1)}, bf16[128,640]{1,0:T(8,128)(2,1)S(1)}, u32[]{:S(2)}, u32[]{:S(2)}) collective-permute-start(bf16[128,640]{1,0:T(8,128)(2,1)S(1)} %get-tuple-element.46), channel_id=1, source_target_pairs={{0,6},{1,7},{2,0},{3,1},{4,2},{5,3},{6,4},{7,5},{8,14},{9,15},{10,... | collective-permute-start | bytes 491528 | tf_op jit(solution)/shard_map/ppermute | solution.py:413
  44.5 7.3 %collective-permute-start.9 = (bf16[128,640]{1,0:T(8,128)(2,1)S(1)}, bf16[128,640]{1,0:T(8,128)(2,1)S(1)}, u32[]{:S(2)}, u32[]{:S(2)}) collective-permute-start(bf16[128,640]{1,0:T(8,128)(2,1)S(1)} %get-tuple-element.45), channel_id=1, source_target_pairs={{0,2},{1,3},{2,4},{3,5},{4,6},{5,7},{6,0},{7,1},{8,10},{9,11},{10,... | collective-permute-start | bytes 491528 | tf_op jit(solution)/shard_map/ppermute | solution.py:412
  51.9 10.1 %collective-permute-start.11 = (bf16[256,640]{1,0:T(8,128)(2,1)S(1)}, bf16[256,640]{1,0:T(8,128)(2,1)S(1)}, u32[]{:S(2)}, u32[]{:S(2)}) collective-permute-start(bf16[256,640]{1,0:T(8,128)(2,1)S(1)} %get-tuple-element.47), channel_id=1, source_target_pairs={{0,2},{1,3},{2,4},{3,5},{4,6},{5,7},{6,0},{7,1},{8,10},{9,11},{10,... | collective-permute-start | bytes 983048 | tf_op jit(solution)/shard_map/ppermute | solution.py:418
  52.0 10.0 %collective-permute-start.12 = (bf16[256,640]{1,0:T(8,128)(2,1)S(1)}, bf16[256,640]{1,0:T(8,128)(2,1)S(1)}, u32[]{:S(2)}, u32[]{:S(2)}) collective-permute-start(bf16[256,640]{1,0:T(8,128)(2,1)S(1)} %get-tuple-element.48), channel_id=1, source_target_pairs={{0,6},{1,7},{2,0},{3,1},{4,2},{5,3},{6,4},{7,5},{8,14},{9,15},{10,... | collective-permute-start | bytes 983048 | tf_op jit(solution)/shard_map/ppermute | solution.py:419

commit v6 on v5

--- a/solution.py
+++ b/solution.py
@@ -66,17 +66,22 @@
 
 def route_kernel(pick_ref, piece_ref, out_ref):
     count, size, width = piece_ref.shape
-    pieces = piece_ref[...].reshape(count * size, width)
-    picked = jnp.dot(pick_ref[...], pieces, preferred_element_type=jnp.float32)
-    out_ref[...] = picked.astype(jnp.bfloat16).reshape(count, size, width)
-
-
-def route(pick, pieces):
+    slots = out_ref.shape[0]
+    part = pick_ref.shape[0] // slots
+    for i in range(size // part):
+        at = slice(i * part, (i + 1) * part)
+        pieces = piece_ref[:, at, :].reshape(count * part, width)
+        picked = jnp.dot(pick_ref[...], pieces, preferred_element_type=jnp.float32)
+        out_ref[:, at, :] = picked.astype(jnp.bfloat16).reshape(slots, part, width)
+
+
+def route(pick, pieces, slots):
+    _, size, width = pieces.shape
     return pl.pallas_call(
         route_kernel,
         in_specs=[VMEM, VMEM],
         out_specs=VMEM,
-        out_shape=jax.ShapeDtypeStruct(pieces.shape, pieces.dtype),
+        out_shape=jax.ShapeDtypeStruct((slots, size, width), pieces.dtype),
         compiler_params=params(8),
     )(pick, pieces)
 
@@ -197,10 +202,12 @@
         return (v.reshape(-1, tokens, HD) * cosine + turned).astype(jnp.bfloat16).reshape(rows, HD)
 
     scale = 1.0 / math.sqrt(HD)
-    half = cache_ref.shape[0] // 2
+    near = cache_ref.shape[0] // 2
+    cache = cache_ref[:near] + cache_ref[near:]
+    half = near // 2
     own_values = both[:, (heads + 1) * HD :].astype(jnp.bfloat16)
-    keys = jnp.concatenate([cache_ref[:half].reshape(PL, HD), rotated(heads)], 0)
-    values = jnp.concatenate([cache_ref[half:].reshape(PL, HD), own_values], 0)
+    keys = jnp.concatenate([cache[:half].reshape(PL, HD), rotated(heads)], 0)
+    values = jnp.concatenate([cache[half:].reshape(PL, HD), own_values], 0)
     row = lax.broadcasted_iota(jnp.int32, (rows, rows), 0)
     col = lax.broadcasted_iota(jnp.int32, (rows, rows), 1)
     seen = (row // tokens == col // tokens) & (col <= row)
@@ -377,24 +384,28 @@
     group_size, tokens, width = resp_rows.shape
     rows = group_size * tokens
 
-    pieces = prompt_kv.reshape(learners, -1, HD)
-    size = pieces.shape[1]
-    source = group_prompt[:, None] * size + jnp.arange(size)[None, :]
-    prompts = (source.reshape(-1)[:, None] == jnp.arange(learners * size)[None, :]).astype(jnp.bfloat16)
-    pieces = lax.all_to_all(pieces, "seq", 0, 0, tiled=True)
+    near = learners // 2
+    halves = [list(range(near)), list(range(near, learners))]
+    pieces = prompt_kv.reshape(near, -1, HD)
+    part = 16
+    source = group_prompt - group // near * near
+    held = (source >= 0) & (source < near)
+    source = jnp.where(held, source, -near)[:, None] * part + jnp.arange(part)[None, :]
+    prompts = source.reshape(-1)[:, None] == jnp.arange(near * part)[None, :]
+    prompts = prompts.astype(jnp.bfloat16)
+    pieces = lax.all_to_all(pieces, "seq", 0, 0, axis_index_groups=halves, tiled=True)
 
     x = resp_rows.reshape(rows, width)
     swap = lambda v: lax.ppermute(v, "tp", CORE_SWAP)
     below = lax.ppermute(x, "tp", chip_shift(1))
     above = lax.ppermute(x, "tp", chip_shift(-1))
-    x_again, below, above = lax.optimization_barrier((x, below, above))
-    x_far = swap(x_again)
-    x_last, x_far = lax.optimization_barrier((x, x_far))
+    x_far = swap(x)
+    x_last, below, above = lax.optimization_barrier((x, below, above))
     across = lax.ppermute(x_last, "tp", chip_shift(2))
     out_far = swap(w_out)
     shards = [x_far, below, swap(below), above, swap(above)]
     pieces, *shards = lax.optimization_barrier((pieces, *shards))
-    cache = lax.all_to_all(route(prompts, pieces), "seq", 0, 0, tiled=True)
+    cache = lax.all_to_all(route(prompts, pieces, learners), "seq", 0, 0, tiled=True)
 
     cosine, sine = rope_tables(tokens)
     acc, w_last = project(x, shards, w_query, w_keyval)

time: 87.7 us -> 87.4 us (level)
  starting transfers between devices: 28.9 us -> 28 us
  waiting for transfers between devices: 18 us -> 18.9 us
    all_to_all x2, waiting for transfers between devices: 8.09 us -> 9.79 us  [the longest x1 5.5 us: per_device(): lax.all_to_all(route(prompts, pieces, learners), 'seq', 0, 0, tiled=True)]
    ppermute x6, waiting for transfers between devices: 1.33 us -> 0.2 us  [per_device(): swap = lambda v: lax.ppermute(v, 'tp', CORE_SWAP)]
  transfers between devices with their start and end apart: 15 -> 15, of which waited for: 7 -> 6; matrix products, arithmetic and copies ran while one was open for 2% -> 2% of each run, Pallas kernels for 14% -> 14%
where the time goes in v6:
time: 87.4 us; the launch traced here: 86.8 us
  starting transfers between devices  28 us (32%)
  blocking collectives  23.4 us (27%)
  waiting for transfers between devices  18.9 us (22%)
  Pallas kernels  13.2 us (15%)
  local copies, waits for them, and re-layouts  1.9 us (2%)
  other arithmetic  1.16 us (1%)
    all_to_all x1, blocking collectives, per_device(): return lax.all_to_all(slots, 'seq', 0, 0, tiled=True)  23.4 us
    all_to_all x1, starting transfers between devices, per_device(): lax.all_to_all(pieces, 'seq', 0, 0, axis_index_groups=halves, tiled=True)  8.91 us
    all_to_all x1, starting transfers between devices, per_device(): lax.all_to_all(route(prompts, pieces, learners), 'seq', 0, 0, tiled=True)  7.56 us
    all_to_all x1, waiting for transfers between devices, per_device(): lax.all_to_all(route(prompts, pieces, learners), 'seq', 0, 0, tiled=True)  5.5 us
    pallas_call x1, Pallas kernels, project(): pl.pallas_call(project_kernel, in_specs=[ANY] * 8, out_specs=[VMEM] * 2,...  4.51 us
    all_to_all x1, waiting for transfers between devices, per_device(): lax.all_to_all(pieces, 'seq', 0, 0, axis_index_groups=halves, tiled=True)  4.29 us
    ppermute x1, waiting for transfers between devices, per_device(): lax.ppermute(to_above, 'tp', chip_shift(1))  4.11 us
    pallas_call x2, Pallas kernels, output(): pl.pallas_call(functools.partial(output_kernel, shifts), in_specs=[VMEM]...  3.95 us
  transfers between devices with their start and end apart: 15, of which 6 were waited for; matrix products, arithmetic and copies ran while one was open for 2% of the time, Pallas kernels for 14%

profile of v6, /device:TPU:2, one launch (start us, length us, event | category | flops | bytes accessed | tf_op | source)
XLA Modules:
  0.0 86.8 jit_solution(3880874510488489093)
XLA Ops:
  0.0 0.0 copy-start
  0.0 0.0 collective-permute-start.8
  0.0 1.7 %collective-permute-start.1 = (bf16[256,640]{1,0:T(8,128)(2,1)}, bf16[256,640]{1,0:T(8,128)(2,1)S(1)}, u32[]{:S(2)}, u32[]{:S(2)}) collective-permute-start(bf16[256,640]{1,0:T(8,128)(2,1)} %bitcast.4), channel_id=1, source_target_pairs={{0,2},{1,3},{2,4},{3,5},{4,6},{5,7},{6,0},{7,1},{8,10},{9,11},{10,... | collective-permute-start | bytes 983048 | tf_op jit(solution)/shard_map/ppermute | solution.py:400
  1.7 1.7 %collective-permute-start.2 = (bf16[256,640]{1,0:T(8,128)(2,1)}, bf16[256,640]{1,0:T(8,128)(2,1)S(1)}, u32[]{:S(2)}, u32[]{:S(2)}) collective-permute-start(bf16[256,640]{1,0:T(8,128)(2,1)} %bitcast.5), channel_id=1, source_target_pairs={{0,6},{1,7},{2,0},{3,1},{4,2},{5,3},{6,4},{7,5},{8,14},{9,15},{10,... | collective-permute-start | bytes 983048 | tf_op jit(solution)/shard_map/ppermute | solution.py:401
  3.3 0.0 collective-permute-start
  3.3 8.9 %all-to-all-start = ((bf16[16,32,128]{2,1,0:T(8,128)(2,1)}), bf16[16,32,128]{2,1,0:T(8,128)(2,1)S(1)}, u32[]{:S(2)}, u32[]{:S(2)}) async-start(bf16[16,32,128]{2,1,0:T(8,128)(2,1)} %bitcast.9), calls=%async_computation | async-start | bytes 262144 | tf_op jit(solution)/shard_map/all_to_all | solution.py:396
  12.2 0.7 fusion.2
  12.9 0.1 iota_add_fusion
  13.0 0.0 collective-permute-done.1.refs_2_
  13.0 0.0 copy-start.1
  13.0 0.0 collective-permute-done.2.refs_4_
  13.0 0.0 copy-start.2
  13.0 0.1 collective-permute-start.3
  13.1 0.5 collective-permute-start.4
  13.6 0.1 add.44
  13.7 2.0 %collective-permute-start.5 = (bf16[256,640]{1,0:T(8,128)(2,1)}, bf16[256,640]{1,0:T(8,128)(2,1)S(1)}, u32[]{:S(2)}, u32[]{:S(2)}) collective-permute-start(bf16[256,640]{1,0:T(8,128)(2,1)} %bitcast.7), channel_id=1, source_target_pairs={{0,4},{1,5},{2,6},{3,7},{4,0},{5,1},{6,2},{7,3},{8,12},{9,13},{10,... | collective-permute-start | bytes 983048 | tf_op jit(solution)/shard_map/ppermute | solution.py:404
  15.7 0.1 fusion.pick_ref
  15.8 4.3 %all-to-all-done.piece_ref = bf16[16,32,128]{2,1,0:T(8,128)(2,1)S(1)} async-done(((bf16[16,32,128]{2,1,0:T(8,128)(2,1)}), bf16[16,32,128]{2,1,0:T(8,128)(2,1)S(1)}, u32[]{:S(2)}, u32[]{:S(2)}) %all-to-all-start) | async-done | bytes 131104 | tf_op jit(solution)/shard_map/all_to_all | solution.py:396
  20.1 0.0 collective-permute-done.refs_1_
  20.1 0.0 copy-start.3
  20.1 0.0 collective-permute-done.3.refs_3_
  20.1 0.0 copy-start.4
  20.1 0.0 collective-permute-done.4.refs_5_
  20.1 0.0 copy-start.5
  20.2 1.0 %shard_map.83 = bf16[32,32,128]{2,1,0:T(8,128)(2,1)} custom-call(bf16[512,256]{1,0:T(8,128)(2,1)S(1)} %fusion.pick_ref, bf16[16,32,128]{2,1,0:T(8,128)(2,1)S(1)} %all-to-all-done.piece_ref), custom_call_target="tpu_custom_call" | custom-call | tf_op jit(solution)/shard_map/pallas_call | solution.py:80
  21.2 0.0 copy-done.5
  21.2 7.6 %all-to-all-start.1 = ((bf16[32,32,128]{2,1,0:T(8,128)(2,1)}), bf16[32,32,128]{2,1,0:T(8,128)(2,1)S(1)}, u32[]{:S(2)}, u32[]{:S(2)}) async-start(bf16[32,32,128]{2,1,0:T(8,128)(2,1)} %shard_map.83), calls=%async_computation.1 | async-start | bytes 524288 | tf_op jit(solution)/shard_map/all_to_all | solution.py:408
  28.7 0.0 collective-permute-done.5.near_ref
  28.7 0.1 collective-permute-start.6
  28.8 0.1 fusion.1
  29.0 0.0 copy-done.1
  29.0 0.0 copy-done.2
  29.0 0.0 copy-done.3
  29.0 0.0 copy-done.4
  29.0 0.1 pad_maximum_fusion
  29.1 4.5 %shard_map.82 = (f32[256,640]{1,0:T(8,128)S(1)}, bf16[2,640,640]{2,1,0:T(8,128)(2,1)S(1)}) custom-call(bf16[256,640]{1,0:T(8,128)(2,1)} %bitcast.8, bf16[256,640]{1,0:T(8,128)(2,1)} %copy-done.3, bf16[256,640]{1,0:T(8,128)(2,1)} %copy-done.1, bf16[256,640]{1,0:T(8,128)(2,1)} %copy-done.4, bf16[256,640]{1,0:T(8,128)(2,1)} %copy-done.2, ...), custom_call_target="tpu_custom_call" | custom-call | flops 1258291200 | bytes 6553600 | tf_op jit(solution)/shard_map/pallas_call | solution.py:163
  33.6 0.0 collective-permute-done.6.far_ref
  33.6 5.5 %all-to-all-done.1.cache_ref = bf16[32,32,128]{2,1,0:T(8,128)(2,1)S(1)} async-done(((bf16[32,32,128]{2,1,0:T(8,128)(2,1)}), bf16[32,32,128]{2,1,0:T(8,128)(2,1)S(1)}, u32[]{:S(2)}, u32[]{:S(2)}) %all-to-all-start.1) | async-done | bytes 262176 | tf_op jit(solution)/shard_map/all_to_all | solution.py:408
  39.1 1.5 %shard_map.84.near_ref.after_ref = bf16[256,384]{1,0:T(8,128)(2,1)S(1)} custom-call(f32[256,640]{1,0:T(8,128)S(1)} %get-tuple-element.32.acc_ref, bf16[256,640]{1,0:T(8,128)(2,1)S(1)} %collective-permute-done.5.near_ref, bf16[256,640]{1,0:T(8,128)(2,1)S(1)} %collective-permute-done.6.far_ref, bf16[2,640,640]{2,1,0:T(8,128)(2,1)S(1)} %get-tuple-element.34.weight_ref, ...), custom_call_target="tpu_custom_call" | custom-call | flops 201326592 | bytes 393216 | tf_op jit(solution)/shard_map/pallas_call | solution.py:236
  40.6 0.1 collective-permute-start.7
  40.7 0.0 collective-permute-done.8.far_hbm
  40.7 1.2 %shard_map.87.wo_ref = bf16[1,768,640]{2,1,0:T(8,128)(2,1)S(1)} custom-call(bf16[256,384]{1,0:T(8,128)(2,1)S(1)} %shard_map.84.near_ref.after_ref, bf16[384,5120]{1,0:T(8,128)(2,1)} %near_hbm.5, bf16[384,5120]{1,0:T(8,128)(2,1)} %collective-permute-done.8.far_hbm), custom_call_target="tpu_custom_call" | custom-call | bytes 1966080 | tf_op jit(solution)/shard_map/pallas_call | solution.py:261
  42.0 0.2 collective-permute-done.7.far_ref
  42.1 0.5 shard_map.88
  42.6 1.8 %collective-permute-start.10 = (bf16[128,640]{1,0:T(8,128)(2,1)S(1)}, bf16[128,640]{1,0:T(8,128)(2,1)S(1)}, u32[]{:S(2)}, u32[]{:S(2)}) collective-permute-start(bf16[128,640]{1,0:T(8,128)(2,1)S(1)} %get-tuple-element.42), channel_id=1, source_target_pairs={{0,6},{1,7},{2,0},{3,1},{4,2},{5,3},{6,4},{7,5},{8,14},{9,15},{10,... | collective-permute-start | bytes 491528 | tf_op jit(solution)/shard_map/ppermute | solution.py:424
  44.4 0.3 collective-permute-start.9
  44.7 2.3 %shard_map.86 = (f32[256,640]{1,0:T(8,128)S(1)}, f32[256,640]{1,0:T(8,128)S(1)}) custom-call(bf16[256,384]{1,0:T(8,128)(2,1)S(1)} %shard_map.84.near_ref.after_ref, bf16[256,384]{1,0:T(8,128)(2,1)S(1)} %collective-permute-done.7.far_ref, bf16[384,5120]{1,0:T(8,128)(2,1)} %near_hbm.5, bf16[384,5120]{1,0:T(8,128)(2,1)} %collective-permute-done.8.far_hbm), custom_call_target="tpu_custom_call" | custom-call | flops 503316480 | bytes 1966080 | tf_op jit(solution)/shard_map/pallas_call | solution.py:322
  47.0 2.1 %collective-permute-done.10.bottom_ref = bf16[128,640]{1,0:T(8,128)(2,1)S(1)} collective-permute-done((bf16[128,640]{1,0:T(8,128)(2,1)S(1)}, bf16[128,640]{1,0:T(8,128)(2,1)S(1)}, u32[]{:S(2)}, u32[]{:S(2)}) %collective-permute-start.10) | collective-permute-done | bytes 163872 | tf_op jit(solution)/shard_map/ppermute | solution.py:424
  49.1 2.7 %collective-permute-done.9.top_ref = bf16[128,640]{1,0:T(8,128)(2,1)S(1)} collective-permute-done((bf16[128,640]{1,0:T(8,128)(2,1)S(1)}, bf16[128,640]{1,0:T(8,128)(2,1)S(1)}, u32[]{:S(2)}, u32[]{:S(2)}) %collective-permute-start.9) | collective-permute-done | bytes 163872 | tf_op jit(solution)/shard_map/ppermute | solution.py:423
  51.8 0.1 shard_map.89
  51.9 0.1 collective-permute-start.11
  52.0 3.2 %collective-permute-start.12 = (bf16[256,640]{1,0:T(8,128)(2,1)S(1)}, bf16[256,640]{1,0:T(8,128)(2,1)S(1)}, u32[]{:S(2)}, u32[]{:S(2)}) collective-permute-start(bf16[256,640]{1,0:T(8,128)(2,1)S(1)} %get-tuple-element.44), channel_id=1, source_target_pairs={{0,6},{1,7},{2,0},{3,1},{4,2},{5,3},{6,4},{7,5},{8,14},{9,15},{10,... | collective-permute-start | bytes 983048 | tf_op jit(solution)/shard_map/ppermute | solution.py:430
  55.2 0.8 dynamic_slice.7
  55.9 0.0 copy-done
  55.9 0.1 dynamic-slice_bitcast_fusion
  56.0 0.1 select_reduce_fusion
  56.1 1.7 %shard_map.85.mine_ref = f32[256,640]{1,0:T(8,128)S(1)} custom-call(bf16[256,384]{1,0:T(8,128)(2,1)S(1)} %shard_map.84.near_ref.after_ref, bf16[256,384]{1,0:T(8,128)(2,1)S(1)} %collective-permute-done.7.far_ref, bf16[384,5120]{1,0:T(8,128)(2,1)} %near_hbm.5, bf16[384,5120]{1,0:T(8,128)(2,1)} %collective-permute-done.8.far_hbm), custom_call_target="tpu_custom_call" | custom-call | flops 251658240 | bytes 983040 | tf_op jit(solution)/shard_map/pallas_call | solution.py:322
  57.8 4.1 %collective-permute-done.11.refs_0_ = bf16[256,640]{1,0:T(8,128)(2,1)S(1)} collective-permute-done((bf16[256,640]{1,0:T(8,128)(2,1)S(1)}, bf16[256,640]{1,0:T(8,128)(2,1)S(1)}, u32[]{:S(2)}, u32[]{:S(2)}) %collective-permute-start.11) | collective-permute-done | bytes 327712 | tf_op jit(solution)/shard_map/ppermute | solution.py:429
  61.9 0.0 collective-permute-done.12.refs_1_
  61.9 0.1 broadcast_in_dim.45.pick_ref
  62.0 0.1 broadcast_in_dim.48.count_ref
  62.1 0.4 shard_map.90
  62.5 23.4 %all_to_all.15 = bf16[32,16,640]{2,1,0:T(8,128)(2,1)S(1)} all-to-all(bf16[32,16,640]{2,1,0:T(8,128)(2,1)S(1)} %shard_map.90), channel_id=1, replica_groups=mesh['seq'=32,'tp'=8] {'seq'}, dimensions={0} | all-to-all | bytes 1310720 | tf_op jit(solution)/shard_map/all_to_all | solution.py:433
  85.9 0.8 copy.10
  (2 shorter events, 0.0 us)
Async XLA Ops:
  0.0 55.9 %copy-start = (s32[512,1]{0,1:T(1,128)S(1)}, s32[512,1]{0,1:T(1,128)}, u32[]{:S(2)}) copy-start(s32[512,1]{0,1:T(1,128)} %param.10) | copy-start | bytes 6148
  0.0 40.7 %collective-permute-start.8 = (bf16[384,5120]{1,0:T(8,128)(2,1)}, bf16[384,5120]{1,0:T(8,128)(2,1)}, u32[]{:S(2)}, u32[]{:S(2)}) collective-permute-start(bf16[384,5120]{1,0:T(8,128)(2,1)} %near_hbm.5), channel_id=1, source_target_pairs={{0,1},{1,0},{2,3},{3,2},{4,5},{5,4},{6,7},{7,6},{8,9},{9,8},{10,11... | collective-permute-start | bytes 11796488 | tf_op jit(solution)/shard_map/ppermute | solution.py:399
  0.0 13.0 %collective-permute-start.1 = (bf16[256,640]{1,0:T(8,128)(2,1)}, bf16[256,640]{1,0:T(8,128)(2,1)S(1)}, u32[]{:S(2)}, u32[]{:S(2)}) collective-permute-start(bf16[256,640]{1,0:T(8,128)(2,1)} %bitcast.4), channel_id=1, source_target_pairs={{0,2},{1,3},{2,4},{3,5},{4,6},{5,7},{6,0},{7,1},{8,10},{9,11},{10,... | collective-permute-start | bytes 983048 | tf_op jit(solution)/shard_map/ppermute | solution.py:400
  1.7 11.3 %collective-permute-start.2 = (bf16[256,640]{1,0:T(8,128)(2,1)}, bf16[256,640]{1,0:T(8,128)(2,1)S(1)}, u32[]{:S(2)}, u32[]{:S(2)}) collective-permute-start(bf16[256,640]{1,0:T(8,128)(2,1)} %bitcast.5), channel_id=1, source_target_pairs={{0,6},{1,7},{2,0},{3,1},{4,2},{5,3},{6,4},{7,5},{8,14},{9,15},{10,... | collective-permute-start | bytes 983048 | tf_op jit(solution)/shard_map/ppermute | solution.py:401
  3.3 16.8 %collective-permute-start = (bf16[256,640]{1,0:T(8,128)(2,1)}, bf16[256,640]{1,0:T(8,128)(2,1)S(1)}, u32[]{:S(2)}, u32[]{:S(2)}) collective-permute-start(bf16[256,640]{1,0:T(8,128)(2,1)} %bitcast.6), channel_id=1, source_target_pairs={{0,1},{1,0},{2,3},{3,2},{4,5},{5,4},{6,7},{7,6},{8,9},{9,8},{10,11... | collective-permute-start | bytes 983048 | tf_op jit(solution)/shard_map/ppermute | solution.py:399
  3.3 16.8 %all-to-all-start = ((bf16[16,32,128]{2,1,0:T(8,128)(2,1)}), bf16[16,32,128]{2,1,0:T(8,128)(2,1)S(1)}, u32[]{:S(2)}, u32[]{:S(2)}) async-start(bf16[16,32,128]{2,1,0:T(8,128)(2,1)} %bitcast.9), calls=%async_computation | async-start | bytes 262144 | tf_op jit(solution)/shard_map/all_to_all | solution.py:396
  13.0 16.0 %copy-start.1 = (bf16[256,640]{1,0:T(8,128)(2,1)}, bf16[256,640]{1,0:T(8,128)(2,1)S(1)}, u32[]{:S(2)}) copy-start(bf16[256,640]{1,0:T(8,128)(2,1)S(1)} %collective-permute-done.1.refs_2_) | copy-start | bytes 983044
  13.0 16.0 %copy-start.2 = (bf16[256,640]{1,0:T(8,128)(2,1)}, bf16[256,640]{1,0:T(8,128)(2,1)S(1)}, u32[]{:S(2)}) copy-start(bf16[256,640]{1,0:T(8,128)(2,1)S(1)} %collective-permute-done.2.refs_4_) | copy-start | bytes 983044
  13.0 7.1 %collective-permute-start.3 = (bf16[256,640]{1,0:T(8,128)(2,1)S(1)}, bf16[256,640]{1,0:T(8,128)(2,1)S(1)}, u32[]{:S(2)}, u32[]{:S(2)}) collective-permute-start(bf16[256,640]{1,0:T(8,128)(2,1)S(1)} %collective-permute-done.1.refs_2_), channel_id=1, source_target_pairs={{0,1},{1,0},{2,3},{3,2},{4,5},{5,4},{6,7},{7,6},{8,9},{9,8},{10,11... | collective-permute-start | bytes 983048 | tf_op jit(solution)/shard_map/ppermute | solution.py:399
  13.1 7.0 %collective-permute-start.4 = (bf16[256,640]{1,0:T(8,128)(2,1)S(1)}, bf16[256,640]{1,0:T(8,128)(2,1)S(1)}, u32[]{:S(2)}, u32[]{:S(2)}) collective-permute-start(bf16[256,640]{1,0:T(8,128)(2,1)S(1)} %collective-permute-done.2.refs_4_), channel_id=1, source_target_pairs={{0,1},{1,0},{2,3},{3,2},{4,5},{5,4},{6,7},{7,6},{8,9},{9,8},{10,11... | collective-permute-start | bytes 983048 | tf_op jit(solution)/shard_map/ppermute | solution.py:399
  13.7 15.1 %collective-permute-start.5 = (bf16[256,640]{1,0:T(8,128)(2,1)}, bf16[256,640]{1,0:T(8,128)(2,1)S(1)}, u32[]{:S(2)}, u32[]{:S(2)}) collective-permute-start(bf16[256,640]{1,0:T(8,128)(2,1)} %bitcast.7), channel_id=1, source_target_pairs={{0,4},{1,5},{2,6},{3,7},{4,0},{5,1},{6,2},{7,3},{8,12},{9,13},{10,... | collective-permute-start | bytes 983048 | tf_op jit(solution)/shard_map/ppermute | solution.py:404
  20.1 8.9 %copy-start.3 = (bf16[256,640]{1,0:T(8,128)(2,1)}, bf16[256,640]{1,0:T(8,128)(2,1)S(1)}, u32[]{:S(2)}) copy-start(bf16[256,640]{1,0:T(8,128)(2,1)S(1)} %collective-permute-done.refs_1_) | copy-start | bytes 983044
  20.1 8.9 %copy-start.4 = (bf16[256,640]{1,0:T(8,128)(2,1)}, bf16[256,640]{1,0:T(8,128)(2,1)S(1)}, u32[]{:S(2)}) copy-start(bf16[256,640]{1,0:T(8,128)(2,1)S(1)} %collective-permute-done.3.refs_3_) | copy-start | bytes 983044
  20.1 1.0 %copy-start.5 = (bf16[256,640]{1,0:T(8,128)(2,1)}, bf16[256,640]{1,0:T(8,128)(2,1)S(1)}, u32[]{:S(2)}) copy-start(bf16[256,640]{1,0:T(8,128)(2,1)S(1)} %collective-permute-done.4.refs_5_) | copy-start | bytes 983044
  21.2 18.0 %all-to-all-start.1 = ((bf16[32,32,128]{2,1,0:T(8,128)(2,1)}), bf16[32,32,128]{2,1,0:T(8,128)(2,1)S(1)}, u32[]{:S(2)}, u32[]{:S(2)}) async-start(bf16[32,32,128]{2,1,0:T(8,128)(2,1)} %shard_map.83), calls=%async_computation.1 | async-start | bytes 524288 | tf_op jit(solution)/shard_map/all_to_all | solution.py:408
  28.7 4.9 %collective-permute-start.6 = (bf16[256,640]{1,0:T(8,128)(2,1)S(1)}, bf16[256,640]{1,0:T(8,128)(2,1)S(1)}, u32[]{:S(2)}, u32[]{:S(2)}) collective-permute-start(bf16[256,640]{1,0:T(8,128)(2,1)S(1)} %collective-permute-done.5.near_ref), channel_id=1, source_target_pairs={{0,1},{1,0},{2,3},{3,2},{4,5},{5,4},{6,7},{7,6},{8,9},{9,8},{10,11... | collective-permute-start | bytes 983048 | tf_op jit(solution)/shard_map/ppermute | solution.py:399
  40.6 1.5 %collective-permute-start.7 = (bf16[256,384]{1,0:T(8,128)(2,1)S(1)}, bf16[256,384]{1,0:T(8,128)(2,1)S(1)}, u32[]{:S(2)}, u32[]{:S(2)}) collective-permute-start(bf16[256,384]{1,0:T(8,128)(2,1)S(1)} %shard_map.84.near_ref.after_ref), channel_id=1, source_target_pairs={{0,1},{1,0},{2,3},{3,2},{4,5},{5,4},{6,7},{7,6},{8,9},{9,8},{10,11... | collective-permute-start | bytes 589832 | tf_op jit(solution)/shard_map/ppermute | solution.py:399
  42.6 6.5 %collective-permute-start.10 = (bf16[128,640]{1,0:T(8,128)(2,1)S(1)}, bf16[128,640]{1,0:T(8,128)(2,1)S(1)}, u32[]{:S(2)}, u32[]{:S(2)}) collective-permute-start(bf16[128,640]{1,0:T(8,128)(2,1)S(1)} %get-tuple-element.42), channel_id=1, source_target_pairs={{0,6},{1,7},{2,0},{3,1},{4,2},{5,3},{6,4},{7,5},{8,14},{9,15},{10,... | collective-permute-start | bytes 491528 | tf_op jit(solution)/shard_map/ppermute | solution.py:424
  44.4 7.3 %collective-permute-start.9 = (bf16[128,640]{1,0:T(8,128)(2,1)S(1)}, bf16[128,640]{1,0:T(8,128)(2,1)S(1)}, u32[]{:S(2)}, u32[]{:S(2)}) collective-permute-start(bf16[128,640]{1,0:T(8,128)(2,1)S(1)} %get-tuple-element.41), channel_id=1, source_target_pairs={{0,2},{1,3},{2,4},{3,5},{4,6},{5,7},{6,0},{7,1},{8,10},{9,11},{10,... | collective-permute-start | bytes 491528 | tf_op jit(solution)/shard_map/ppermute | solution.py:423
  51.9 10.1 %collective-permute-start.11 = (bf16[256,640]{1,0:T(8,128)(2,1)S(1)}, bf16[256,640]{1,0:T(8,128)(2,1)S(1)}, u32[]{:S(2)}, u32[]{:S(2)}) collective-permute-start(bf16[256,640]{1,0:T(8,128)(2,1)S(1)} %get-tuple-element.43), channel_id=1, source_target_pairs={{0,2},{1,3},{2,4},{3,5},{4,6},{5,7},{6,0},{7,1},{8,10},{9,11},{10,... | collective-permute-start | bytes 983048 | tf_op jit(solution)/shard_map/ppermute | solution.py:429
  52.0 10.0 %collective-permute-start.12 = (bf16[256,640]{1,0:T(8,128)(2,1)S(1)}, bf16[256,640]{1,0:T(8,128)(2,1)S(1)}, u32[]{:S(2)}, u32[]{:S(2)}) collective-permute-start(bf16[256,640]{1,0:T(8,128)(2,1)S(1)} %get-tuple-element.44), channel_id=1, source_target_pairs={{0,6},{1,7},{2,0},{3,1},{4,2},{5,3},{6,4},{7,5},{8,14},{9,15},{10,... | collective-permute-start | bytes 983048 | tf_op jit(solution)/shard_map/ppermute | solution.py:430

commit v7 on v6

--- a/solution.py
+++ b/solution.py
@@ -333,14 +333,47 @@
     )(near, far, in_hbm(out_near), in_hbm(out_far))
 
 
+def output_neighbours_kernel(near_ref, far_ref, near_hbm, far_hbm, *refs):
+    above_late, above_early, below_early, below_late, wo_ref, sems = refs
+    half = above_late.shape[0]
+    copies = [
+        out_weight_copies(i, shift, near_hbm, far_hbm, wo_ref, sems)
+        for i, shift in enumerate((1, -1))
+    ]
+    for pair in copies:
+        for copy in pair:
+            copy.start()
+    both = jnp.concatenate([near_ref[...], far_ref[...]], -1)
+    for i, (top_ref, bottom_ref) in enumerate(((above_late, above_early), (below_early, below_late))):
+        for copy in copies[i]:
+            copy.wait()
+        block = jnp.dot(both, wo_ref[i], preferred_element_type=jnp.float32)
+        top_ref[...] = block[:half].astype(top_ref.dtype)
+        bottom_ref[...] = block[half:].astype(bottom_ref.dtype)
+
+
+def output_neighbours(near, far, out_near, out_far):
+    rows = near.shape[0]
+    depth, width = out_near.shape[0], out_near.shape[1] // (CHIPS * CORES)
+    late = jax.ShapeDtypeStruct((rows // 2, width), jnp.float32)
+    early = jax.ShapeDtypeStruct((rows // 2, width), jnp.bfloat16)
+    return pl.pallas_call(
+        output_neighbours_kernel,
+        in_specs=[VMEM] * 2 + [ANY] * 2,
+        out_specs=[VMEM] * 4,
+        out_shape=[late, early, early, late],
+        scratch_shapes=[
+            pltpu.VMEM((2, 2 * depth, width), jnp.bfloat16),
+            pltpu.SemaphoreType.DMA((2, 2)),
+        ],
+        compiler_params=params(8),
+        cost_estimate=output_cost(2, rows, 2 * depth, width),
+    )(near, far, in_hbm(out_near), in_hbm(out_far))
+
+
 def pass_on_kernel(above_ref, below_ref, top_ref, bottom_ref, to_above_ref, to_below_ref):
-    half = top_ref.shape[0]
-    top = above_ref[:half] + top_ref[...].astype(jnp.float32)
-    to_above_ref[:half] = top.astype(jnp.bfloat16)
-    to_above_ref[half:] = above_ref[half:].astype(jnp.bfloat16)
-    bottom = below_ref[half:] + bottom_ref[...].astype(jnp.float32)
-    to_below_ref[:half] = below_ref[:half].astype(jnp.bfloat16)
-    to_below_ref[half:] = bottom.astype(jnp.bfloat16)
+    to_above_ref[...] = (above_ref[...] + top_ref[...].astype(jnp.float32)).astype(jnp.bfloat16)
+    to_below_ref[...] = (below_ref[...] + bottom_ref[...].astype(jnp.float32)).astype(jnp.bfloat16)
 
 
 def pass_on(above, below, top, bottom):
@@ -355,10 +388,11 @@
 
 
 def place_kernel(pick_ref, count_ref, mine_ref, *refs):
-    parts, out_ref = refs[:-1], refs[-1]
-    total = mine_ref[...]
-    for part in parts:
-        total = total + part[...].astype(jnp.float32)
+    parts, out_ref = [ref[...].astype(jnp.float32) for ref in refs[:-1]], refs[-1]
+    half = mine_ref.shape[0] // 2
+    top = mine_ref[:half] + parts[0] + parts[1]
+    bottom = mine_ref[half:] + parts[2] + parts[3]
+    total = jnp.concatenate([top, bottom], 0)
     slots, tokens, width = out_ref.shape
     picks = block_picks(pick_ref[...], slots, tokens, total.shape[0])
     placed = jnp.dot(picks, total.astype(jnp.bfloat16), preferred_element_type=jnp.float32)
@@ -422,12 +456,18 @@
     top, bottom = output_halves(attn, attn_far, w_across)
     top = lax.ppermute(top, "tp", chip_shift(1))
     bottom = lax.ppermute(bottom, "tp", chip_shift(-1))
-    for_above, for_below = output(attn, attn_far, (1, -1), w_out, out_far)
-    to_above, to_below = pass_on(for_above, for_below, top, bottom)
+    above_late, above_early, below_early, below_late = output_neighbours(
+        attn, attn_far, w_out, out_far
+    )
+    above_early = lax.ppermute(above_early, "tp", chip_shift(1))
+    below_early = lax.ppermute(below_early, "tp", chip_shift(-1))
+    above_late, below_late = pass_on(above_late, below_late, top, bottom)
     (mine,) = output(attn, attn_far, (0,), w_out, out_far)
     parts = [
-        lax.ppermute(to_above, "tp", chip_shift(1)),
-        lax.ppermute(to_below, "tp", chip_shift(-1)),
+        lax.ppermute(above_late, "tp", chip_shift(1)),
+        below_early,
+        above_early,
+        lax.ppermute(below_late, "tp", chip_shift(-1)),
     ]
     slots = place(spread(pick), spread(count), mine, parts, learners, tokens)
     return lax.all_to_all(slots, "seq", 0, 0, tiled=True)

time: 87.4 us -> 85.9 us (0.983)
  waiting for transfers between devices: 18.9 us -> 14.2 us
  starting transfers between devices: 28 us -> 31 us
    ppermute x2 -> x4, starting transfers between devices: 3.31 us -> 6.34 us  [the longest x1 3.22 us: per_device(): lax.ppermute(below_late, 'tp', chip_shift(-1))]
    pallas_call x0 -> x1, Pallas kernels: none -> 2.26 us  [output_neighbours(): pl.pallas_call(output_neighbours_kernel, in_specs=[VMEM] * 2 + [ANY] * 2,...]
    pallas_call x2 -> x1, Pallas kernels: 3.95 us -> 1.7 us  [output(): pl.pallas_call(functools.partial(output_kernel, shifts), in_specs=[VMEM]...]
    ppermute x1, waiting for transfers between devices: 2.11 us -> 0.01 us  [per_device(): bottom = lax.ppermute(bottom, 'tp', chip_shift(-1))]
    ppermute x2 -> x4, waiting for transfers between devices: 4.12 us -> 2.5 us  [the longest x1 1.93 us: per_device(): lax.ppermute(above_late, 'tp', chip_shift(1))]
    ppermute x1, waiting for transfers between devices: 2.66 us -> 1.74 us  [per_device(): top = lax.ppermute(top, 'tp', chip_shift(1))]
  transfers between devices with their start and end apart: 15 -> 17, of which waited for: 6 -> 6; matrix products, arithmetic and copies ran while one was open for 2% -> 2% of each run, Pallas kernels for 14% -> 14%
where the time goes in v7:
time: 85.9 us; the launch traced here: 85.5 us
  starting transfers between devices  31 us (36%)
  blocking collectives  23.7 us (28%)
  waiting for transfers between devices  14.2 us (17%)
  Pallas kernels  13.2 us (15%)
  local copies, waits for them, and re-layouts  1.91 us (2%)
  other arithmetic  1.16 us (1%)
    all_to_all x1, blocking collectives, per_device(): return lax.all_to_all(slots, 'seq', 0, 0, tiled=True)  23.7 us
    all_to_all x1, starting transfers between devices, per_device(): lax.all_to_all(pieces, 'seq', 0, 0, axis_index_groups=halves, tiled=True)  8.91 us
    all_to_all x1, starting transfers between devices, per_device(): lax.all_to_all(route(prompts, pieces, learners), 'seq', 0, 0, tiled=True)  7.55 us
    all_to_all x1, waiting for transfers between devices, per_device(): lax.all_to_all(route(prompts, pieces, learners), 'seq', 0, 0, tiled=True)  5.49 us
    pallas_call x1, Pallas kernels, project(): pl.pallas_call(project_kernel, in_specs=[ANY] * 8, out_specs=[VMEM] * 2,...  4.51 us
    all_to_all x1, waiting for transfers between devices, per_device(): lax.all_to_all(pieces, 'seq', 0, 0, axis_index_groups=halves, tiled=True)  4.29 us
    ppermute x1, starting transfers between devices, per_device(): lax.ppermute(below_late, 'tp', chip_shift(-1))  3.22 us
    ppermute x1, starting transfers between devices, per_device(): below_early = lax.ppermute(below_early, 'tp', chip_shift(-1))  3.03 us
  transfers between devices with their start and end apart: 17, of which 6 were waited for; matrix products, arithmetic and copies ran while one was open for 2% of the time, Pallas kernels for 14%

profile of v7, /device:TPU:2, one launch (start us, length us, event | category | flops | bytes accessed | tf_op | source)
XLA Modules:
  0.0 85.5 jit_solution(3519997641878365006)
XLA Ops:
  0.0 0.0 copy-start
  0.0 0.0 collective-permute-start.8
  0.0 1.7 %collective-permute-start.1 = (bf16[256,640]{1,0:T(8,128)(2,1)}, bf16[256,640]{1,0:T(8,128)(2,1)S(1)}, u32[]{:S(2)}, u32[]{:S(2)}) collective-permute-start(bf16[256,640]{1,0:T(8,128)(2,1)} %bitcast.4), channel_id=1, source_target_pairs={{0,2},{1,3},{2,4},{3,5},{4,6},{5,7},{6,0},{7,1},{8,10},{9,11},{10,... | collective-permute-start | bytes 983048 | tf_op jit(solution)/shard_map/ppermute | solution.py:434
  1.7 1.7 %collective-permute-start.2 = (bf16[256,640]{1,0:T(8,128)(2,1)}, bf16[256,640]{1,0:T(8,128)(2,1)S(1)}, u32[]{:S(2)}, u32[]{:S(2)}) collective-permute-start(bf16[256,640]{1,0:T(8,128)(2,1)} %bitcast.5), channel_id=1, source_target_pairs={{0,6},{1,7},{2,0},{3,1},{4,2},{5,3},{6,4},{7,5},{8,14},{9,15},{10,... | collective-permute-start | bytes 983048 | tf_op jit(solution)/shard_map/ppermute | solution.py:435
  3.3 0.0 collective-permute-start
  3.3 8.9 %all-to-all-start = ((bf16[16,32,128]{2,1,0:T(8,128)(2,1)}), bf16[16,32,128]{2,1,0:T(8,128)(2,1)S(1)}, u32[]{:S(2)}, u32[]{:S(2)}) async-start(bf16[16,32,128]{2,1,0:T(8,128)(2,1)} %bitcast.9), calls=%async_computation | async-start | bytes 262144 | tf_op jit(solution)/shard_map/all_to_all | solution.py:430
  12.2 0.7 fusion.2
  12.9 0.1 iota_add_fusion
  13.0 0.0 collective-permute-done.1.refs_2_
  13.0 0.0 collective-permute-done.2.refs_4_
  13.0 0.0 copy-start.2
  13.0 0.1 collective-permute-start.3
  13.1 0.5 collective-permute-start.4
  13.6 0.1 add.44
  13.7 2.0 %collective-permute-start.5 = (bf16[256,640]{1,0:T(8,128)(2,1)}, bf16[256,640]{1,0:T(8,128)(2,1)S(1)}, u32[]{:S(2)}, u32[]{:S(2)}) collective-permute-start(bf16[256,640]{1,0:T(8,128)(2,1)} %bitcast.7), channel_id=1, source_target_pairs={{0,4},{1,5},{2,6},{3,7},{4,0},{5,1},{6,2},{7,3},{8,12},{9,13},{10,... | collective-permute-start | bytes 983048 | tf_op jit(solution)/shard_map/ppermute | solution.py:438
  15.7 0.1 fusion.pick_ref
  15.8 4.3 %all-to-all-done.piece_ref = bf16[16,32,128]{2,1,0:T(8,128)(2,1)S(1)} async-done(((bf16[16,32,128]{2,1,0:T(8,128)(2,1)}), bf16[16,32,128]{2,1,0:T(8,128)(2,1)S(1)}, u32[]{:S(2)}, u32[]{:S(2)}) %all-to-all-start) | async-done | bytes 131104 | tf_op jit(solution)/shard_map/all_to_all | solution.py:430
  20.1 0.0 collective-permute-done.refs_1_
  20.1 0.0 collective-permute-done.3.refs_3_
  20.1 0.0 copy-start.4
  20.1 0.0 collective-permute-done.4.refs_5_
  20.1 0.0 copy-start.5
  20.2 1.0 %shard_map.83 = bf16[32,32,128]{2,1,0:T(8,128)(2,1)} custom-call(bf16[512,256]{1,0:T(8,128)(2,1)S(1)} %fusion.pick_ref, bf16[16,32,128]{2,1,0:T(8,128)(2,1)S(1)} %all-to-all-done.piece_ref), custom_call_target="tpu_custom_call" | custom-call | tf_op jit(solution)/shard_map/pallas_call | solution.py:80
  21.2 0.0 copy-done.5
  21.2 7.6 %all-to-all-start.1 = ((bf16[32,32,128]{2,1,0:T(8,128)(2,1)}), bf16[32,32,128]{2,1,0:T(8,128)(2,1)S(1)}, u32[]{:S(2)}, u32[]{:S(2)}) async-start(bf16[32,32,128]{2,1,0:T(8,128)(2,1)} %shard_map.83), calls=%async_computation.1 | async-start | bytes 524288 | tf_op jit(solution)/shard_map/all_to_all | solution.py:442
  28.8 0.0 collective-permute-done.5.near_ref
  28.8 0.1 collective-permute-start.6
  28.9 0.1 fusion.1
  29.0 0.0 copy-done.1
  29.0 0.0 copy-done.2
  29.0 0.0 copy-done.3
  29.0 0.1 pad_maximum_fusion
  29.1 4.5 %shard_map.82 = (f32[256,640]{1,0:T(8,128)S(1)}, bf16[2,640,640]{2,1,0:T(8,128)(2,1)S(1)}) custom-call(bf16[256,640]{1,0:T(8,128)(2,1)} %bitcast.8, bf16[256,640]{1,0:T(8,128)(2,1)} %copy-done.3, bf16[256,640]{1,0:T(8,128)(2,1)} %copy-done.1, bf16[256,640]{1,0:T(8,128)(2,1)} %copy-done.4, bf16[256,640]{1,0:T(8,128)(2,1)} %copy-done.2, ...), custom_call_target="tpu_custom_call" | custom-call | flops 1258291200 | bytes 6553600 | tf_op jit(solution)/shard_map/pallas_call | solution.py:163
  33.6 0.0 collective-permute-done.6.far_ref
  33.6 5.5 %all-to-all-done.1.cache_ref = bf16[32,32,128]{2,1,0:T(8,128)(2,1)S(1)} async-done(((bf16[32,32,128]{2,1,0:T(8,128)(2,1)}), bf16[32,32,128]{2,1,0:T(8,128)(2,1)S(1)}, u32[]{:S(2)}, u32[]{:S(2)}) %all-to-all-start.1) | async-done | bytes 262176 | tf_op jit(solution)/shard_map/all_to_all | solution.py:442
  39.1 1.5 %shard_map.84.near_ref.after_ref = bf16[256,384]{1,0:T(8,128)(2,1)S(1)} custom-call(f32[256,640]{1,0:T(8,128)S(1)} %get-tuple-element.34.acc_ref, bf16[256,640]{1,0:T(8,128)(2,1)S(1)} %collective-permute-done.5.near_ref, bf16[256,640]{1,0:T(8,128)(2,1)S(1)} %collective-permute-done.6.far_ref, bf16[2,640,640]{2,1,0:T(8,128)(2,1)S(1)} %get-tuple-element.36.weight_ref, ...), custom_call_target="tpu_custom_call" | custom-call | flops 201326592 | bytes 393216 | tf_op jit(solution)/shard_map/pallas_call | solution.py:236
  40.6 0.1 collective-permute-start.7
  40.7 0.0 collective-permute-done.8.far_hbm
  40.7 1.2 %shard_map.87.wo_ref = bf16[1,768,640]{2,1,0:T(8,128)(2,1)S(1)} custom-call(bf16[256,384]{1,0:T(8,128)(2,1)S(1)} %shard_map.84.near_ref.after_ref, bf16[384,5120]{1,0:T(8,128)(2,1)} %near_hbm.5, bf16[384,5120]{1,0:T(8,128)(2,1)} %collective-permute-done.8.far_hbm), custom_call_target="tpu_custom_call" | custom-call | bytes 1966080 | tf_op jit(solution)/shard_map/pallas_call | solution.py:261
  42.0 0.2 collective-permute-done.7.far_ref
  42.2 0.5 shard_map.88
  42.7 1.8 %collective-permute-start.10 = (bf16[128,640]{1,0:T(8,128)(2,1)S(1)}, bf16[128,640]{1,0:T(8,128)(2,1)S(1)}, u32[]{:S(2)}, u32[]{:S(2)}) collective-permute-start(bf16[128,640]{1,0:T(8,128)(2,1)S(1)} %get-tuple-element.44), channel_id=1, source_target_pairs={{0,6},{1,7},{2,0},{3,1},{4,2},{5,3},{6,4},{7,5},{8,14},{9,15},{10,... | collective-permute-start | bytes 491528 | tf_op jit(solution)/shard_map/ppermute | solution.py:458
  44.5 0.3 collective-permute-start.9
  44.8 2.3 %shard_map.86 = (f32[128,640]{1,0:T(8,128)S(1)}, bf16[128,640]{1,0:T(8,128)(2,1)S(1)}, bf16[128,640]{1,0:T(8,128)(2,1)S(1)}, f32[128,640]{1,0:T(8,128)S(1)}) custom-call(bf16[256,384]{1,0:T(8,128)(2,1)S(1)} %shard_map.84.near_ref.after_ref, bf16[256,384]{1,0:T(8,128)(2,1)S(1)} %collective-permute-done.7.far_ref, bf16[384,5120]{1,0:T(8,128)(2,1)} %near_hbm.5, ...), custom_call_target="tpu_custom_call" | custom-call | flops 503316480 | bytes 1966080 | tf_op jit(solution)/shard_map/pallas_call | solution.py:360
  47.0 3.0 %collective-permute-start.12 = (bf16[128,640]{1,0:T(8,128)(2,1)S(1)}, bf16[128,640]{1,0:T(8,128)(2,1)S(1)}, u32[]{:S(2)}, u32[]{:S(2)}) collective-permute-start(bf16[128,640]{1,0:T(8,128)(2,1)S(1)} %get-tuple-element.46), channel_id=1, source_target_pairs={{0,6},{1,7},{2,0},{3,1},{4,2},{5,3},{6,4},{7,5},{8,14},{9,15},{10,... | collective-permute-start | bytes 491528 | tf_op jit(solution)/shard_map/ppermute | solution.py:463
  50.1 0.0 collective-permute-start.13
  50.1 0.0 collective-permute-done.10.bottom_ref
  50.1 1.7 %collective-permute-done.9.top_ref = bf16[128,640]{1,0:T(8,128)(2,1)S(1)} collective-permute-done((bf16[128,640]{1,0:T(8,128)(2,1)S(1)}, bf16[128,640]{1,0:T(8,128)(2,1)S(1)}, u32[]{:S(2)}, u32[]{:S(2)}) %collective-permute-start.9) | collective-permute-done | bytes 163872 | tf_op jit(solution)/shard_map/ppermute | solution.py:457
  51.8 0.1 shard_map.89
  51.9 0.1 collective-permute-start.11
  52.0 3.2 %collective-permute-start.14 = (bf16[128,640]{1,0:T(8,128)(2,1)S(1)}, bf16[128,640]{1,0:T(8,128)(2,1)S(1)}, u32[]{:S(2)}, u32[]{:S(2)}) collective-permute-start(bf16[128,640]{1,0:T(8,128)(2,1)S(1)} %get-tuple-element.48), channel_id=1, source_target_pairs={{0,6},{1,7},{2,0},{3,1},{4,2},{5,3},{6,4},{7,5},{8,14},{9,15},{10,... | collective-permute-start | bytes 491528 | tf_op jit(solution)/shard_map/ppermute | solution.py:470
  55.2 0.1 dynamic-slice_bitcast_fusion
  55.3 0.8 dynamic_slice.7
  56.0 0.1 select_reduce_fusion
  56.1 1.7 %shard_map.85.mine_ref = f32[256,640]{1,0:T(8,128)S(1)} custom-call(bf16[256,384]{1,0:T(8,128)(2,1)S(1)} %shard_map.84.near_ref.after_ref, bf16[256,384]{1,0:T(8,128)(2,1)S(1)} %collective-permute-done.7.far_ref, bf16[384,5120]{1,0:T(8,128)(2,1)} %near_hbm.5, bf16[384,5120]{1,0:T(8,128)(2,1)} %collective-permute-done.8.far_hbm), custom_call_target="tpu_custom_call" | custom-call | flops 251658240 | bytes 983040 | tf_op jit(solution)/shard_map/pallas_call | solution.py:322
  57.8 0.0 collective-permute-done.12.refs_1_
  57.8 0.6 collective-permute-done.13.refs_2_
  58.4 1.9 %collective-permute-done.11.refs_0_ = bf16[128,640]{1,0:T(8,128)(2,1)S(1)} collective-permute-done((bf16[128,640]{1,0:T(8,128)(2,1)S(1)}, bf16[128,640]{1,0:T(8,128)(2,1)S(1)}, u32[]{:S(2)}, u32[]{:S(2)}) %collective-permute-start.11) | collective-permute-done | bytes 163872 | tf_op jit(solution)/shard_map/ppermute | solution.py:467
  60.3 0.0 collective-permute-done.14.refs_3_
  60.3 0.1 broadcast_in_dim.45.pick_ref
  60.4 0.1 broadcast_in_dim.48.count_ref
  60.5 0.4 shard_map.90
  60.9 23.7 %all_to_all.15 = bf16[32,16,640]{2,1,0:T(8,128)(2,1)S(1)} all-to-all(bf16[32,16,640]{2,1,0:T(8,128)(2,1)S(1)} %shard_map.90), channel_id=1, replica_groups=mesh['seq'=32,'tp'=8] {'seq'}, dimensions={0} | all-to-all | bytes 1310720 | tf_op jit(solution)/shard_map/all_to_all | solution.py:473
  84.6 0.8 copy.10
  (6 shorter events, 0.0 us)
Async XLA Ops:
  0.0 55.2 %copy-start = (s32[512,1]{0,1:T(1,128)S(1)}, s32[512,1]{0,1:T(1,128)}, u32[]{:S(2)}) copy-start(s32[512,1]{0,1:T(1,128)} %param.10) | copy-start | bytes 6148
  0.0 40.7 %collective-permute-start.8 = (bf16[384,5120]{1,0:T(8,128)(2,1)}, bf16[384,5120]{1,0:T(8,128)(2,1)}, u32[]{:S(2)}, u32[]{:S(2)}) collective-permute-start(bf16[384,5120]{1,0:T(8,128)(2,1)} %near_hbm.5), channel_id=1, source_target_pairs={{0,1},{1,0},{2,3},{3,2},{4,5},{5,4},{6,7},{7,6},{8,9},{9,8},{10,11... | collective-permute-start | bytes 11796488 | tf_op jit(solution)/shard_map/ppermute | solution.py:433
  0.0 13.0 %collective-permute-start.1 = (bf16[256,640]{1,0:T(8,128)(2,1)}, bf16[256,640]{1,0:T(8,128)(2,1)S(1)}, u32[]{:S(2)}, u32[]{:S(2)}) collective-permute-start(bf16[256,640]{1,0:T(8,128)(2,1)} %bitcast.4), channel_id=1, source_target_pairs={{0,2},{1,3},{2,4},{3,5},{4,6},{5,7},{6,0},{7,1},{8,10},{9,11},{10,... | collective-permute-start | bytes 983048 | tf_op jit(solution)/shard_map/ppermute | solution.py:434
  1.7 11.3 %collective-permute-start.2 = (bf16[256,640]{1,0:T(8,128)(2,1)}, bf16[256,640]{1,0:T(8,128)(2,1)S(1)}, u32[]{:S(2)}, u32[]{:S(2)}) collective-permute-start(bf16[256,640]{1,0:T(8,128)(2,1)} %bitcast.5), channel_id=1, source_target_pairs={{0,6},{1,7},{2,0},{3,1},{4,2},{5,3},{6,4},{7,5},{8,14},{9,15},{10,... | collective-permute-start | bytes 983048 | tf_op jit(solution)/shard_map/ppermute | solution.py:435
  3.3 16.8 %collective-permute-start = (bf16[256,640]{1,0:T(8,128)(2,1)}, bf16[256,640]{1,0:T(8,128)(2,1)S(1)}, u32[]{:S(2)}, u32[]{:S(2)}) collective-permute-start(bf16[256,640]{1,0:T(8,128)(2,1)} %bitcast.6), channel_id=1, source_target_pairs={{0,1},{1,0},{2,3},{3,2},{4,5},{5,4},{6,7},{7,6},{8,9},{9,8},{10,11... | collective-permute-start | bytes 983048 | tf_op jit(solution)/shard_map/ppermute | solution.py:433
  3.3 16.8 %all-to-all-start = ((bf16[16,32,128]{2,1,0:T(8,128)(2,1)}), bf16[16,32,128]{2,1,0:T(8,128)(2,1)S(1)}, u32[]{:S(2)}, u32[]{:S(2)}) async-start(bf16[16,32,128]{2,1,0:T(8,128)(2,1)} %bitcast.9), calls=%async_computation | async-start | bytes 262144 | tf_op jit(solution)/shard_map/all_to_all | solution.py:430
  13.0 16.0 %copy-start.1 = (bf16[256,640]{1,0:T(8,128)(2,1)}, bf16[256,640]{1,0:T(8,128)(2,1)S(1)}, u32[]{:S(2)}) copy-start(bf16[256,640]{1,0:T(8,128)(2,1)S(1)} %collective-permute-done.1.refs_2_) | copy-start | bytes 983044
  13.0 16.0 %copy-start.2 = (bf16[256,640]{1,0:T(8,128)(2,1)}, bf16[256,640]{1,0:T(8,128)(2,1)S(1)}, u32[]{:S(2)}) copy-start(bf16[256,640]{1,0:T(8,128)(2,1)S(1)} %collective-permute-done.2.refs_4_) | copy-start | bytes 983044
  13.0 7.1 %collective-permute-start.3 = (bf16[256,640]{1,0:T(8,128)(2,1)S(1)}, bf16[256,640]{1,0:T(8,128)(2,1)S(1)}, u32[]{:S(2)}, u32[]{:S(2)}) collective-permute-start(bf16[256,640]{1,0:T(8,128)(2,1)S(1)} %collective-permute-done.1.refs_2_), channel_id=1, source_target_pairs={{0,1},{1,0},{2,3},{3,2},{4,5},{5,4},{6,7},{7,6},{8,9},{9,8},{10,11... | collective-permute-start | bytes 983048 | tf_op jit(solution)/shard_map/ppermute | solution.py:433
  13.1 7.0 %collective-permute-start.4 = (bf16[256,640]{1,0:T(8,128)(2,1)S(1)}, bf16[256,640]{1,0:T(8,128)(2,1)S(1)}, u32[]{:S(2)}, u32[]{:S(2)}) collective-permute-start(bf16[256,640]{1,0:T(8,128)(2,1)S(1)} %collective-permute-done.2.refs_4_), channel_id=1, source_target_pairs={{0,1},{1,0},{2,3},{3,2},{4,5},{5,4},{6,7},{7,6},{8,9},{9,8},{10,11... | collective-permute-start | bytes 983048 | tf_op jit(solution)/shard_map/ppermute | solution.py:433
  13.7 15.1 %collective-permute-start.5 = (bf16[256,640]{1,0:T(8,128)(2,1)}, bf16[256,640]{1,0:T(8,128)(2,1)S(1)}, u32[]{:S(2)}, u32[]{:S(2)}) collective-permute-start(bf16[256,640]{1,0:T(8,128)(2,1)} %bitcast.7), channel_id=1, source_target_pairs={{0,4},{1,5},{2,6},{3,7},{4,0},{5,1},{6,2},{7,3},{8,12},{9,13},{10,... | collective-permute-start | bytes 983048 | tf_op jit(solution)/shard_map/ppermute | solution.py:438
  20.1 8.9 %copy-start.3 = (bf16[256,640]{1,0:T(8,128)(2,1)}, bf16[256,640]{1,0:T(8,128)(2,1)S(1)}, u32[]{:S(2)}) copy-start(bf16[256,640]{1,0:T(8,128)(2,1)S(1)} %collective-permute-done.refs_1_) | copy-start | bytes 983044
  20.1 8.9 %copy-start.4 = (bf16[256,640]{1,0:T(8,128)(2,1)}, bf16[256,640]{1,0:T(8,128)(2,1)S(1)}, u32[]{:S(2)}) copy-start(bf16[256,640]{1,0:T(8,128)(2,1)S(1)} %collective-permute-done.3.refs_3_) | copy-start | bytes 983044
  20.1 1.0 %copy-start.5 = (bf16[256,640]{1,0:T(8,128)(2,1)}, bf16[256,640]{1,0:T(8,128)(2,1)S(1)}, u32[]{:S(2)}) copy-start(bf16[256,640]{1,0:T(8,128)(2,1)S(1)} %collective-permute-done.4.refs_5_) | copy-start | bytes 983044
  21.2 17.9 %all-to-all-start.1 = ((bf16[32,32,128]{2,1,0:T(8,128)(2,1)}), bf16[32,32,128]{2,1,0:T(8,128)(2,1)S(1)}, u32[]{:S(2)}, u32[]{:S(2)}) async-start(bf16[32,32,128]{2,1,0:T(8,128)(2,1)} %shard_map.83), calls=%async_computation.1 | async-start | bytes 524288 | tf_op jit(solution)/shard_map/all_to_all | solution.py:442
  28.8 4.9 %collective-permute-start.6 = (bf16[256,640]{1,0:T(8,128)(2,1)S(1)}, bf16[256,640]{1,0:T(8,128)(2,1)S(1)}, u32[]{:S(2)}, u32[]{:S(2)}) collective-permute-start(bf16[256,640]{1,0:T(8,128)(2,1)S(1)} %collective-permute-done.5.near_ref), channel_id=1, source_target_pairs={{0,1},{1,0},{2,3},{3,2},{4,5},{5,4},{6,7},{7,6},{8,9},{9,8},{10,11... | collective-permute-start | bytes 983048 | tf_op jit(solution)/shard_map/ppermute | solution.py:433
  40.6 1.5 %collective-permute-start.7 = (bf16[256,384]{1,0:T(8,128)(2,1)S(1)}, bf16[256,384]{1,0:T(8,128)(2,1)S(1)}, u32[]{:S(2)}, u32[]{:S(2)}) collective-permute-start(bf16[256,384]{1,0:T(8,128)(2,1)S(1)} %shard_map.84.near_ref.after_ref), channel_id=1, source_target_pairs={{0,1},{1,0},{2,3},{3,2},{4,5},{5,4},{6,7},{7,6},{8,9},{9,8},{10,11... | collective-permute-start | bytes 589832 | tf_op jit(solution)/shard_map/ppermute | solution.py:433
  42.7 7.4 %collective-permute-start.10 = (bf16[128,640]{1,0:T(8,128)(2,1)S(1)}, bf16[128,640]{1,0:T(8,128)(2,1)S(1)}, u32[]{:S(2)}, u32[]{:S(2)}) collective-permute-start(bf16[128,640]{1,0:T(8,128)(2,1)S(1)} %get-tuple-element.44), channel_id=1, source_target_pairs={{0,6},{1,7},{2,0},{3,1},{4,2},{5,3},{6,4},{7,5},{8,14},{9,15},{10,... | collective-permute-start | bytes 491528 | tf_op jit(solution)/shard_map/ppermute | solution.py:458
  44.5 7.3 %collective-permute-start.9 = (bf16[128,640]{1,0:T(8,128)(2,1)S(1)}, bf16[128,640]{1,0:T(8,128)(2,1)S(1)}, u32[]{:S(2)}, u32[]{:S(2)}) collective-permute-start(bf16[128,640]{1,0:T(8,128)(2,1)S(1)} %get-tuple-element.43), channel_id=1, source_target_pairs={{0,2},{1,3},{2,4},{3,5},{4,6},{5,7},{6,0},{7,1},{8,10},{9,11},{10,... | collective-permute-start | bytes 491528 | tf_op jit(solution)/shard_map/ppermute | solution.py:457
  47.0 10.8 %collective-permute-start.12 = (bf16[128,640]{1,0:T(8,128)(2,1)S(1)}, bf16[128,640]{1,0:T(8,128)(2,1)S(1)}, u32[]{:S(2)}, u32[]{:S(2)}) collective-permute-start(bf16[128,640]{1,0:T(8,128)(2,1)S(1)} %get-tuple-element.46), channel_id=1, source_target_pairs={{0,6},{1,7},{2,0},{3,1},{4,2},{5,3},{6,4},{7,5},{8,14},{9,15},{10,... | collective-permute-start | bytes 491528 | tf_op jit(solution)/shard_map/ppermute | solution.py:463
  50.1 8.3 %collective-permute-start.13 = (bf16[128,640]{1,0:T(8,128)(2,1)S(1)}, bf16[128,640]{1,0:T(8,128)(2,1)S(1)}, u32[]{:S(2)}, u32[]{:S(2)}) collective-permute-start(bf16[128,640]{1,0:T(8,128)(2,1)S(1)} %get-tuple-element.47), channel_id=1, source_target_pairs={{0,2},{1,3},{2,4},{3,5},{4,6},{5,7},{6,0},{7,1},{8,10},{9,11},{10,... | collective-permute-start | bytes 491528 | tf_op jit(solution)/shard_map/ppermute | solution.py:462
  51.9 8.4 %collective-permute-start.11 = (bf16[128,640]{1,0:T(8,128)(2,1)S(1)}, bf16[128,640]{1,0:T(8,128)(2,1)S(1)}, u32[]{:S(2)}, u32[]{:S(2)}) collective-permute-start(bf16[128,640]{1,0:T(8,128)(2,1)S(1)} %get-tuple-element.45), channel_id=1, source_target_pairs={{0,2},{1,3},{2,4},{3,5},{4,6},{5,7},{6,0},{7,1},{8,10},{9,11},{10,... | collective-permute-start | bytes 491528 | tf_op jit(solution)/shard_map/ppermute | solution.py:467
  52.0 8.4 %collective-permute-start.14 = (bf16[128,640]{1,0:T(8,128)(2,1)S(1)}, bf16[128,640]{1,0:T(8,128)(2,1)S(1)}, u32[]{:S(2)}, u32[]{:S(2)}) collective-permute-start(bf16[128,640]{1,0:T(8,128)(2,1)S(1)} %get-tuple-element.48), channel_id=1, source_target_pairs={{0,6},{1,7},{2,0},{3,1},{4,2},{5,3},{6,4},{7,5},{8,14},{9,15},{10,... | collective-permute-start | bytes 491528 | tf_op jit(solution)/shard_map/ppermute | solution.py:470

commit v8 on v7

--- a/solution.py
+++ b/solution.py
@@ -184,8 +184,8 @@
     )(*[in_hbm(v) for v in (x, *shards, w_query, w_keyval)])
 
 
-def attend_kernel(
-    tokens, acc_ref, near_ref, far_ref, weight_ref, cos_ref, sin_ref, cache_ref, attn_ref
+def finish_kernel(
+    tokens, acc_ref, near_ref, far_ref, weight_ref, cos_ref, sin_ref, q_ref, k_ref, v_ref
 ):
     rows, columns = acc_ref.shape
     heads = columns // HD - 2
@@ -201,19 +201,39 @@
         turned = pltpu.roll(v, HD // 2, 1).reshape(-1, tokens, HD) * sine
         return (v.reshape(-1, tokens, HD) * cosine + turned).astype(jnp.bfloat16).reshape(rows, HD)
 
+    for h in range(heads):
+        q_ref[h] = rotated(h)
+    k_ref[...] = rotated(heads)
+    v_ref[...] = both[:, (heads + 1) * HD :].astype(jnp.bfloat16)
+
+
+def finish(acc, near, far, weights, cosine, sine, tokens):
+    rows, columns = acc.shape
+    heads = columns // HD - 2
+    one = jax.ShapeDtypeStruct((rows, HD), jnp.bfloat16)
+    return pl.pallas_call(
+        functools.partial(finish_kernel, tokens),
+        in_specs=[VMEM] * 6,
+        out_specs=[VMEM] * 3,
+        out_shape=[jax.ShapeDtypeStruct((heads, rows, HD), jnp.bfloat16), one, one],
+        compiler_params=params(16),
+    )(acc, near, far, weights, cosine, sine)
+
+
+def attend_kernel(tokens, q_ref, k_ref, v_ref, cache_ref, attn_ref):
+    heads, rows, _ = q_ref.shape
     scale = 1.0 / math.sqrt(HD)
     near = cache_ref.shape[0] // 2
     cache = cache_ref[:near] + cache_ref[near:]
     half = near // 2
-    own_values = both[:, (heads + 1) * HD :].astype(jnp.bfloat16)
-    keys = jnp.concatenate([cache[:half].reshape(PL, HD), rotated(heads)], 0)
-    values = jnp.concatenate([cache[half:].reshape(PL, HD), own_values], 0)
+    keys = jnp.concatenate([cache[:half].reshape(PL, HD), k_ref[...]], 0)
+    values = jnp.concatenate([cache[half:].reshape(PL, HD), v_ref[...]], 0)
     row = lax.broadcasted_iota(jnp.int32, (rows, rows), 0)
     col = lax.broadcasted_iota(jnp.int32, (rows, rows), 1)
     seen = (row // tokens == col // tokens) & (col <= row)
     nt = (((1,), (1,)), ((), ()))
     scores = [
-        lax.dot_general(rotated(h), keys, nt, preferred_element_type=jnp.float32) * scale
+        lax.dot_general(q_ref[h], keys, nt, preferred_element_type=jnp.float32) * scale
         for h in range(heads)
     ]
     for h in range(heads):
@@ -230,12 +250,11 @@
         attn_ref[:, h * HD : (h + 1) * HD] = mixed.astype(jnp.bfloat16)
 
 
-def attend(acc, near, far, weights, cosine, sine, cache, tokens):
-    rows, columns = acc.shape
-    heads = columns // HD - 2
+def attend(queries, keys, values, cache, tokens):
+    heads, rows, _ = queries.shape
     return pl.pallas_call(
         functools.partial(attend_kernel, tokens),
-        in_specs=[VMEM] * 7,
+        in_specs=[VMEM] * 4,
         out_specs=VMEM,
         out_shape=jax.ShapeDtypeStruct((rows, heads * HD), jnp.bfloat16),
         compiler_params=params(16),
@@ -244,7 +263,7 @@
             bytes_accessed=4 * rows * heads * HD,
             transcendentals=2 * heads * rows * PL,
         ),
-    )(acc, near, far, weights, cosine, sine, cache)
+    )(queries, keys, values, cache)
 
 
 def fetch_kernel(shift, after_ref, near_hbm, far_hbm, wo_ref, sems):
@@ -443,7 +462,8 @@
 
     cosine, sine = rope_tables(tokens)
     acc, w_last = project(x, shards, w_query, w_keyval)
-    attn = attend(acc, across, swap(across), w_last, cosine, sine, cache, tokens)
+    projected = finish(acc, across, swap(across), w_last, cosine, sine, tokens)
+    attn = attend(*projected, cache, tokens)
     resp_len, resp_shard, attn = lax.optimization_barrier((resp_len, resp_shard, attn))
     own_len = lax.dynamic_slice_in_dim(resp_len, group * group_size, group_size, 0)
     own_shard = lax.dynamic_slice_in_dim(resp_shard[:, 0], group * group_size, group_size, 0)

time: 85.9 us -> 85.3 us (level)
  transfers between devices with their start and end apart: 17 -> 17, of which waited for: 6 -> 6; matrix products, arithmetic and copies ran while one was open for 2% -> 2% of each run, Pallas kernels for 14% -> 15%
where the time goes in v8:
time: 85.3 us; the launch traced here: 84.9 us
  starting transfers between devices  31 us (36%)
  blocking collectives  23.7 us (28%)
  waiting for transfers between devices  13.5 us (16%)
  Pallas kernels  13.4 us (16%)
  local copies, waits for them, and re-layouts  1.91 us (2%)
  other arithmetic  1.16 us (1%)
    all_to_all x1, blocking collectives, per_device(): return lax.all_to_all(slots, 'seq', 0, 0, tiled=True)  23.7 us
    all_to_all x1, starting transfers between devices, per_device(): lax.all_to_all(pieces, 'seq', 0, 0, axis_index_groups=halves, tiled=True)  8.91 us
    all_to_all x1, starting transfers between devices, per_device(): lax.all_to_all(route(prompts, pieces, learners), 'seq', 0, 0, tiled=True)  7.55 us
    all_to_all x1, waiting for transfers between devices, per_device(): lax.all_to_all(route(prompts, pieces, learners), 'seq', 0, 0, tiled=True)  4.77 us
    pallas_call x1, Pallas kernels, project(): pl.pallas_call(project_kernel, in_specs=[ANY] * 8, out_specs=[VMEM] * 2,...  4.55 us
    all_to_all x1, waiting for transfers between devices, per_device(): lax.all_to_all(pieces, 'seq', 0, 0, axis_index_groups=halves, tiled=True)  4.29 us
    ppermute x1, starting transfers between devices, per_device(): lax.ppermute(below_late, 'tp', chip_shift(-1))  3.22 us
    ppermute x1, starting transfers between devices, per_device(): below_early = lax.ppermute(below_early, 'tp', chip_shift(-1))  3.03 us
  transfers between devices with their start and end apart: 17, of which 6 were waited for; matrix products, arithmetic and copies ran while one was open for 2% of the time, Pallas kernels for 15%

profile of v8, /device:TPU:2, one launch (start us, length us, event | category | flops | bytes accessed | tf_op | source)
XLA Modules:
  0.0 84.9 jit_solution(4537134053926516905)
XLA Ops:
  0.0 0.0 copy-start
  0.0 0.0 collective-permute-start.8
  0.0 1.7 %collective-permute-start.1 = (bf16[256,640]{1,0:T(8,128)(2,1)}, bf16[256,640]{1,0:T(8,128)(2,1)S(1)}, u32[]{:S(2)}, u32[]{:S(2)}) collective-permute-start(bf16[256,640]{1,0:T(8,128)(2,1)} %bitcast.4), channel_id=1, source_target_pairs={{0,2},{1,3},{2,4},{3,5},{4,6},{5,7},{6,0},{7,1},{8,10},{9,11},{10,... | collective-permute-start | bytes 983048 | tf_op jit(solution)/shard_map/ppermute | solution.py:453
  1.7 1.7 %collective-permute-start.2 = (bf16[256,640]{1,0:T(8,128)(2,1)}, bf16[256,640]{1,0:T(8,128)(2,1)S(1)}, u32[]{:S(2)}, u32[]{:S(2)}) collective-permute-start(bf16[256,640]{1,0:T(8,128)(2,1)} %bitcast.5), channel_id=1, source_target_pairs={{0,6},{1,7},{2,0},{3,1},{4,2},{5,3},{6,4},{7,5},{8,14},{9,15},{10,... | collective-permute-start | bytes 983048 | tf_op jit(solution)/shard_map/ppermute | solution.py:454
  3.3 0.0 collective-permute-start
  3.3 8.9 %all-to-all-start = ((bf16[16,32,128]{2,1,0:T(8,128)(2,1)}), bf16[16,32,128]{2,1,0:T(8,128)(2,1)S(1)}, u32[]{:S(2)}, u32[]{:S(2)}) async-start(bf16[16,32,128]{2,1,0:T(8,128)(2,1)} %bitcast.9), calls=%async_computation | async-start | bytes 262144 | tf_op jit(solution)/shard_map/all_to_all | solution.py:449
  12.2 0.7 fusion.2
  12.9 0.1 iota_add_fusion
  13.0 0.0 collective-permute-done.1.refs_2_
  13.0 0.0 collective-permute-done.2.refs_4_
  13.0 0.0 copy-start.2
  13.0 0.1 collective-permute-start.3
  13.1 0.5 collective-permute-start.4
  13.6 0.1 add.44
  13.7 2.0 %collective-permute-start.5 = (bf16[256,640]{1,0:T(8,128)(2,1)}, bf16[256,640]{1,0:T(8,128)(2,1)S(1)}, u32[]{:S(2)}, u32[]{:S(2)}) collective-permute-start(bf16[256,640]{1,0:T(8,128)(2,1)} %bitcast.7), channel_id=1, source_target_pairs={{0,4},{1,5},{2,6},{3,7},{4,0},{5,1},{6,2},{7,3},{8,12},{9,13},{10,... | collective-permute-start | bytes 983048 | tf_op jit(solution)/shard_map/ppermute | solution.py:457
  15.7 0.1 fusion.pick_ref
  15.8 4.3 %all-to-all-done.piece_ref = bf16[16,32,128]{2,1,0:T(8,128)(2,1)S(1)} async-done(((bf16[16,32,128]{2,1,0:T(8,128)(2,1)}), bf16[16,32,128]{2,1,0:T(8,128)(2,1)S(1)}, u32[]{:S(2)}, u32[]{:S(2)}) %all-to-all-start) | async-done | bytes 131104 | tf_op jit(solution)/shard_map/all_to_all | solution.py:449
  20.1 0.0 collective-permute-done.refs_1_
  20.1 0.0 collective-permute-done.3.refs_3_
  20.1 0.0 copy-start.4
  20.1 0.0 collective-permute-done.4.refs_5_
  20.1 0.0 copy-start.5
  20.2 1.1 %shard_map.84 = bf16[32,32,128]{2,1,0:T(8,128)(2,1)} custom-call(bf16[512,256]{1,0:T(8,128)(2,1)S(1)} %fusion.pick_ref, bf16[16,32,128]{2,1,0:T(8,128)(2,1)S(1)} %all-to-all-done.piece_ref), custom_call_target="tpu_custom_call" | custom-call | tf_op jit(solution)/shard_map/pallas_call | solution.py:80
  21.2 7.6 %all-to-all-start.1 = ((bf16[32,32,128]{2,1,0:T(8,128)(2,1)}), bf16[32,32,128]{2,1,0:T(8,128)(2,1)S(1)}, u32[]{:S(2)}, u32[]{:S(2)}) async-start(bf16[32,32,128]{2,1,0:T(8,128)(2,1)} %shard_map.84), calls=%async_computation.1 | async-start | bytes 524288 | tf_op jit(solution)/shard_map/all_to_all | solution.py:461
  28.8 0.0 collective-permute-done.5.near_ref
  28.8 0.1 collective-permute-start.6
  28.9 0.1 fusion.1
  29.0 0.1 pad_maximum_fusion
  29.1 0.0 copy-done.1
  29.1 0.0 copy-done.2
  29.1 0.0 copy-done.3
  29.1 4.5 %shard_map.82 = (f32[256,640]{1,0:T(8,128)S(1)}, bf16[2,640,640]{2,1,0:T(8,128)(2,1)S(1)}) custom-call(bf16[256,640]{1,0:T(8,128)(2,1)} %bitcast.8, bf16[256,640]{1,0:T(8,128)(2,1)} %copy-done.3, bf16[256,640]{1,0:T(8,128)(2,1)} %copy-done.1, bf16[256,640]{1,0:T(8,128)(2,1)} %copy-done.4, bf16[256,640]{1,0:T(8,128)(2,1)} %copy-done.2, ...), custom_call_target="tpu_custom_call" | custom-call | flops 1258291200 | bytes 6553600 | tf_op jit(solution)/shard_map/pallas_call | solution.py:163
  33.7 0.0 collective-permute-done.6.far_ref
  33.7 0.7 shard_map.83
  34.4 4.8 %all-to-all-done.1.cache_ref = bf16[32,32,128]{2,1,0:T(8,128)(2,1)S(1)} async-done(((bf16[32,32,128]{2,1,0:T(8,128)(2,1)}), bf16[32,32,128]{2,1,0:T(8,128)(2,1)S(1)}, u32[]{:S(2)}, u32[]{:S(2)}) %all-to-all-start.1) | async-done | bytes 262176 | tf_op jit(solution)/shard_map/all_to_all | solution.py:461
  39.2 0.9 %shard_map.85.near_ref.after_ref = bf16[256,384]{1,0:T(8,128)(2,1)S(1)} custom-call(bf16[3,256,128]{2,1,0:T(8,128)(2,1)S(1)} %get-tuple-element.40.q_ref, bf16[256,128]{1,0:T(8,128)(2,1)S(1)} %get-tuple-element.41.k_ref, bf16[256,128]{1,0:T(8,128)(2,1)S(1)} %get-tuple-element.42.v_ref, bf16[32,32,128]{2,1,0:T(8,128)(2,1)S(1)} %all-to-all-done.1.cache_ref), custom_call_target="tpu_custom_call" | custom-call | flops 201326592 | bytes 393216 | tf_op jit(solution)/shard_map/pallas_call | solution.py:255
  40.1 0.1 collective-permute-start.7
  40.2 0.0 collective-permute-done.8.far_hbm
  40.2 1.2 %shard_map.88.wo_ref = bf16[1,768,640]{2,1,0:T(8,128)(2,1)S(1)} custom-call(bf16[256,384]{1,0:T(8,128)(2,1)S(1)} %shard_map.85.near_ref.after_ref, bf16[384,5120]{1,0:T(8,128)(2,1)} %near_hbm.5, bf16[384,5120]{1,0:T(8,128)(2,1)} %collective-permute-done.8.far_hbm), custom_call_target="tpu_custom_call" | custom-call | bytes 1966080 | tf_op jit(solution)/shard_map/pallas_call | solution.py:280
  41.4 0.2 collective-permute-done.7.far_ref
  41.6 0.5 shard_map.89
  42.1 1.8 %collective-permute-start.10 = (bf16[128,640]{1,0:T(8,128)(2,1)S(1)}, bf16[128,640]{1,0:T(8,128)(2,1)S(1)}, u32[]{:S(2)}, u32[]{:S(2)}) collective-permute-start(bf16[128,640]{1,0:T(8,128)(2,1)S(1)} %get-tuple-element.50), channel_id=1, source_target_pairs={{0,6},{1,7},{2,0},{3,1},{4,2},{5,3},{6,4},{7,5},{8,14},{9,15},{10,... | collective-permute-start | bytes 491528 | tf_op jit(solution)/shard_map/ppermute | solution.py:478
  43.9 0.3 collective-permute-start.9
  44.2 2.3 %shard_map.87 = (f32[128,640]{1,0:T(8,128)S(1)}, bf16[128,640]{1,0:T(8,128)(2,1)S(1)}, bf16[128,640]{1,0:T(8,128)(2,1)S(1)}, f32[128,640]{1,0:T(8,128)S(1)}) custom-call(bf16[256,384]{1,0:T(8,128)(2,1)S(1)} %shard_map.85.near_ref.after_ref, bf16[256,384]{1,0:T(8,128)(2,1)S(1)} %collective-permute-done.7.far_ref, bf16[384,5120]{1,0:T(8,128)(2,1)} %near_hbm.5, ...), custom_call_target="tpu_custom_call" | custom-call | flops 503316480 | bytes 1966080 | tf_op jit(solution)/shard_map/pallas_call | solution.py:379
  46.5 3.0 %collective-permute-start.12 = (bf16[128,640]{1,0:T(8,128)(2,1)S(1)}, bf16[128,640]{1,0:T(8,128)(2,1)S(1)}, u32[]{:S(2)}, u32[]{:S(2)}) collective-permute-start(bf16[128,640]{1,0:T(8,128)(2,1)S(1)} %get-tuple-element.52), channel_id=1, source_target_pairs={{0,6},{1,7},{2,0},{3,1},{4,2},{5,3},{6,4},{7,5},{8,14},{9,15},{10,... | collective-permute-start | bytes 491528 | tf_op jit(solution)/shard_map/ppermute | solution.py:483
  49.5 0.0 collective-permute-start.13
  49.5 0.0 collective-permute-done.10.bottom_ref
  49.5 1.7 %collective-permute-done.9.top_ref = bf16[128,640]{1,0:T(8,128)(2,1)S(1)} collective-permute-done((bf16[128,640]{1,0:T(8,128)(2,1)S(1)}, bf16[128,640]{1,0:T(8,128)(2,1)S(1)}, u32[]{:S(2)}, u32[]{:S(2)}) %collective-permute-start.9) | collective-permute-done | bytes 163872 | tf_op jit(solution)/shard_map/ppermute | solution.py:477
  51.2 0.1 shard_map.90
  51.3 0.1 collective-permute-start.11
  51.4 3.2 %collective-permute-start.14 = (bf16[128,640]{1,0:T(8,128)(2,1)S(1)}, bf16[128,640]{1,0:T(8,128)(2,1)S(1)}, u32[]{:S(2)}, u32[]{:S(2)}) collective-permute-start(bf16[128,640]{1,0:T(8,128)(2,1)S(1)} %get-tuple-element.54), channel_id=1, source_target_pairs={{0,6},{1,7},{2,0},{3,1},{4,2},{5,3},{6,4},{7,5},{8,14},{9,15},{10,... | collective-permute-start | bytes 491528 | tf_op jit(solution)/shard_map/ppermute | solution.py:490
  54.6 0.1 dynamic-slice_bitcast_fusion
  54.7 0.8 dynamic_slice.7
  55.5 0.1 select_reduce_fusion
  55.6 1.7 %shard_map.86.mine_ref = f32[256,640]{1,0:T(8,128)S(1)} custom-call(bf16[256,384]{1,0:T(8,128)(2,1)S(1)} %shard_map.85.near_ref.after_ref, bf16[256,384]{1,0:T(8,128)(2,1)S(1)} %collective-permute-done.7.far_ref, bf16[384,5120]{1,0:T(8,128)(2,1)} %near_hbm.5, bf16[384,5120]{1,0:T(8,128)(2,1)} %collective-permute-done.8.far_hbm), custom_call_target="tpu_custom_call" | custom-call | flops 251658240 | bytes 983040 | tf_op jit(solution)/shard_map/pallas_call | solution.py:341
  57.3 0.0 collective-permute-done.12.refs_1_
  57.3 0.6 collective-permute-done.13.refs_2_
  57.8 1.9 %collective-permute-done.11.refs_0_ = bf16[128,640]{1,0:T(8,128)(2,1)S(1)} collective-permute-done((bf16[128,640]{1,0:T(8,128)(2,1)S(1)}, bf16[128,640]{1,0:T(8,128)(2,1)S(1)}, u32[]{:S(2)}, u32[]{:S(2)}) %collective-permute-start.11) | collective-permute-done | bytes 163872 | tf_op jit(solution)/shard_map/ppermute | solution.py:487
  59.8 0.0 collective-permute-done.14.refs_3_
  59.8 0.1 broadcast_in_dim.45.pick_ref
  59.8 0.1 broadcast_in_dim.48.count_ref
  59.9 0.5 shard_map.91
  60.4 23.7 %all_to_all.15 = bf16[32,16,640]{2,1,0:T(8,128)(2,1)S(1)} all-to-all(bf16[32,16,640]{2,1,0:T(8,128)(2,1)S(1)} %shard_map.91), channel_id=1, replica_groups=mesh['seq'=32,'tp'=8] {'seq'}, dimensions={0} | all-to-all | bytes 1310720 | tf_op jit(solution)/shard_map/all_to_all | solution.py:493
  84.1 0.8 copy.10
  (7 shorter events, 0.0 us)
Async XLA Ops:
  0.0 54.6 %copy-start = (s32[512,1]{0,1:T(1,128)S(1)}, s32[512,1]{0,1:T(1,128)}, u32[]{:S(2)}) copy-start(s32[512,1]{0,1:T(1,128)} %param.10) | copy-start | bytes 6148
  0.0 40.2 %collective-permute-start.8 = (bf16[384,5120]{1,0:T(8,128)(2,1)}, bf16[384,5120]{1,0:T(8,128)(2,1)}, u32[]{:S(2)}, u32[]{:S(2)}) collective-permute-start(bf16[384,5120]{1,0:T(8,128)(2,1)} %near_hbm.5), channel_id=1, source_target_pairs={{0,1},{1,0},{2,3},{3,2},{4,5},{5,4},{6,7},{7,6},{8,9},{9,8},{10,11... | collective-permute-start | bytes 11796488 | tf_op jit(solution)/shard_map/ppermute | solution.py:452
  0.0 13.0 %collective-permute-start.1 = (bf16[256,640]{1,0:T(8,128)(2,1)}, bf16[256,640]{1,0:T(8,128)(2,1)S(1)}, u32[]{:S(2)}, u32[]{:S(2)}) collective-permute-start(bf16[256,640]{1,0:T(8,128)(2,1)} %bitcast.4), channel_id=1, source_target_pairs={{0,2},{1,3},{2,4},{3,5},{4,6},{5,7},{6,0},{7,1},{8,10},{9,11},{10,... | collective-permute-start | bytes 983048 | tf_op jit(solution)/shard_map/ppermute | solution.py:453
  1.7 11.3 %collective-permute-start.2 = (bf16[256,640]{1,0:T(8,128)(2,1)}, bf16[256,640]{1,0:T(8,128)(2,1)S(1)}, u32[]{:S(2)}, u32[]{:S(2)}) collective-permute-start(bf16[256,640]{1,0:T(8,128)(2,1)} %bitcast.5), channel_id=1, source_target_pairs={{0,6},{1,7},{2,0},{3,1},{4,2},{5,3},{6,4},{7,5},{8,14},{9,15},{10,... | collective-permute-start | bytes 983048 | tf_op jit(solution)/shard_map/ppermute | solution.py:454
  3.3 16.8 %collective-permute-start = (bf16[256,640]{1,0:T(8,128)(2,1)}, bf16[256,640]{1,0:T(8,128)(2,1)S(1)}, u32[]{:S(2)}, u32[]{:S(2)}) collective-permute-start(bf16[256,640]{1,0:T(8,128)(2,1)} %bitcast.6), channel_id=1, source_target_pairs={{0,1},{1,0},{2,3},{3,2},{4,5},{5,4},{6,7},{7,6},{8,9},{9,8},{10,11... | collective-permute-start | bytes 983048 | tf_op jit(solution)/shard_map/ppermute | solution.py:452
  3.3 16.8 %all-to-all-start = ((bf16[16,32,128]{2,1,0:T(8,128)(2,1)}), bf16[16,32,128]{2,1,0:T(8,128)(2,1)S(1)}, u32[]{:S(2)}, u32[]{:S(2)}) async-start(bf16[16,32,128]{2,1,0:T(8,128)(2,1)} %bitcast.9), calls=%async_computation | async-start | bytes 262144 | tf_op jit(solution)/shard_map/all_to_all | solution.py:449
  13.0 16.1 %copy-start.1 = (bf16[256,640]{1,0:T(8,128)(2,1)}, bf16[256,640]{1,0:T(8,128)(2,1)S(1)}, u32[]{:S(2)}) copy-start(bf16[256,640]{1,0:T(8,128)(2,1)S(1)} %collective-permute-done.1.refs_2_) | copy-start | bytes 983044
  13.0 16.1 %copy-start.2 = (bf16[256,640]{1,0:T(8,128)(2,1)}, bf16[256,640]{1,0:T(8,128)(2,1)S(1)}, u32[]{:S(2)}) copy-start(bf16[256,640]{1,0:T(8,128)(2,1)S(1)} %collective-permute-done.2.refs_4_) | copy-start | bytes 983044
  13.0 7.1 %collective-permute-start.3 = (bf16[256,640]{1,0:T(8,128)(2,1)S(1)}, bf16[256,640]{1,0:T(8,128)(2,1)S(1)}, u32[]{:S(2)}, u32[]{:S(2)}) collective-permute-start(bf16[256,640]{1,0:T(8,128)(2,1)S(1)} %collective-permute-done.1.refs_2_), channel_id=1, source_target_pairs={{0,1},{1,0},{2,3},{3,2},{4,5},{5,4},{6,7},{7,6},{8,9},{9,8},{10,11... | collective-permute-start | bytes 983048 | tf_op jit(solution)/shard_map/ppermute | solution.py:452
  13.1 7.0 %collective-permute-start.4 = (bf16[256,640]{1,0:T(8,128)(2,1)S(1)}, bf16[256,640]{1,0:T(8,128)(2,1)S(1)}, u32[]{:S(2)}, u32[]{:S(2)}) collective-permute-start(bf16[256,640]{1,0:T(8,128)(2,1)S(1)} %collective-permute-done.2.refs_4_), channel_id=1, source_target_pairs={{0,1},{1,0},{2,3},{3,2},{4,5},{5,4},{6,7},{7,6},{8,9},{9,8},{10,11... | collective-permute-start | bytes 983048 | tf_op jit(solution)/shard_map/ppermute | solution.py:452
  13.7 15.1 %collective-permute-start.5 = (bf16[256,640]{1,0:T(8,128)(2,1)}, bf16[256,640]{1,0:T(8,128)(2,1)S(1)}, u32[]{:S(2)}, u32[]{:S(2)}) collective-permute-start(bf16[256,640]{1,0:T(8,128)(2,1)} %bitcast.7), channel_id=1, source_target_pairs={{0,4},{1,5},{2,6},{3,7},{4,0},{5,1},{6,2},{7,3},{8,12},{9,13},{10,... | collective-permute-start | bytes 983048 | tf_op jit(solution)/shard_map/ppermute | solution.py:457
  20.1 9.0 %copy-start.3 = (bf16[256,640]{1,0:T(8,128)(2,1)}, bf16[256,640]{1,0:T(8,128)(2,1)S(1)}, u32[]{:S(2)}) copy-start(bf16[256,640]{1,0:T(8,128)(2,1)S(1)} %collective-permute-done.refs_1_) | copy-start | bytes 983044
  20.1 9.0 %copy-start.4 = (bf16[256,640]{1,0:T(8,128)(2,1)}, bf16[256,640]{1,0:T(8,128)(2,1)S(1)}, u32[]{:S(2)}) copy-start(bf16[256,640]{1,0:T(8,128)(2,1)S(1)} %collective-permute-done.3.refs_3_) | copy-start | bytes 983044
  20.1 9.0 %copy-start.5 = (bf16[256,640]{1,0:T(8,128)(2,1)}, bf16[256,640]{1,0:T(8,128)(2,1)S(1)}, u32[]{:S(2)}) copy-start(bf16[256,640]{1,0:T(8,128)(2,1)S(1)} %collective-permute-done.4.refs_5_) | copy-start | bytes 983044
  21.2 17.9 %all-to-all-start.1 = ((bf16[32,32,128]{2,1,0:T(8,128)(2,1)}), bf16[32,32,128]{2,1,0:T(8,128)(2,1)S(1)}, u32[]{:S(2)}, u32[]{:S(2)}) async-start(bf16[32,32,128]{2,1,0:T(8,128)(2,1)} %shard_map.84), calls=%async_computation.1 | async-start | bytes 524288 | tf_op jit(solution)/shard_map/all_to_all | solution.py:461
  28.8 4.9 %collective-permute-start.6 = (bf16[256,640]{1,0:T(8,128)(2,1)S(1)}, bf16[256,640]{1,0:T(8,128)(2,1)S(1)}, u32[]{:S(2)}, u32[]{:S(2)}) collective-permute-start(bf16[256,640]{1,0:T(8,128)(2,1)S(1)} %collective-permute-done.5.near_ref), channel_id=1, source_target_pairs={{0,1},{1,0},{2,3},{3,2},{4,5},{5,4},{6,7},{7,6},{8,9},{9,8},{10,11... | collective-permute-start | bytes 983048 | tf_op jit(solution)/shard_map/ppermute | solution.py:452
  40.1 1.5 %collective-permute-start.7 = (bf16[256,384]{1,0:T(8,128)(2,1)S(1)}, bf16[256,384]{1,0:T(8,128)(2,1)S(1)}, u32[]{:S(2)}, u32[]{:S(2)}) collective-permute-start(bf16[256,384]{1,0:T(8,128)(2,1)S(1)} %shard_map.85.near_ref.after_ref), channel_id=1, source_target_pairs={{0,1},{1,0},{2,3},{3,2},{4,5},{5,4},{6,7},{7,6},{8,9},{9,8},{10,11... | collective-permute-start | bytes 589832 | tf_op jit(solution)/shard_map/ppermute | solution.py:452
  42.1 7.4 %collective-permute-start.10 = (bf16[128,640]{1,0:T(8,128)(2,1)S(1)}, bf16[128,640]{1,0:T(8,128)(2,1)S(1)}, u32[]{:S(2)}, u32[]{:S(2)}) collective-permute-start(bf16[128,640]{1,0:T(8,128)(2,1)S(1)} %get-tuple-element.50), channel_id=1, source_target_pairs={{0,6},{1,7},{2,0},{3,1},{4,2},{5,3},{6,4},{7,5},{8,14},{9,15},{10,... | collective-permute-start | bytes 491528 | tf_op jit(solution)/shard_map/ppermute | solution.py:478
  43.9 7.3 %collective-permute-start.9 = (bf16[128,640]{1,0:T(8,128)(2,1)S(1)}, bf16[128,640]{1,0:T(8,128)(2,1)S(1)}, u32[]{:S(2)}, u32[]{:S(2)}) collective-permute-start(bf16[128,640]{1,0:T(8,128)(2,1)S(1)} %get-tuple-element.49), channel_id=1, source_target_pairs={{0,2},{1,3},{2,4},{3,5},{4,6},{5,7},{6,0},{7,1},{8,10},{9,11},{10,... | collective-permute-start | bytes 491528 | tf_op jit(solution)/shard_map/ppermute | solution.py:477
  46.5 10.8 %collective-permute-start.12 = (bf16[128,640]{1,0:T(8,128)(2,1)S(1)}, bf16[128,640]{1,0:T(8,128)(2,1)S(1)}, u32[]{:S(2)}, u32[]{:S(2)}) collective-permute-start(bf16[128,640]{1,0:T(8,128)(2,1)S(1)} %get-tuple-element.52), channel_id=1, source_target_pairs={{0,6},{1,7},{2,0},{3,1},{4,2},{5,3},{6,4},{7,5},{8,14},{9,15},{10,... | collective-permute-start | bytes 491528 | tf_op jit(solution)/shard_map/ppermute | solution.py:483
  49.5 8.4 %collective-permute-start.13 = (bf16[128,640]{1,0:T(8,128)(2,1)S(1)}, bf16[128,640]{1,0:T(8,128)(2,1)S(1)}, u32[]{:S(2)}, u32[]{:S(2)}) collective-permute-start(bf16[128,640]{1,0:T(8,128)(2,1)S(1)} %get-tuple-element.53), channel_id=1, source_target_pairs={{0,2},{1,3},{2,4},{3,5},{4,6},{5,7},{6,0},{7,1},{8,10},{9,11},{10,... | collective-permute-start | bytes 491528 | tf_op jit(solution)/shard_map/ppermute | solution.py:482
  51.3 8.5 %collective-permute-start.11 = (bf16[128,640]{1,0:T(8,128)(2,1)S(1)}, bf16[128,640]{1,0:T(8,128)(2,1)S(1)}, u32[]{:S(2)}, u32[]{:S(2)}) collective-permute-start(bf16[128,640]{1,0:T(8,128)(2,1)S(1)} %get-tuple-element.51), channel_id=1, source_target_pairs={{0,2},{1,3},{2,4},{3,5},{4,6},{5,7},{6,0},{7,1},{8,10},{9,11},{10,... | collective-permute-start | bytes 491528 | tf_op jit(solution)/shard_map/ppermute | solution.py:487
  51.4 8.4 %collective-permute-start.14 = (bf16[128,640]{1,0:T(8,128)(2,1)S(1)}, bf16[128,640]{1,0:T(8,128)(2,1)S(1)}, u32[]{:S(2)}, u32[]{:S(2)}) collective-permute-start(bf16[128,640]{1,0:T(8,128)(2,1)S(1)} %get-tuple-element.54), channel_id=1, source_target_pairs={{0,6},{1,7},{2,0},{3,1},{4,2},{5,3},{6,4},{7,5},{8,14},{9,15},{10,... | collective-permute-start | bytes 491528 | tf_op jit(solution)/shard_map/ppermute | solution.py:490
